TPU v7x, 32 devices: a whole 2x2x4 slice. The times are simulated.
32 devices in a mesh: wide: 8 (over z, core), narrow: 4 (over y, x).
Axes of the slice: x: 2, y: 2, z: 4, core: 2. Of those that a mesh axis runs over, the one named last changes fastest.
Arguments:
- latents: float32 [2, 64, 256, 16], P(None, ('wide', 'narrow')), may hold values from -6 to 6
- noise_field: float32 [2, 64, 256, 16], P(None, ('wide', 'narrow')), may hold values from -6 to 6
- labels: int32 [2, 64], P(None, ('wide', 'narrow')), may hold values from 0 to 999
- label_drop: int32 [2, 64], P(None, ('wide', 'narrow')), may hold values 0 or 1
- time_steps: int32 [2, 64], P(None, ('wide', 'narrow')), may hold values from 0 to 999
- loss_weights: float32 [2, 64], P(None, ('wide', 'narrow')), may hold values from 0.5 to 7.5, as said below
- attend_weight: float32 [768, 2304], P('narrow'), may hold values from -0.21875 to 0.21875
- attend_first: float32 [768, 2304], P('narrow'), may hold values from -9.536743e-07 to 9.536743e-07
- attend_second: float32 [768, 2304], P('narrow'), may hold values from 1.5e-16 to 2.4e-15
- attend_left: float32 [24, 32, 32], P('narrow'), may hold values from -1 to 1, as said below
- attend_right: float32 [72, 32, 32], replicated, may hold values from -1 to 1, as said below
- output_weight: float32 [768, 768], P('narrow'), may hold values from -0.625 to 0.625
- output_first: float32 [768, 768], P('narrow'), may hold values from -9.536743e-07 to 9.536743e-07
- output_second: float32 [768, 768], P('narrow'), may hold values from 1e-17 to 1.6e-16
- output_left: float32 [24, 32, 32], P('narrow'), may hold values from -1 to 1, as said below
- output_right: float32 [24, 32, 32], replicated, may hold values from -1 to 1, as said below
- expand_weight: float32 [768, 3072], P('narrow'), may hold values from -0.21875 to 0.21875
- expand_first: float32 [768, 3072], P('narrow'), may hold values from -9.536743e-07 to 9.536743e-07
- expand_second: float32 [768, 3072], P('narrow'), may hold values from 1e-17 to 1.6e-16
- expand_left: float32 [24, 32, 32], P('narrow'), may hold values from -1 to 1, as said below
- expand_right: float32 [96, 32, 32], replicated, may hold values from -1 to 1, as said below
- shrink_weight: float32 [3072, 768], P('narrow'), may hold values from -0.109375 to 0.109375
- shrink_first: float32 [3072, 768], P('narrow'), may hold values from -9.536743e-07 to 9.536743e-07
- shrink_second: float32 [3072, 768], P('narrow'), may hold values from 1e-17 to 1.6e-16
- shrink_left: float32 [96, 32, 32], P('narrow'), may hold values from -1 to 1, as said below
- shrink_right: float32 [24, 32, 32], replicated, may hold values from -1 to 1, as said below
- adaptive_weight: float32 [768, 6144], P('narrow'), may hold values from -0.21875 to 0.21875
- adaptive_first: float32 [768, 6144], P('narrow'), may hold values from -9.536743e-07 to 9.536743e-07
- adaptive_second: float32 [768, 6144], P('narrow'), may hold values from 1.5e-16 to 2.4e-15
- adaptive_left: float32 [24, 32, 32], P('narrow'), may hold values from -1 to 1, as said below
- adaptive_right: float32 [192, 32, 32], replicated, may hold values from -1 to 1, as said below
- shared_weight: float32 [1592848], P('narrow')
- shared_first: float32 [1592848], P('narrow'), may hold values from -6e-07 to 6e-07
- shared_second: float32 [1592848], P('narrow'), may hold values from 1.5e-16 to 1.2e-13
Outputs:
- attend_new: float32 [768, 2304], P('narrow')
- attend_mean: float32 [768, 2304], P('narrow')
- attend_square: float32 [768, 2304], P('narrow')
- attend_copy: bfloat16 [768, 2304], P('narrow')
- output_new: float32 [768, 768], P('narrow')
- output_mean: float32 [768, 768], P('narrow')
- output_square: float32 [768, 768], P('narrow')
- output_copy: bfloat16 [768, 768], P('narrow')
- expand_new: float32 [768, 3072], P('narrow')
- expand_mean: float32 [768, 3072], P('narrow')
- expand_square: float32 [768, 3072], P('narrow')
- expand_copy: bfloat16 [768, 3072], P('narrow')
- shrink_new: float32 [3072, 768], P('narrow')
- shrink_mean: float32 [3072, 768], P('narrow')
- shrink_square: float32 [3072, 768], P('narrow')
- shrink_copy: bfloat16 [3072, 768], P('narrow')
- adaptive_new: float32 [768, 6144], P('narrow')
- adaptive_mean: float32 [768, 6144], P('narrow')
- adaptive_square: float32 [768, 6144], P('narrow')
- adaptive_copy: bfloat16 [768, 6144], P('narrow')
- shared_new: float32 [1592848], P('narrow')
- shared_mean: float32 [1592848], P('narrow')
- shared_square: float32 [1592848], P('narrow')
- shared_copy: bfloat16 [1592848], P('narrow')
- loss_sum: float32 [], replicated
- weight_sum: float32 [], replicated
- clip_norm: float32 [], replicated
Inputs may be any that keep to these rules, and one draw needn't show every extreme that they name: `loss_weights`: its scale grows from the first image to the last. `attend_left`: each block is an orthogonal matrix. `attend_right`: each block is an orthogonal matrix. `output_left`: each block is an orthogonal matrix. `output_right`: each block is an orthogonal matrix. `expand_left`: each block is an orthogonal matrix. `expand_right`: each block is an orthogonal matrix. `shrink_left`: each block is an orthogonal matrix. `shrink_right`: each block is an orthogonal matrix. `adaptive_left`: each block is an orthogonal matrix. `adaptive_right`: each block is an orthogonal matrix.
All inputs are finite; a program needn't handle non-finite values. No bound on the sum of `label_drop` on one device may be relied on, other than what follows from the above.
Results may differ from a plain program's by a relative error of at most 0.0064.
Values may be sent and summed in bfloat16 or wider, within the bound.
A program may use at most 320 MiB of HBM per device.

v0:
```python
from functools import partial
import math

import jax
import jax.numpy as jnp
from jax import lax
from jax.sharding import PartitionSpec as P

HEADS = 12
HEAD_DIM = 64
MLP_WIDTH = 3072
CLASSES = 1001
FREQS = 256
PATCH = 16
TIMESTEPS = 1000
STEP_COUNT = 10
WIDTH = 768
SEQUENCE = 256


beta_one = 0.9
beta_two = 0.999
epsilon_adam = 1e-08
learn_rate = 0.03
decay_rate = 0.01
clip_limit = 0.002
highest = lax.Precision.HIGHEST


def positions(tokens, width):
    side = math.isqrt(tokens)
    quarter = width // 4
    omega = 1.0 / 10000.0 ** (jnp.arange(quarter, dtype=jnp.float32) / quarter)
    place = jnp.arange(tokens)
    column = (place % side).astype(jnp.float32)[:, None] * omega
    row = (place // side).astype(jnp.float32)[:, None] * omega
    return jnp.concatenate([jnp.sin(column), jnp.cos(column), jnp.sin(row), jnp.cos(row)], axis=1)


def frequencies(moment, width):
    half = width // 2
    phases = jnp.exp(-math.log(10000.0) * jnp.arange(half, dtype=jnp.float32) / half)
    angles = moment[:, None] * 1000.0 * phases
    return jnp.concatenate([jnp.cos(angles), jnp.sin(angles)], axis=1)


def normalize(hidden):
    centered = hidden - jnp.mean(hidden, axis=-1, keepdims=True)
    return centered * lax.rsqrt(jnp.mean(centered * centered, axis=-1, keepdims=True) + 1e-06)


def modulate(hidden, shift, scale):
    return normalize(hidden) * (1.0 + scale[:, None, :]) + shift[:, None, :]


def split_shared(shared):
    shapes = [
        (PATCH, WIDTH),
        (FREQS, WIDTH),
        (WIDTH, WIDTH),
        (CLASSES, WIDTH),
        (WIDTH, PATCH),
        (WIDTH,),
        (WIDTH,),
        (WIDTH,),
        (WIDTH,),
        (MLP_WIDTH,),
        (WIDTH,),
        (8 * WIDTH,),
        (PATCH,),
    ]
    pieces = []
    start = 0
    for shape in shapes:
        count = math.prod(shape)
        pieces.append(shared[start : start + count].reshape(shape))
        start = start + count
    return pieces


def rotate(grad, left, right):
    rows, cols = grad.shape
    size = left.shape[1]
    blocks = grad.reshape(rows // size, size, cols // size, size)
    turned = jnp.einsum("iab,iajd->ibjd", left, blocks, precision=highest)
    turned = jnp.einsum("ibjc,jcd->ibjd", turned, right, precision=highest)
    return turned.reshape(rows, cols)


def unrotate(step, left, right):
    rows, cols = step.shape
    size = left.shape[1]
    blocks = step.reshape(rows // size, size, cols // size, size)
    turned = jnp.einsum("iab,ibjd->iajd", left, blocks, precision=highest)
    turned = jnp.einsum("iajd,jcd->iajc", turned, right, precision=highest)
    return turned.reshape(rows, cols)


def adam_direction(first, second):
    return (
        first
        / (1.0 - beta_one**STEP_COUNT)
        / (jnp.sqrt(second / (1.0 - beta_two**STEP_COUNT)) + epsilon_adam)
    )


def rotated_update(weight, first, second, grad, left, right):
    turned = rotate(grad, left, right)
    first = beta_one * first + (1.0 - beta_one) * turned
    second = beta_two * second + (1.0 - beta_two) * turned * turned
    weight = weight - learn_rate * (
        unrotate(adam_direction(first, second), left, right) + decay_rate * weight
    )
    return (weight, first, second)


def plain_update(weight, first, second, grad):
    first = beta_one * first + (1.0 - beta_one) * grad
    second = beta_two * second + (1.0 - beta_two) * grad * grad
    weight = weight - learn_rate * (adam_direction(first, second) + decay_rate * weight)
    return (weight, first, second)


def rounded(value):
    return value.astype(jnp.bfloat16)


def product(inputs, weight):
    return jnp.dot(inputs, weight, preferred_element_type=jnp.float32)


def backprod(gradient, weight):
    return jnp.einsum("...n,kn->...k", gradient, weight, preferred_element_type=jnp.float32)


def weight_grad(inputs, gradient):
    flat_in = inputs.reshape(-1, inputs.shape[-1])
    flat_grad = gradient.reshape(-1, gradient.shape[-1])
    return lax.dot_general(
        flat_in, flat_grad, (((0,), (0,)), ((), ())), preferred_element_type=jnp.float32
    )


def bias_grad(gradient):
    return jnp.sum(gradient.astype(jnp.float32).reshape(-1, gradient.shape[-1]), axis=0)


def forward(full, microbatch):
    attend_full, output_full, expand_full, shrink_full, adaptive_full, shared_full = full
    pieces = split_shared(shared_full)
    latent, noisy, label, dropped, steps = microbatch
    images, tokens = (latent.shape[0], latent.shape[1])
    moment = (steps.astype(jnp.float32) + 0.5) / TIMESTEPS
    chosen = jnp.where(dropped == 1, CLASSES - 1, label)
    weight_t = moment[:, None, None]
    blended = rounded((1.0 - weight_t) * latent + weight_t * noisy)
    target = noisy - latent
    hidden = product(blended, pieces[0]) + pieces[5].astype(jnp.float32) + positions(tokens, WIDTH)
    freqs = rounded(frequencies(moment, FREQS))
    time_pre = product(freqs, pieces[1]) + pieces[6].astype(jnp.float32)
    time_act = rounded(jax.nn.silu(time_pre))
    condition = (
        product(time_act, pieces[2])
        + pieces[7].astype(jnp.float32)
        + pieces[3][chosen].astype(jnp.float32)
    )
    cond_act = rounded(jax.nn.silu(condition))
    spans = jnp.split(product(cond_act, adaptive_full) + pieces[11].astype(jnp.float32), 8, axis=1)
    normed = rounded(modulate(hidden, spans[0], spans[1]))
    triple = rounded(product(normed, attend_full)).reshape(images, tokens, 3, HEADS, HEAD_DIM)
    query, keys, values = (triple[:, :, 0], triple[:, :, 1], triple[:, :, 2])
    scores = jnp.einsum(
        "bqhd,bkhd->bhqk", query, keys, preferred_element_type=jnp.float32
    ) * HEAD_DIM ** (-0.5)
    probs = jax.nn.softmax(scores, axis=-1)
    attended = jnp.einsum(
        "bhqk,bkhd->bqhd", rounded(probs), values, preferred_element_type=jnp.float32
    )
    attended = rounded(attended).reshape(images, tokens, WIDTH)
    branch = product(attended, output_full) + pieces[8].astype(jnp.float32)
    middle = hidden + spans[2][:, None, :] * branch
    normed_two = rounded(modulate(middle, spans[3], spans[4]))
    expand_pre = product(normed_two, expand_full) + pieces[9].astype(jnp.float32)
    expand_act = rounded(jax.nn.gelu(expand_pre, approximate=True))
    branch_two = product(expand_act, shrink_full) + pieces[10].astype(jnp.float32)
    upper = middle + spans[5][:, None, :] * branch_two
    final = rounded(modulate(upper, spans[6], spans[7]))
    output = product(final, pieces[4]) + pieces[12].astype(jnp.float32)
    kept = (
        blended,
        freqs,
        time_pre,
        time_act,
        condition,
        cond_act,
        spans,
        hidden,
        normed,
        query,
        keys,
        values,
        probs,
        attended,
        branch,
        middle,
        normed_two,
        expand_pre,
        expand_act,
        branch_two,
        upper,
        final,
        chosen,
    )
    return (kept, output, target)


def backward(full, kept, grad_out):
    attend_full, output_full, expand_full, shrink_full, adaptive_full, shared_full = full
    pieces = split_shared(shared_full)
    (
        blended,
        freqs,
        time_pre,
        time_act,
        condition,
        cond_act,
        spans,
        hidden,
        normed,
        query,
        keys,
        values,
        probs,
        attended,
        branch,
        middle,
        normed_two,
        expand_pre,
        expand_act,
        branch_two,
        upper,
        final,
        chosen,
    ) = kept
    images, tokens = (hidden.shape[0], hidden.shape[1])
    grad_final_w = weight_grad(final, grad_out)
    unused, pullback = jax.vjp(modulate, upper, spans[6], spans[7])
    grad_upper, grad_shift_f, grad_scale_f = pullback(backprod(grad_out, pieces[4]))
    grad_branch_two = rounded(spans[5][:, None, :] * grad_upper)
    grad_gate_two = jnp.sum(branch_two * grad_upper, axis=1)
    grad_shrink = weight_grad(expand_act, grad_branch_two)
    unused, pullback = jax.vjp(partial(jax.nn.gelu, approximate=True), expand_pre)
    grad_expand_pre = rounded(pullback(backprod(grad_branch_two, shrink_full))[0])
    grad_expand = weight_grad(normed_two, grad_expand_pre)
    unused, pullback = jax.vjp(modulate, middle, spans[3], spans[4])
    grad_middle, grad_shift_two, grad_scale_two = pullback(backprod(grad_expand_pre, expand_full))
    grad_middle = grad_middle + grad_upper
    grad_branch = rounded(spans[2][:, None, :] * grad_middle)
    grad_gate = jnp.sum(branch * grad_middle, axis=1)
    grad_output = weight_grad(attended, grad_branch)
    grad_attended = rounded(backprod(grad_branch, output_full)).reshape(
        images, tokens, HEADS, HEAD_DIM
    )
    grad_probs = jnp.einsum(
        "bqhd,bkhd->bhqk", grad_attended, values, preferred_element_type=jnp.float32
    )
    grad_values = jnp.einsum(
        "bhqk,bqhd->bkhd", rounded(probs), grad_attended, preferred_element_type=jnp.float32
    )
    grad_scores = rounded(
        probs * (grad_probs - jnp.sum(probs * grad_probs, axis=-1, keepdims=True))
    )
    grad_query = jnp.einsum(
        "bhqk,bkhd->bqhd", grad_scores, keys, preferred_element_type=jnp.float32
    ) * HEAD_DIM ** (-0.5)
    grad_keys = jnp.einsum(
        "bhqk,bqhd->bkhd", grad_scores, query, preferred_element_type=jnp.float32
    ) * HEAD_DIM ** (-0.5)
    grad_triple = rounded(jnp.stack([grad_query, grad_keys, grad_values], axis=2)).reshape(
        images, tokens, 3 * WIDTH
    )
    grad_attend = weight_grad(normed, grad_triple)
    unused, pullback = jax.vjp(modulate, hidden, spans[0], spans[1])
    grad_hidden, grad_shift, grad_scale = pullback(backprod(grad_triple, attend_full))
    grad_hidden = rounded(grad_hidden + grad_middle)
    grad_spans = rounded(
        jnp.concatenate(
            [
                grad_shift,
                grad_scale,
                grad_gate,
                grad_shift_two,
                grad_scale_two,
                grad_gate_two,
                grad_shift_f,
                grad_scale_f,
            ],
            axis=1,
        )
    )
    grad_adaptive = weight_grad(cond_act, grad_spans)
    unused, pullback = jax.vjp(jax.nn.silu, condition)
    grad_condition = pullback(backprod(grad_spans, adaptive_full))[0]
    choose = (chosen[:, None] == jnp.arange(CLASSES)[None, :]).astype(jnp.float32)
    grad_table = jnp.einsum("ic,iw->cw", choose, grad_condition, precision=highest)
    grad_condition = rounded(grad_condition)
    grad_time_two = weight_grad(time_act, grad_condition)
    unused, pullback = jax.vjp(jax.nn.silu, time_pre)
    grad_time_pre = rounded(pullback(backprod(grad_condition, pieces[2]))[0])
    grad_time_one = weight_grad(freqs, grad_time_pre)
    grad_patch = weight_grad(blended, grad_hidden)
    flat = [
        grad_patch,
        grad_time_one,
        grad_time_two,
        grad_table,
        grad_final_w,
        bias_grad(grad_hidden),
        bias_grad(grad_time_pre),
        bias_grad(grad_condition),
        bias_grad(grad_branch),
        bias_grad(grad_expand_pre),
        bias_grad(grad_branch_two),
        bias_grad(grad_spans),
        bias_grad(grad_out),
    ]
    grad_shared = jnp.concatenate([piece.reshape(-1) for piece in flat])
    return (grad_attend, grad_output, grad_expand, grad_shrink, grad_adaptive, grad_shared)


def narrow_sums(grads):
    return (
        lax.psum_scatter(
            grads[0].astype(jnp.bfloat16), "narrow", scatter_dimension=0, tiled=True
        ).astype(jnp.float32),
        lax.psum_scatter(
            grads[1].astype(jnp.bfloat16), "narrow", scatter_dimension=0, tiled=True
        ).astype(jnp.float32),
        lax.psum_scatter(
            grads[2].astype(jnp.bfloat16), "narrow", scatter_dimension=0, tiled=True
        ).astype(jnp.float32),
        lax.psum_scatter(
            grads[3].astype(jnp.bfloat16), "narrow", scatter_dimension=0, tiled=True
        ).astype(jnp.float32),
        lax.psum_scatter(
            grads[4].astype(jnp.bfloat16), "narrow", scatter_dimension=0, tiled=True
        ).astype(jnp.float32),
        lax.psum_scatter(
            grads[5].astype(jnp.bfloat16), "narrow", scatter_dimension=0, tiled=True
        ).astype(jnp.float32),
    )


def local(
    latents,
    noise_field,
    labels,
    label_drop,
    time_steps,
    loss_weights,
    attend_weight,
    attend_first,
    attend_second,
    attend_left,
    attend_right,
    output_weight,
    output_first,
    output_second,
    output_left,
    output_right,
    expand_weight,
    expand_first,
    expand_second,
    expand_left,
    expand_right,
    shrink_weight,
    shrink_first,
    shrink_second,
    shrink_left,
    shrink_right,
    adaptive_weight,
    adaptive_first,
    adaptive_second,
    adaptive_left,
    adaptive_right,
    shared_weight,
    shared_first,
    shared_second,
):
    weight_sum = lax.psum(jnp.sum(loss_weights), ("wide", "narrow"))
    full = (
        lax.all_gather(rounded(attend_weight), "narrow", axis=0, tiled=True),
        lax.all_gather(rounded(output_weight), "narrow", axis=0, tiled=True),
        lax.all_gather(rounded(expand_weight), "narrow", axis=0, tiled=True),
        lax.all_gather(rounded(shrink_weight), "narrow", axis=0, tiled=True),
        lax.all_gather(rounded(adaptive_weight), "narrow", axis=0, tiled=True),
        lax.all_gather(rounded(shared_weight), "narrow", axis=0, tiled=True),
    )
    grad_totals = None
    loss_part = jnp.zeros((), jnp.float32)
    for number in range(latents.shape[0]):
        microbatch = (
            latents[number],
            noise_field[number],
            labels[number],
            label_drop[number],
            time_steps[number],
        )
        kept, output, target = forward(full, microbatch)
        mismatch = output - target
        loss_part = loss_part + jnp.sum(
            loss_weights[number] * jnp.mean(mismatch * mismatch, axis=(1, 2))
        )
        scaling = 2.0 * loss_weights[number] / (SEQUENCE * PATCH * weight_sum)
        grads = backward(full, kept, rounded(scaling[:, None, None] * mismatch))
        grads = narrow_sums(grads)
        if grad_totals is None:
            grad_totals = grads
        else:
            grad_totals = tuple(
                (running + gradient for running, gradient in zip(grad_totals, grads))
            )
    summed = lax.psum(
        (
            grad_totals[0],
            grad_totals[1],
            grad_totals[2],
            grad_totals[3],
            grad_totals[4],
            grad_totals[5],
            loss_part,
        ),
        "wide",
    )
    squares = sum((jnp.sum(gradient * gradient) for gradient in summed[:6]))
    square_total, loss_sum = lax.psum((squares, summed[6]), "narrow")
    clip_norm = jnp.sqrt(square_total)
    factor = clip_limit / jnp.maximum(clip_norm, clip_limit)
    states = (
        (attend_weight, attend_first, attend_second, attend_left, attend_right),
        (output_weight, output_first, output_second, output_left, output_right),
        (expand_weight, expand_first, expand_second, expand_left, expand_right),
        (shrink_weight, shrink_first, shrink_second, shrink_left, shrink_right),
        (adaptive_weight, adaptive_first, adaptive_second, adaptive_left, adaptive_right),
    )
    results = []
    for number in range(5):
        weight, first, second, left, right = states[number]
        fresh = rotated_update(weight, first, second, summed[number] * factor, left, right)
        results += [fresh[0], fresh[1], fresh[2], fresh[0].astype(jnp.bfloat16)]
    fresh = plain_update(shared_weight, shared_first, shared_second, summed[5] * factor)
    results += [fresh[0], fresh[1], fresh[2], fresh[0].astype(jnp.bfloat16)]
    return (
        results[0],
        results[1],
        results[2],
        results[3],
        results[4],
        results[5],
        results[6],
        results[7],
        results[8],
        results[9],
        results[10],
        results[11],
        results[12],
        results[13],
        results[14],
        results[15],
        results[16],
        results[17],
        results[18],
        results[19],
        results[20],
        results[21],
        results[22],
        results[23],
        loss_sum,
        weight_sum,
        clip_norm,
    )


def solution(mesh):
    placed = (
        P(None, ("wide", "narrow"), None, None),
        P(None, ("wide", "narrow"), None, None),
        P(None, ("wide", "narrow")),
        P(None, ("wide", "narrow")),
        P(None, ("wide", "narrow")),
        P(None, ("wide", "narrow")),
        P("narrow", None),
        P("narrow", None),
        P("narrow", None),
        P("narrow", None, None),
        P(),
        P("narrow", None),
        P("narrow", None),
        P("narrow", None),
        P("narrow", None, None),
        P(),
        P("narrow", None),
        P("narrow", None),
        P("narrow", None),
        P("narrow", None, None),
        P(),
        P("narrow", None),
        P("narrow", None),
        P("narrow", None),
        P("narrow", None, None),
        P(),
        P("narrow", None),
        P("narrow", None),
        P("narrow", None),
        P("narrow", None, None),
        P(),
        P("narrow"),
        P("narrow"),
        P("narrow"),
    )
    return jax.shard_map(
        local,
        mesh=mesh,
        in_specs=placed,
        out_specs=(
            P("narrow", None),
            P("narrow", None),
            P("narrow", None),
            P("narrow", None),
            P("narrow", None),
            P("narrow", None),
            P("narrow", None),
            P("narrow", None),
            P("narrow", None),
            P("narrow", None),
            P("narrow", None),
            P("narrow", None),
            P("narrow", None),
            P("narrow", None),
            P("narrow", None),
            P("narrow", None),
            P("narrow", None),
            P("narrow", None),
            P("narrow", None),
            P("narrow", None),
            P("narrow"),
            P("narrow"),
            P("narrow"),
            P("narrow"),
            P(),
            P(),
            P(),
        ),
        check_vma=False,
    )
```

profile of v0, /device:TPU:0, one launch (start us, length us, event | category | flops | bytes accessed | tf_op | source)
XLA Modules:
  0.0 2303.9 jit_solution(10145690909134066981)
XLA Ops:
  38.2 42.2 %psum.70 = f32[]{:T(128)} all-reduce(f32[]{:T(128)} %reduce_sum.625), channel_id=1, replica_groups=mesh['wide'=8,'narrow'=4] {'wide','narrow'}, use_global_device_ids=true, to_apply=%region_5.6 | all-reduce | flops 1 | bytes 8 | tf_op jit(solution)/shard_map/psum | solution.py:390
  84.4 32.0 %all-reduce.10.cloned.1.call-done = bf16[1592848]{0:T(1024)(128)(2,1)} async-done(((bf16[1592848]{0:T(1024)(128)(2,1)}), bf16[1592848]{0:T(1024)(128)(2,1)}) %all-reduce.10.cloned.1.call-update) | async-done | bytes 3185712
  140.5 75.0 %all-gather.6.cloned.1.call-done = bf16[768,6144]{1,0:T(8,128)(2,1)} async-done(((bf16[192,6144]{1,0:T(8,128)(2,1)}), bf16[768,6144]{1,0:T(8,128)(2,1)}) %all-gather.6.cloned.1.call-update) | async-done | bytes 9437200 | tf_op jit(solution)/shard_map/all_gather | solution.py:396
  225.1 40.1 %all-gather.8.cloned.1.call-done = bf16[768,2304]{1,0:T(8,128)(2,1)} async-done(((bf16[192,2304]{1,0:T(8,128)(2,1)}), bf16[768,2304]{1,0:T(8,128)(2,1)}) %all-gather.8.cloned.1.call-update) | async-done | bytes 3538960 | tf_op jit(solution)/shard_map/all_gather | solution.py:392
  289.1 16.6 fusion.241
  329.2 25.4 %all-gather.12.cloned.1.call-done = bf16[768,3072]{1,0:T(8,128)(2,1)} async-done(((bf16[192,3072]{1,0:T(8,128)(2,1)}), bf16[768,3072]{1,0:T(8,128)(2,1)}) %all-gather.12.cloned.1.call-update) | async-done | bytes 4718608 | tf_op jit(solution)/shard_map/all_gather | solution.py:394
  367.8 46.2 %all-gather.14.cloned.1.call-done = bf16[3072,768]{1,0:T(8,128)(2,1)} async-done(((bf16[768,768]{1,0:T(8,128)(2,1)}), bf16[3072,768]{1,0:T(8,128)(2,1)}) %all-gather.14.cloned.1.call-update) | async-done | bytes 4718608 | tf_op jit(solution)/shard_map/all_gather | solution.py:395
  589.5 24.1 %dynamic-update-slice.4 = bf16[1592848]{0:T(1024)(128)(2,1)} dynamic-update-slice(bf16[1592848]{0:T(1024)(128)(2,1)} %constant_dynamic-update-slice_fusion.19, bf16[768768]{0:T(1024)(128)(2,1)} %reshape.683, s32[]{} %constant.251) | dynamic-update-slice | bytes 3075076
  613.7 23.7 %dynamic-update-slice.17 = bf16[1592848]{0:T(1024)(128)(2,1)} dynamic-update-slice(bf16[1592848]{0:T(1024)(128)(2,1)} %constant_dynamic-update-slice_fusion.18, bf16[768768]{0:T(1024)(128)(2,1)S(1)} %reshape.678, s32[]{} %constant.251) | dynamic-update-slice | bytes 3075076
  731.6 72.1 %all-reduce.14.cloned.1.call-done = (bf16[1592848]{0:T(1024)(128)(2,1)}, bf16[1592848]{0:T(1024)(128)(2,1)}) async-done(((bf16[1592848]{0:T(1024)(128)(2,1)}, bf16[1592848]{0:T(1024)(128)(2,1)}), (bf16[1592848]{0:T(1024)(128)(2,1)}, bf16[1592848]{0:T(1024)(128)(2,1)})) %all-reduce.14.cloned.1.call-update) | async-done | bytes 6371408
  807.1 47.4 %reduce-scatter.13.cloned.1.call-done = bf16[192,2304]{1,0:T(8,128)(2,1)} async-done(((bf16[768,2304]{1,0:T(8,128)(2,1)}), bf16[192,2304]{1,0:T(8,128)(2,1)}) %reduce-scatter.13.cloned.1.call-update) | async-done | bytes 884752 | tf_op jit(solution)/shard_map/reduce_scatter | solution.py:333
  854.5 50.3 %reduce-scatter.11.cloned.1.call-done = bf16[192,2304]{1,0:T(8,128)(2,1)} async-done(((bf16[768,2304]{1,0:T(8,128)(2,1)}), bf16[192,2304]{1,0:T(8,128)(2,1)}) %reduce-scatter.11.cloned.1.call-update) | async-done | bytes 884752 | tf_op jit(solution)/shard_map/reduce_scatter | solution.py:333
  907.6 57.1 %reduce-scatter.23.cloned.1.call-done = bf16[768,768]{1,0:T(8,128)(2,1)} async-done(((bf16[3072,768]{1,0:T(8,128)(2,1)}), bf16[768,768]{1,0:T(8,128)(2,1)}) %reduce-scatter.23.cloned.1.call-update) | async-done | bytes 1179664 | tf_op jit(solution)/shard_map/reduce_scatter | solution.py:342
  964.8 60.7 %reduce-scatter.25.cloned.1.call-done = bf16[768,768]{1,0:T(8,128)(2,1)} async-done(((bf16[3072,768]{1,0:T(8,128)(2,1)}), bf16[768,768]{1,0:T(8,128)(2,1)}) %reduce-scatter.25.cloned.1.call-update) | async-done | bytes 1179664 | tf_op jit(solution)/shard_map/reduce_scatter | solution.py:342
  1028.7 57.3 %reduce-scatter.21.cloned.1.call-done = bf16[192,3072]{1,0:T(8,128)(2,1)} async-done(((bf16[768,3072]{1,0:T(8,128)(2,1)}), bf16[192,3072]{1,0:T(8,128)(2,1)}) %reduce-scatter.21.cloned.1.call-update) | async-done | bytes 1179664 | tf_op jit(solution)/shard_map/reduce_scatter | solution.py:339
  1086.0 60.5 %reduce-scatter.19.cloned.1.call-done = bf16[192,3072]{1,0:T(8,128)(2,1)} async-done(((bf16[768,3072]{1,0:T(8,128)(2,1)}), bf16[192,3072]{1,0:T(8,128)(2,1)}) %reduce-scatter.19.cloned.1.call-update) | async-done | bytes 1179664 | tf_op jit(solution)/shard_map/reduce_scatter | solution.py:339
  1149.9 94.7 %reduce-scatter.29.cloned.1.call-done = bf16[192,6144]{1,0:T(8,128)(2,1)} async-done(((bf16[768,6144]{1,0:T(8,128)(2,1)}), bf16[192,6144]{1,0:T(8,128)(2,1)}) %reduce-scatter.29.cloned.1.call-update) | async-done | bytes 2359312 | tf_op jit(solution)/shard_map/reduce_scatter | solution.py:345
  1244.6 98.0 %reduce-scatter.27.cloned.1.call-done = bf16[192,6144]{1,0:T(8,128)(2,1)} async-done(((bf16[768,6144]{1,0:T(8,128)(2,1)}), bf16[192,6144]{1,0:T(8,128)(2,1)}) %reduce-scatter.27.cloned.1.call-update) | async-done | bytes 2359312 | tf_op jit(solution)/shard_map/reduce_scatter | solution.py:345
  1353.6 17.3 psum.78
  1370.9 249.6 %all-reduce.12.cloned.1.call-done = (f32[192,2304]{1,0:T(8,128)}, f32[192,768]{1,0:T(8,128)}, f32[192,3072]{1,0:T(8,128)}, f32[768,768]{1,0:T(8,128)}, f32[192,6144]{1,0:T(8,128)}, /*index=5*/f32[398212]{0:T(1024)}) async-done(((f32[192,2304]{1,0:T(8,128)}, f32[192,768]{1,0:T(8,128)}, f32[192,3072]{1,0:T(8,128)}, f32[768,768]{1,0:T(8,128)}, f32[192,6144]{1,0:T(8,128)}, /*index=5*/f32[398212]{0:T(1024)}), ...) | async-done | bytes 13389344 | tf_op jit(solution)/shard_map/psum | solution.py:423
  1939.9 18.7 fusion.8
  1958.6 16.0 fusion.53
  2005.5 18.7 fusion.6
  2024.3 16.0 fusion.56
  2075.1 13.7 copy.290
  2110.6 22.3 convolution_bitcast_fusion.1
  2132.9 22.0 copy.294
  2155.0 14.0 reshape.702
  2190.5 13.7 copy.295
  2226.0 22.3 convolution_bitcast_fusion
  2248.3 22.0 copy.298
  2270.3 14.0 reshape.704
  (862 shorter events, 874.0 us)
Async XLA Ops:
  7.2 1932.7 %copy-start = (f32[24,32,32]{2,1,0:T(8,128)S(1)}, f32[24,32,32]{2,1,0:T(8,128)}, u32[]{:S(2)}) copy-start(f32[24,32,32]{2,1,0:T(8,128)} %param.58) | copy-start | bytes 294916
  7.2 109.2 %all-reduce.10.cloned.1.call-start = ((), (), s32[]{:S(2)}) async-start(), calls=%async_computation.25 | async-start | bytes 6373376
  25.0 190.4 %all-gather.6.cloned.1.call-start = ((), (), s32[]{:S(2)}) async-start(), calls=%async_computation.10 | async-start | bytes 11796480 | tf_op jit(solution)/shard_map/all_gather | solution.py:396
  29.2 236.0 %all-gather.8.cloned.1.call-start = ((), (), s32[]{:S(2)}) async-start(), calls=%async_computation.11 | async-start | bytes 4423680 | tf_op jit(solution)/shard_map/all_gather | solution.py:392
  31.9 279.2 %all-gather.10.cloned.1.call-start = ((), (), s32[]{:S(2)}) async-start(), calls=%async_computation.12 | async-start | bytes 1474560 | tf_op jit(solution)/shard_map/all_gather | solution.py:393
  32.7 321.9 %all-gather.12.cloned.1.call-start = ((), (), s32[]{:S(2)}) async-start(), calls=%async_computation.13 | async-start | bytes 5898240 | tf_op jit(solution)/shard_map/all_gather | solution.py:394
  34.0 379.9 %all-gather.14.cloned.1.call-start = ((), (), s32[]{:S(2)}) async-start(), calls=%async_computation.14 | async-start | bytes 5898240 | tf_op jit(solution)/shard_map/all_gather | solution.py:395
  36.9 692.7 %reduce-scatter.15.cloned.1.call-start = ((), (), s32[]{:S(2)}) async-start(), calls=%async_computation.17 | async-start | bytes 1474560 | tf_op jit(solution)/shard_map/reduce_scatter | solution.py:336
  37.6 95.8 %copy-start.220 = (f32[2]{0:T(128)}, f32[2]{0:T(128)S(1)}, u32[]{:S(2)}) copy-start(f32[2]{0:T(128)S(1)} %get-tuple-element.164) | copy-start | bytes 28
  37.6 95.8 %copy-start.222 = (f32[2]{0:T(128)}, f32[2]{0:T(128)S(1)}, u32[]{:S(2)}) copy-start(f32[2]{0:T(128)S(1)} %get-tuple-element.165) | copy-start | bytes 28
  82.2 55.5 %copy-start.214 = (bf16[2,128]{1,0:T(2,128)(2,1)}, bf16[2,128]{1,0:T(2,128)(2,1)S(1)}, u32[]{:S(2)}) copy-start(bf16[2,128]{1,0:T(2,128)(2,1)S(1)} %get-tuple-element.173) | copy-start | bytes 1540
  82.2 55.7 %copy-start.210 = (bf16[2,128]{1,0:T(2,128)(2,1)}, bf16[2,128]{1,0:T(2,128)(2,1)S(1)}, u32[]{:S(2)}) copy-start(bf16[2,128]{1,0:T(2,128)(2,1)S(1)} %get-tuple-element.159) | copy-start | bytes 1540
  82.2 55.7 %copy-start.212 = (bf16[2,128]{1,0:T(2,128)(2,1)}, bf16[2,128]{1,0:T(2,128)(2,1)S(1)}, u32[]{:S(2)}) copy-start(bf16[2,128]{1,0:T(2,128)(2,1)S(1)} %get-tuple-element.160) | copy-start | bytes 1540
  84.4 49.0 %copy-start.40 = (f32[256,768]{1,0:T(8,128)}, f32[256,768]{1,0:T(8,128)S(1)}, u32[]{:S(2)}) copy-start(f32[256,768]{1,0:T(8,128)S(1)} %pad_maximum_fusion) | copy-start | bytes 2359300
  138.4 82.9 %copy-start.99 = (f32[2,768]{1,0:T(2,128)}, f32[2,768]{1,0:T(2,128)S(1)}, u32[]{:S(2)}) copy-start(f32[2,768]{1,0:T(2,128)S(1)} %fusion.114) | copy-start | bytes 18436
  138.7 81.9 %copy-start.101 = (f32[2,768]{1,0:T(2,128)}, f32[2,768]{1,0:T(2,128)S(1)}, u32[]{:S(2)}) copy-start(f32[2,768]{1,0:T(2,128)S(1)} %fusion.113) | copy-start | bytes 18436
  223.8 51.3 %copy-start.123 = (f32[2,768]{1,0:T(2,128)}, f32[2,768]{1,0:T(2,128)S(1)}, u32[]{:S(2)}) copy-start(f32[2,768]{1,0:T(2,128)S(1)} %get-tuple-element.140) | copy-start | bytes 18436
  223.8 252.6 %copy-start.104 = (f32[2,768]{1,0:T(2,128)}, f32[2,768]{1,0:T(2,128)S(1)}, u32[]{:S(2)}) copy-start(f32[2,768]{1,0:T(2,128)S(1)} %get-tuple-element.133) | copy-start | bytes 18436
  367.8 53.8 %copy-start.161 = (f32[2,768]{1,0:T(2,128)S(1)}, f32[2,768]{1,0:T(2,128)}, u32[]{:S(2)}) copy-start(f32[2,768]{1,0:T(2,128)} %get-tuple-element.137) | copy-start | bytes 18436
  427.7 48.8 %copy-start.126 = (f32[2,256]{1,0:T(2,128)}, f32[2,256]{1,0:T(2,128)S(1)}, u32[]{:S(2)}) copy-start(f32[2,256]{1,0:T(2,128)S(1)} %broadcast_multiply_fusion.8) | copy-start | bytes 6148
  524.7 205.0 %reduce-scatter.17.cloned.1.call-start = ((), (), s32[]{:S(2)}) async-start(), calls=%async_computation.18 | async-start | bytes 1474560 | tf_op jit(solution)/shard_map/reduce_scatter | solution.py:336
  568.9 234.8 %all-reduce.14.cloned.1.call-start = ((), (), s32[]{:S(2)}) async-start(), calls=%async_computation.27 | async-start | bytes 12746752
  613.7 48.2 %copy-start.229 = (bf16[16]{0:T(256)(128)(2,1)S(1)}, bf16[16]{0:T(256)(128)(2,1)}, u32[]{:S(2)}) copy-start(bf16[16]{0:T(256)(128)(2,1)} %get-tuple-element.88) | copy-start | bytes 100
  663.2 191.3 %reduce-scatter.13.cloned.1.call-start = ((), (), s32[]{:S(2)}) async-start(), calls=%async_computation.16 | async-start | bytes 4423680 | tf_op jit(solution)/shard_map/reduce_scatter | solution.py:333
  672.3 232.5 %reduce-scatter.11.cloned.1.call-start = ((), (), s32[]{:S(2)}) async-start(), calls=%async_computation.15 | async-start | bytes 4423680 | tf_op jit(solution)/shard_map/reduce_scatter | solution.py:333
  681.6 283.1 %reduce-scatter.23.cloned.1.call-start = ((), (), s32[]{:S(2)}) async-start(), calls=%async_computation.21 | async-start | bytes 5898240 | tf_op jit(solution)/shard_map/reduce_scatter | solution.py:342
  691.4 334.0 %reduce-scatter.25.cloned.1.call-start = ((), (), s32[]{:S(2)}) async-start(), calls=%async_computation.22 | async-start | bytes 5898240 | tf_op jit(solution)/shard_map/reduce_scatter | solution.py:342
  701.4 384.7 %reduce-scatter.21.cloned.1.call-start = ((), (), s32[]{:S(2)}) async-start(), calls=%async_computation.20 | async-start | bytes 5898240 | tf_op jit(solution)/shard_map/reduce_scatter | solution.py:339
  709.2 437.3 %reduce-scatter.19.cloned.1.call-start = ((), (), s32[]{:S(2)}) async-start(), calls=%async_computation.19 | async-start | bytes 5898240 | tf_op jit(solution)/shard_map/reduce_scatter | solution.py:339
  717.2 527.4 %reduce-scatter.29.cloned.1.call-start = ((), (), s32[]{:S(2)}) async-start(), calls=%async_computation.24 | async-start | bytes 11796480 | tf_op jit(solution)/shard_map/reduce_scatter | solution.py:345
  723.2 619.4 %reduce-scatter.27.cloned.1.call-start = ((), (), s32[]{:S(2)}) async-start(), calls=%async_computation.23 | async-start | bytes 11796480 | tf_op jit(solution)/shard_map/reduce_scatter | solution.py:345
  728.9 891.6 %all-reduce.12.cloned.1.call-start = ((), (), s32[]{:S(2)}) async-start(), calls=%async_computation.26 | async-start | bytes 26779648 | tf_op jit(solution)/shard_map/psum | solution.py:423
  (242 other events, 1698.3 us)
Sparse Core Ops, SparseCore 0:
  25.2 91.2 all-reduce.9
  118.9 96.5 all-gather.5
  217.9 47.2 all-gather.7
  267.5 27.7 all-gather.9
  297.5 57.0 all-gather.11
  356.9 57.0 all-gather.13
  524.8 28.5 reduce-scatter.14
  569.1 28.6 reduce-scatter.16
  663.3 140.3 all-reduce.13
  806.7 47.7 reduce-scatter.12
  857.5 47.2 reduce-scatter.10
  907.6 57.0 reduce-scatter.22
  968.3 57.0 reduce-scatter.24
  1028.9 57.0 reduce-scatter.20
  1089.4 57.0 reduce-scatter.18
  1149.5 95.0 reduce-scatter.28
  1247.5 95.0 reduce-scatter.26
  1348.0 272.5 all-reduce.11
where the time goes:
time: 2320 us; the launch traced here: 2300 us
  waiting for transfers between devices  1070 us (46%)
  local copies, waits for them, and re-layouts  538 us (23%)
  matrix products  420 us (18%)
  other arithmetic  180 us (8%)
  blocking collectives  70.1 us (3%)
  between operations  26.1 us (1%)
    psum x1, waiting for transfers between devices, local(): lax.psum((grad_totals[0], grad_totals[1], grad_totals[2], grad_totals[3],...  250 us
    reduce_scatter x2, waiting for transfers between devices, narrow_sums(): lax.psum_scatter(grads[4].astype(jnp.bfloat16), 'narrow', scatter_dimensi...  193 us
    unnamed x556, local copies, waits for them, and re-layouts  134 us
    reduce_scatter x2, waiting for transfers between devices, narrow_sums(): lax.psum_scatter(grads[3].astype(jnp.bfloat16), 'narrow', scatter_dimensi...  118 us
    reduce_scatter x2, waiting for transfers between devices, narrow_sums(): lax.psum_scatter(grads[2].astype(jnp.bfloat16), 'narrow', scatter_dimensi...  118 us
    unnamed x20, waiting for transfers between devices  104 us
    reduce_scatter x2, waiting for transfers between devices, narrow_sums(): lax.psum_scatter(grads[0].astype(jnp.bfloat16), 'narrow', scatter_dimensi...  97.7 us
    all_gather x1, waiting for transfers between devices, local(): lax.all_gather(rounded(adaptive_weight), 'narrow', axis=0, tiled=True)  75 us
  transfers between devices with their start and end apart: 18, of which 15 were waited for; matrix products, arithmetic and copies ran while one was open for 14% of the time, Pallas kernels for 0%

commit v1 on v0

v1 whole, which is shorter than its diff:
```python
from functools import partial
import math

import jax
import jax.numpy as jnp
import numpy as np
from jax import lax
from jax.experimental import pallas as pl
from jax.experimental.pallas import tpu as pltpu
from jax.sharding import PartitionSpec as P

HEADS = 12
HEAD_DIM = 64
MLP_WIDTH = 3072
CLASSES = 1001
FREQS = 256
PATCH = 16
TIMESTEPS = 1000
BLOCK = 32
STEP_COUNT = 10
WIDTH = 768
SEQUENCE = 256


beta_one = 0.9
beta_two = 0.999
epsilon_adam = 1e-08
learn_rate = 0.03
decay_rate = 0.01
clip_limit = 0.002
highest = lax.Precision.HIGHEST
bf16 = jnp.bfloat16
f32 = jnp.float32

ROW_PATCH = 0
ROW_TIME_ONE = 16
ROW_TIME_TWO = 272
ROW_TABLE = 1040
ROW_FINAL = 2041
ROW_BIAS = 2057


def positions(tokens, width):
    side = math.isqrt(tokens)
    quarter = width // 4
    omega = 1.0 / 10000.0 ** (np.arange(quarter, dtype=np.float64) / quarter)
    place = np.arange(tokens)
    column = (place % side)[:, None] * omega
    row = (place // side)[:, None] * omega
    table = np.concatenate([np.sin(column), np.cos(column), np.sin(row), np.cos(row)], axis=1)
    return jnp.asarray(table.astype(np.float32))


def frequencies(moment, width):
    half = width // 2
    phases = jnp.exp(-math.log(10000.0) * jnp.arange(half, dtype=jnp.float32) / half)
    angles = moment[:, None] * 1000.0 * phases
    return jnp.concatenate([jnp.cos(angles), jnp.sin(angles)], axis=1)


def normalize(hidden):
    centered = hidden - jnp.mean(hidden, axis=-1, keepdims=True)
    return centered * lax.rsqrt(jnp.mean(centered * centered, axis=-1, keepdims=True) + 1e-06)


def modulate(hidden, shift, scale):
    return normalize(hidden) * (1.0 + scale[:, None, :]) + shift[:, None, :]


def adam_direction(first, second):
    return (
        first
        / (1.0 - beta_one**STEP_COUNT)
        / (jnp.sqrt(second / (1.0 - beta_two**STEP_COUNT)) + epsilon_adam)
    )


def plain_update(weight, first, second, grad):
    first = beta_one * first + (1.0 - beta_one) * grad
    second = beta_two * second + (1.0 - beta_two) * grad * grad
    weight = weight - learn_rate * (adam_direction(first, second) + decay_rate * weight)
    return (weight, first, second)


def rounded(value):
    return value.astype(jnp.bfloat16)


def product(inputs, weight):
    return jnp.dot(inputs, weight, preferred_element_type=jnp.float32)


def backprod(gradient, weight):
    return jnp.einsum("...n,kn->...k", gradient, weight, preferred_element_type=jnp.float32)


def weight_grad(inputs, gradient):
    flat_in = inputs.reshape(-1, inputs.shape[-1])
    flat_grad = gradient.reshape(-1, gradient.shape[-1])
    return lax.dot_general(
        flat_in, flat_grad, (((0,), (0,)), ((), ())), preferred_element_type=jnp.float32
    )


def bias_grad(gradient):
    return jnp.sum(gradient.astype(jnp.float32).reshape(-1, gradient.shape[-1]), axis=0)


def halves(value):
    high = value.astype(bf16)
    return high, (value - high.astype(f32)).astype(bf16)


def spread_blocks(blocks):
    count = blocks.shape[0]
    size = count * BLOCK
    high, low = halves(blocks.reshape(size, BLOCK))
    place = lax.broadcasted_iota(jnp.int32, (BLOCK, size), 0)
    column = lax.broadcasted_iota(jnp.int32, (BLOCK, size), 1)
    repeat = (place == column % BLOCK).astype(bf16)
    row_block = lax.broadcasted_iota(jnp.int32, (size, size), 0) // BLOCK
    col_block = lax.broadcasted_iota(jnp.int32, (size, size), 1) // BLOCK
    inside = row_block == col_block
    high = jnp.dot(high, repeat, preferred_element_type=f32)
    low = jnp.dot(low, repeat, preferred_element_type=f32)
    return jnp.where(inside, high, 0.0), jnp.where(inside, low, 0.0)


def dot(left, right):
    return jnp.dot(left, right, preferred_element_type=f32)


def dot_t(left, right):
    return lax.dot_general(left, right, (((1,), (1,)), ((), ())), preferred_element_type=f32)


def adam_kernel(
    factor_ref,
    weight_ref,
    first_ref,
    second_ref,
    grad_ref,
    left_ref,
    right_ref,
    new_ref,
    mean_ref,
    square_ref,
    copy_ref,
    left_high,
    turn_high,
    turn_low,
):
    @pl.when(pl.program_id(1) == 0)
    def _():
        high, low = spread_blocks(left_ref[...])
        left_high[...] = high.astype(bf16)
        turn_high[...] = high.T.astype(bf16)
        turn_low[...] = low.T.astype(bf16)

    factor = factor_ref[0]
    chunk = 256
    for start in range(0, weight_ref.shape[1], chunk):
        span = pl.ds(start, chunk)
        right_high, right_low = spread_blocks(
            right_ref[start // BLOCK : (start + chunk) // BLOCK]
        )
        right_high = right_high.astype(bf16)
        right_low = right_low.astype(bf16)
        if grad_ref.dtype == bf16:
            grad = grad_ref[:, span]
            turned = dot(grad, right_high) + dot(grad, right_low)
        else:
            grad_high, grad_low = halves(grad_ref[:, span])
            turned = dot(grad_high, right_high) + (
                dot(grad_high, right_low) + dot(grad_low, right_high)
            )
        high, low = halves(turned)
        turned = dot(turn_high[...], high) + (
            dot(turn_low[...], high) + dot(turn_high[...], low)
        )
        turned = turned * factor
        first = beta_one * first_ref[:, span] + (1.0 - beta_one) * turned
        second = beta_two * second_ref[:, span] + (1.0 - beta_two) * turned * turned
        mean_ref[:, span] = first
        square_ref[:, span] = second
        step = adam_direction(first, second)
        step = dot_t(step.astype(bf16), right_high)
        step = dot(left_high[...], step.astype(bf16))
        weight = weight_ref[:, span]
        weight = weight - learn_rate * (step + decay_rate * weight)
        new_ref[:, span] = weight
        copy_ref[:, span] = weight.astype(bf16)


def rotated_update(weight, first, second, grad, base, left, right, factor, tile_rows):
    rows, cols = weight.shape
    tile_cols = WIDTH
    tile = pl.BlockSpec((tile_rows, tile_cols), lambda i, j: (i, j))
    if base is None:
        grad_tile = tile
    else:
        across = cols // tile_cols
        grad_tile = pl.BlockSpec(
            (tile_rows, tile_cols), lambda i, j: (base + i * across + j, 0)
        )
    return pl.pallas_call(
        adam_kernel,
        grid=(rows // tile_rows, cols // tile_cols),
        in_specs=[
            pl.BlockSpec(memory_space=pltpu.SMEM),
            tile,
            tile,
            tile,
            grad_tile,
            pl.BlockSpec((tile_rows // BLOCK, BLOCK, BLOCK), lambda i, j: (i, 0, 0)),
            pl.BlockSpec((tile_cols // BLOCK, BLOCK, BLOCK), lambda i, j: (j, 0, 0)),
        ],
        out_specs=[tile] * 4,
        out_shape=[jax.ShapeDtypeStruct((rows, cols), f32)] * 3
        + [jax.ShapeDtypeStruct((rows, cols), bf16)],
        scratch_shapes=[pltpu.VMEM((tile_rows, tile_rows), bf16)] * 3,
        compiler_params=pltpu.CompilerParams(vmem_limit_bytes=48 * 1024 * 1024),
        name="rotated_adam",
    )(factor.reshape(1), weight, first, second, grad, left, right)


def bits_of(extent):
    return extent.bit_length() - 1


def flipped(index, mask, count):
    for bit in range(count):
        if mask >> bit & 1:
            index = index + (1 - 2 * (index // (1 << bit) % 2)) * (1 << bit)
    return index


def greet(n_wide, n_narrow):
    barrier = pltpu.get_barrier_semaphore()
    count = 0
    for axis, extent in (("narrow", n_narrow), ("wide", n_wide)):
        me = lax.axis_index(axis)
        for bit in range(bits_of(extent)):
            pl.semaphore_signal(
                barrier,
                inc=1,
                device_id={axis: flipped(me, 1 << bit, bits_of(extent))},
                device_id_type=pl.DeviceIdType.MESH,
            )
            count = count + 1
    pl.semaphore_wait(barrier, count)


def remote(source, target, send_sem, recv_sem, axis, peer):
    return pltpu.make_async_remote_copy(
        src_ref=source,
        dst_ref=target,
        send_sem=send_sem,
        recv_sem=recv_sem,
        device_id={axis: peer},
        device_id_type=pl.DeviceIdType.MESH,
    )


def route(path, step, count):
    return (step + path) % count


ROW_TAIL = 2048
TAIL = 32
ALIGN = 16
SHEET = 384


def shard_rows(shard):
    rows = (shard + WIDTH - 2) // WIDTH + 1 + ALIGN
    return -(-rows // 32) * 32


def shard_start(number, shard):
    return number * shard // WIDTH // ALIGN * ALIGN


def flat_rows(n_narrow, shard):
    last = shard_start(n_narrow - 1, shard) + shard_rows(shard)
    return max(-(-last // ALIGN) * ALIGN, 2112)


def silu_slope(value):
    gate = jax.nn.sigmoid(value)
    return gate * (1.0 + value * (1.0 - gate))


def own_columns(value, n_narrow):
    here = lax.axis_index("narrow")
    width = value.shape[1] // n_narrow
    result = value[:, :width]
    for number in range(1, n_narrow):
        result = jnp.where(
            here == number, value[:, number * width : (number + 1) * width], result
        )
    return result


def gather_kernel(n_wide, n_narrow, images, shard, *refs):
    count = 5
    shards = refs[:count]
    adaptive_ref, info_ref = refs[count : count + 2]
    outs = refs[count + 2 : count + 14]
    flat, sheet, time_pre, condition, own_act, adaptive_low, mods_ref, total_ref = outs[4:12]
    scratch = refs[count + 14 :]
    gathered = scratch[0]
    wides = scratch[1 : count + 1]
    lows = scratch[count + 1 : 2 * count + 1]
    (
        adaptive_wide,
        info_all,
        lined,
        part,
        part_in,
        load_sem,
        keep_sem,
        send_sem,
        recv_sem,
        core_send,
        core_recv,
        info_sem,
        info_send,
        info_recv,
        part_send,
        part_recv,
    ) = scratch[2 * count + 1 :]
    fulls = (gathered,) + tuple(outs[:4])
    here = lax.axis_index("narrow")
    there = lax.axis_index("wide")
    core = there % 2
    n_bits = bits_of(n_narrow)
    w_bits = bits_of(n_wide)
    sibling = flipped(there, 1, w_bits)

    loads = [
        pltpu.make_async_copy(shards[number], wides[number], load_sem.at[number])
        for number in range(count)
    ]
    loads.append(pltpu.make_async_copy(adaptive_ref, adaptive_wide, load_sem.at[count]))
    for load in loads:
        load.start()
    slot = there * n_narrow + here
    info_own = pltpu.make_async_copy(info_ref, info_all.at[pl.ds(slot, 1)], info_sem)
    info_own.start()
    greet(n_wide, n_narrow)
    sends = []

    def region(number, owner, half, path):
        rows, cols = shards[number].shape
        return (
            pl.ds(pl.multiple_of(owner * rows + half * (rows // 2), 16), rows // 2),
            pl.ds(path * (cols // 2), cols // 2),
        )

    def narrow_step(number, step):
        for path in range(2):
            bit = route(path, step, n_bits)
            peer = flipped(here, 1 << bit, n_bits)
            done = sum(1 << route(path, earlier, n_bits) for earlier in range(step))
            for mask in range(n_narrow):
                if mask & ~done:
                    continue
                place = region(number, flipped(here, mask, n_bits), core, path)
                arrives = mask | 1 << bit
                if mask == 0:
                    rows, cols = shards[number].shape
                    source = lows[number].at[
                        pl.ds(pl.multiple_of(core * (rows // 2), 16), rows // 2),
                        pl.ds(path * (cols // 2), cols // 2),
                    ]
                else:
                    source = fulls[number].at[place]
                copy = remote(
                    source,
                    fulls[number].at[place],
                    send_sem.at[number, path, arrives - 1],
                    recv_sem.at[number, path, arrives - 1],
                    "narrow",
                    peer,
                )
                copy.start()
                sends.append(copy)

    def arrive(number, step):
        for path in range(2):
            bit = route(path, step, n_bits)
            done = sum(1 << route(path, earlier, n_bits) for earlier in range(step))
            for mask in range(n_narrow):
                if mask & ~done:
                    continue
                arrived = mask | 1 << bit
                place = region(number, flipped(here, arrived, n_bits), core, path)
                remote(
                    fulls[number].at[place],
                    fulls[number].at[place],
                    send_sem.at[number, path, arrived - 1],
                    recv_sem.at[number, path, arrived - 1],
                    "narrow",
                    flipped(here, 1 << bit, n_bits),
                ).wait_recv()
                copy = remote(
                    fulls[number].at[place],
                    fulls[number].at[place],
                    core_send.at[number, path, arrived - 1],
                    core_recv.at[number, path, arrived - 1],
                    "wide",
                    sibling,
                )
                copy.start()
                sends.append(copy)

    def from_sibling(number):
        for path in range(2):
            for mask in range(1, n_narrow):
                place = region(number, flipped(here, mask, n_bits), 1 - core, path)
                remote(
                    fulls[number].at[place],
                    fulls[number].at[place],
                    core_send.at[number, path, mask - 1],
                    core_recv.at[number, path, mask - 1],
                    "wide",
                    sibling,
                ).wait_recv()

    def cast_rows(source, target):
        def cast(index, carry):
            span = pl.ds(pl.multiple_of(index * 16, 16), 16)
            target[span, :] = source[span, :].astype(bf16)
            return carry

        lax.fori_loop(0, source.shape[0] // 16, cast, 0)

    keeps = []

    def begin(number):
        loads[number].wait()
        rows = shards[number].shape[0]
        cast_rows(wides[number], lows[number])
        keep = pltpu.make_async_copy(
            lows[number],
            fulls[number].at[pl.ds(pl.multiple_of(here * rows, 16), rows)],
            keep_sem.at[number],
        )
        keep.start()
        keeps.append(keep)
        narrow_step(number, 0)

    places = [("narrow", bit, n_bits) for bit in range(n_bits)]
    places += [("wide", bit, w_bits) for bit in range(w_bits)]

    def info_copy(position):
        axis, bit, bits = places[position]
        width = 1 << position
        base = slot // width * width
        return remote(
            info_all.at[pl.ds(base, width)],
            info_all.at[pl.ds(base, width)],
            info_send.at[position],
            info_recv.at[position],
            axis,
            flipped(lax.axis_index(axis), 1 << bit, bits),
        )

    info_own.wait()
    info_copy(0).start()
    begin(0)
    for position in range(len(places)):
        info_copy(position).wait()
        if position + 1 < len(places):
            info_copy(position + 1).start()
    begin(1)
    for step in range(n_bits):
        arrive(0, step)
        if step + 1 < n_bits:
            narrow_step(0, step + 1)
    for number in range(2, count):
        begin(number)
    from_sibling(0)
    keeps[0].wait()

    height = shards[0].shape[0]
    reached = 0
    for number in range(n_narrow):
        start = shard_start(number, shard)
        overlap = max(reached - start, 0)
        block = number * height
        if overlap:
            flat[start:reached, :] = (
                flat[start:reached, :].astype(f32)
                + gathered[block : block + overlap, :].astype(f32)
            ).astype(bf16)
        flat[start + overlap : start + height, :] = gathered[block + overlap : block + height, :]
        reached = start + height
    if reached < flat.shape[0]:
        flat[reached:, :] = jnp.zeros((flat.shape[0] - reached, WIDTH), bf16)

    devices = n_wide * n_narrow
    for number in range(devices):
        sheet[number * images : (number + 1) * images, :] = info_all[number, :images, :]
    weights = sheet[:, FREQS + 1 : FREQS + 2]
    total_ref[...] = jnp.sum(weights, axis=0, keepdims=True)
    tail = flat[ROW_TAIL : ROW_TAIL + TAIL, :].astype(f32)
    tail_row = ROW_BIAS - ROW_TAIL
    value = dot(sheet[:, :FREQS].astype(bf16), flat[ROW_TIME_ONE:ROW_TIME_TWO, :])
    value = value + tail[tail_row + 1 : tail_row + 2]
    time_pre[...] = value
    act = jax.nn.silu(value).astype(bf16)
    value = dot(act, flat[ROW_TIME_TWO:ROW_TABLE, :]) + tail[tail_row + 2 : tail_row + 3]
    labels = lax.broadcasted_iota(jnp.int32, (sheet.shape[0], 1008), 1).astype(f32)
    pick = jnp.where(sheet[:, FREQS : FREQS + 1] == labels, 1.0, 0.0).astype(bf16)
    value = value + dot(pick, flat[ROW_TABLE : ROW_TABLE + 1008, :])
    condition[...] = value
    act = own_columns(jax.nn.silu(value), n_narrow)
    own_act[...] = act.astype(bf16)
    lined[...] = act

    loads[count].wait()
    cast_rows(adaptive_wide, adaptive_low)
    group = n_narrow * images
    near = lined[pl.ds(pl.multiple_of(there * group, 8), group), :]
    blocks = []
    for number in range(n_narrow):
        blocks.append(near[number * images : (number + 1) * images])
        blocks.append(jnp.zeros((8 - images, near.shape[1]), f32))
    near = jnp.concatenate(blocks, axis=0).astype(bf16)
    for index in range(8):
        span = slice(index * WIDTH, (index + 1) * WIDTH)
        value = dot(near, adaptive_low[:, span])
        for number in range(n_narrow):
            part[0, number, :, span] = value[8 * number : 8 * number + 8]

    def part_copy(step, mask):
        bit = 1 << step
        return remote(
            part.at[step, flipped(here, mask, n_bits)],
            part_in.at[step, flipped(here, mask, n_bits)],
            part_send.at[step, mask],
            part_recv.at[step, mask],
            "narrow",
            flipped(here, bit, n_bits),
        )

    def part_back(step, mask):
        bit = 1 << step
        owner = flipped(here, mask - bit, n_bits)
        return remote(
            part_in.at[step, owner],
            part_in.at[step, owner],
            part_send.at[step, mask],
            part_recv.at[step, mask],
            "narrow",
            flipped(here, bit, n_bits),
        ), owner

    for step in range(n_bits):
        bit = 1 << step
        masks = [
            mask for mask in range(n_narrow) if mask & bit and not mask & (bit - 1)
        ]
        for mask in masks:
            copy = part_copy(step, mask)
            copy.start()
            sends.append(copy)
        for mask in masks:
            back, owner = part_back(step, mask)
            back.wait_recv()
            if step + 1 < n_bits:
                part[step + 1, owner] = part[step, owner] + part_in[step, owner]
            else:
                value = part[step, owner] + part_in[step, owner]
                for image in range(images):
                    for index in range(8):
                        mods_ref[image, index : index + 1, :] = (
                            value[image : image + 1, index * WIDTH : (index + 1) * WIDTH]
                            + tail[tail_row + 9 + index : tail_row + 10 + index]
                        )

    for step in range(n_bits):
        for number in range(1, count):
            arrive(number, step)
            if step + 1 < n_bits:
                narrow_step(number, step + 1)
    for number in range(1, count):
        from_sibling(number)
    for keep in keeps[1:]:
        keep.wait()
    for copy in sends:
        copy.wait_send()


def gather_all(n_wide, n_narrow, images, shard, shards, adaptive, info):
    count = len(shards)
    any_space = pl.BlockSpec(memory_space=pl.ANY)
    vmem = pl.BlockSpec(memory_space=pltpu.VMEM)
    devices = n_wide * n_narrow
    n_bits = bits_of(n_narrow)
    rows = adaptive.shape[0]
    dma = pltpu.SemaphoreType.DMA
    total = devices * images
    return pl.pallas_call(
        partial(gather_kernel, n_wide, n_narrow, images, shard),
        in_specs=[any_space] * (count + 2),
        out_specs=[any_space] * (count - 1) + [vmem] * 8,
        out_shape=[
            jax.ShapeDtypeStruct((piece.shape[0] * n_narrow, piece.shape[1]), bf16)
            for piece in shards[1:]
        ]
        + [
            jax.ShapeDtypeStruct((flat_rows(n_narrow, shard), WIDTH), bf16),
            jax.ShapeDtypeStruct((total, SHEET), f32),
            jax.ShapeDtypeStruct((total, WIDTH), f32),
            jax.ShapeDtypeStruct((total, WIDTH), f32),
            jax.ShapeDtypeStruct((total, rows), bf16),
            jax.ShapeDtypeStruct(adaptive.shape, bf16),
            jax.ShapeDtypeStruct((images, 8, WIDTH), f32),
            jax.ShapeDtypeStruct((1, 1), f32),
        ],
        scratch_shapes=[pltpu.VMEM((shards[0].shape[0] * n_narrow, WIDTH), bf16)]
        + [pltpu.VMEM(piece.shape, f32) for piece in shards]
        + [pltpu.VMEM(piece.shape, bf16) for piece in shards]
        + [
            pltpu.VMEM(adaptive.shape, f32),
            pltpu.VMEM((devices,) + info.shape[1:], f32),
            pltpu.VMEM((total, rows), f32),
            pltpu.VMEM((n_bits, n_narrow, 8, 8 * WIDTH), f32),
            pltpu.VMEM((n_bits, n_narrow, 8, 8 * WIDTH), f32),
            dma((count + 1,)),
            dma((count,)),
            dma((count, 2, n_narrow - 1)),
            dma((count, 2, n_narrow - 1)),
            dma((count, 2, n_narrow - 1)),
            dma((count, 2, n_narrow - 1)),
            dma,
            dma((bits_of(devices),)),
            dma((bits_of(devices),)),
            dma((n_bits, n_narrow)),
            dma((n_bits, n_narrow)),
        ],
        compiler_params=pltpu.CompilerParams(
            collective_id=0, has_side_effects=True, vmem_limit_bytes=56 * 1024 * 1024
        ),
        name="gather_weights",
    )(*shards, adaptive, info)


RING = 4


def reduce_kernel(n_wide, n_narrow, images, shard, *refs):
    grad_refs = refs[:4]
    (
        g_mods_ref,
        g_patch_ref,
        g_final_ref,
        g_bias_ref,
        adaptive_low,
        sheet,
        time_pre,
        condition,
        own_act,
        time_two,
    ) = refs[4:14]
    out_ref, adaptive_out, rows_out, window_out, totals_out, clip_out = refs[14:20]
    scratch = refs[20:]
    own, from_core, to_near, from_near, to_far, from_far, acc, acc_far = scratch[:8]
    load_sem, core_sem, near_sem, far_sem, back_sem, last_sem = scratch[8:14]
    (
        mods_all,
        small_out,
        small_in,
        act_all,
        stage,
        norm_out,
        norm_in,
        squares,
        mods_sem,
        small_sem,
        act_sem,
        rows_sem,
        norm_sem,
    ) = scratch[14:]
    here = lax.axis_index("narrow")
    there = lax.axis_index("wide")
    core = there % 2
    n_bits = bits_of(n_narrow)
    w_bits = bits_of(n_wide)
    far_steps = w_bits - 1
    sibling = flipped(there, 1, w_bits)
    chunks, _, half, width = out_ref.shape
    side = width // 2

    leaving = []
    for path in range(2):
        done = 0
        place = 0
        steps = []
        for step in range(n_bits):
            bit = 1 << route(path, step, n_bits)
            masks = [mask for mask in range(n_narrow) if mask & bit and not mask & done]
            steps.append((bit, {mask: place + spot for spot, mask in enumerate(masks)}))
            place = place + len(masks)
            done = done | bit
        leaving.append(steps)

    parts = [(0, half, 0, width)]
    gives = []
    for step in range(far_steps):
        low, rows, left, cols = parts[-1]
        mine = there // (2 << step) % 2
        if rows % 32 == 0:
            keep = (low + mine * (rows // 2), rows // 2, left, cols)
            give = (low + (1 - mine) * (rows // 2), rows // 2, left, cols)
        elif cols % 256 == 0:
            keep = (low, rows, left + mine * (cols // 2), cols // 2)
            give = (low, rows, left + (1 - mine) * (cols // 2), cols // 2)
        else:
            keep = parts[-1]
            give = parts[-1]
        parts.append(keep)
        gives.append(give)
    traded = [gives[step] is not parts[step] for step in range(far_steps)]

    def window(part):
        low, rows, left, cols = part
        if not isinstance(low, int):
            low = pl.multiple_of(low, 16)
        if not isinstance(left, int):
            left = pl.multiple_of(left, 128)
        return (pl.ds(low, rows), pl.ds(left, cols))

    def keep_copy(k, grad_ref, first):
        start = pl.multiple_of((k - first) * 2 * half + core * half, 16)
        return pltpu.make_async_copy(
            grad_ref.at[:, pl.ds(start, half), :], own.at[k % RING], load_sem.at[k]
        )

    def start_keep(k):
        first = 0
        for grad_ref in grad_refs:
            tiles = grad_ref.shape[1] // (2 * half)

            @pl.when(jnp.logical_and(k >= first, k < first + tiles))
            def _(grad_ref=grad_ref, first=first):
                keep_copy(k, grad_ref, first).start()

            first = first + tiles

    def give_copy(k, grad_ref, first):
        start = pl.multiple_of((k - first) * 2 * half + (1 - core) * half, 16)
        return remote(
            grad_ref.at[:, pl.ds(start, half), :],
            from_core.at[k],
            core_sem.at[0, k],
            core_sem.at[1, k],
            "wide",
            sibling,
        )

    def near_copy(path, k, step):
        bit, masks = leaving[path][step]
        spots = pl.ds(min(masks.values()), len(masks))
        return remote(
            to_near.at[path, k, spots],
            from_near.at[path, k, spots],
            near_sem.at[0, path, k, step],
            near_sem.at[1, path, k, step],
            "narrow",
            flipped(here, bit, n_bits),
        )

    def far_copy(k, step, part):
        return remote(
            to_far.at[(k, step) + window(part)],
            from_far.at[(k, step) + window(part)],
            far_sem.at[0, k, step],
            far_sem.at[1, k, step],
            "wide",
            flipped(there, 2 << step, w_bits),
        )

    def back_copy(k, step, part):
        place = (k, core) + window(part)
        return remote(
            out_ref.at[place],
            out_ref.at[place],
            back_sem.at[0, k, step],
            back_sem.at[1, k, step],
            "wide",
            flipped(there, 2 << step, w_bits),
        )

    def last_copy(k, side_of):
        return remote(
            out_ref.at[k, side_of],
            out_ref.at[k, side_of],
            last_sem.at[0, k],
            last_sem.at[1, k],
            "wide",
            sibling,
        )

    def place_near(path, k, step, mask, total):
        columns = pl.ds(path * side, side)
        ring = k % RING
        if step == n_bits:
            acc_far[ring, :, columns] = total
        elif mask in leaving[path][step][1]:
            to_near[path, k, leaving[path][step][1][mask]] = total.astype(bf16)
        else:
            acc[ring, mask, :, columns] = total

    def stage_core(k):
        keep_copy(k, grad_refs[0], k).wait()
        give_copy(k, grad_refs[0], k).wait_recv()
        for path in range(2):
            columns = pl.ds(path * side, side)
            for mask in range(n_narrow):
                owner = flipped(here, mask, n_bits)
                total = own[k % RING, owner, :, columns].astype(f32) + from_core[
                    k, owner, :, columns
                ].astype(f32)
                place_near(path, k, 0, mask, total)
            near_copy(path, k, 0).start()
        start_keep(k + RING - 1)

    def stage_near(step, k):
        ring = k % RING
        for path in range(2):
            columns = pl.ds(path * side, side)
            near_copy(path, k, step).wait_recv()
            bit, masks = leaving[path][step]
            for mask, spot in masks.items():
                total = acc[ring, mask - bit, :, columns] + from_near[path, k, spot].astype(f32)
                place_near(path, k, step + 1, mask - bit, total)
            if step + 1 < n_bits:
                near_copy(path, k, step + 1).start()
        if step + 1 == n_bits:
            start_far(0, k)

    def start_far(step, k):
        ring = k % RING
        if step < far_steps:
            place = window(gives[step])
            to_far[(k, step) + place] = acc_far[(ring,) + place].astype(bf16)
            far_copy(k, step, gives[step]).start()
        else:
            place = window(parts[step])
            out_ref[(k, core) + place] = acc_far[(ring,) + place].astype(bf16)
            start_back(far_steps - 1, k)

    def stage_far(step, k):
        ring = k % RING
        far_copy(k, step, parts[step + 1]).wait_recv()
        place = window(parts[step + 1])
        if traded[step]:
            mine = acc_far[(ring,) + place]
        else:
            mine = to_far[(k, step) + place].astype(f32)
        acc_far[(ring,) + place] = mine + from_far[(k, step) + place].astype(f32)
        start_far(step + 1, k)

    def start_back(step, k):
        while step >= 0 and not traded[step]:
            step = step - 1
        if step >= 0:
            back_copy(k, step, parts[step + 1]).start()
        else:
            last_copy(k, core).start()

    def stage_back(step, k):
        back_copy(k, step, gives[step]).wait_recv()
        start_back(step - 1, k)

    def add_squares(value):
        squares[...] += jnp.sum(value * value, axis=0, keepdims=True)

    def stage_last(k):
        last_copy(k, 1 - core).wait_recv()
        for number in range(2):
            add_squares(out_ref[k, number].astype(f32))

    stages = [stage_core]
    stages += [partial(stage_near, step) for step in range(n_bits)]
    stages += [partial(stage_far, step) for step in range(far_steps)]
    stages += [partial(stage_back, step) for step in reversed(range(far_steps)) if traded[step]]
    stages += [stage_last]

    places = [("narrow", bit, n_bits) for bit in range(n_bits)]
    places += [("wide", bit, w_bits) for bit in range(w_bits)]
    hops = len(places)
    slot = there * n_narrow + here
    per = images * 8
    count = n_wide * n_narrow * images

    def beside(axis, bit, bits, source, target, sem, position):
        return remote(
            source,
            target,
            sem.at[0, position],
            sem.at[1, position],
            axis,
            flipped(lax.axis_index(axis), 1 << bit, bits),
        )

    def mods_copy(position):
        width = 1 << position
        block = mods_all.at[pl.ds(slot // width * width, width)]
        return beside(*places[position], block, block, mods_sem, position)

    def small_copy(position):
        return beside(
            *places[position], small_out.at[position], small_in.at[position], small_sem, position
        )

    def act_copy(position):
        width = 1 << position
        block = act_all.at[pl.ds(here // width * width, width)]
        return beside(*places[position], block, block, act_sem, position)

    def small_total():
        return small_out[hops - 1] + small_in[hops - 1]

    def rows_copy(start, rows, position):
        return pltpu.make_async_copy(
            stage.at[pl.ds(0, rows)], rows_out.at[pl.ds(start, rows)], rows_sem.at[position]
        )

    height = window_out.shape[0]

    def window_copy():
        start = here * shard // (WIDTH * ALIGN) * ALIGN
        return pltpu.make_async_copy(
            rows_out.at[pl.ds(pl.multiple_of(start, ALIGN), height)], window_out, rows_sem.at[2]
        )

    def spread_hop(position):
        if position == 0:
            mods_all[slot] = g_mods_ref[...].astype(bf16)
            small_out[0, 0:PATCH] = g_patch_ref[...]
            small_out[0, PATCH : 2 * PATCH] = g_final_ref[...]
            small_out[0, 2 * PATCH : 2 * PATCH + 8] = g_bias_ref[...]
        else:
            mods_copy(position - 1).wait_recv()
            small_copy(position - 1).wait_recv()
            if position < hops:
                small_out[position] = small_out[position - 1] + small_in[position - 1]
        if position < hops:
            mods_copy(position).start()
            small_copy(position).start()

    def which_mod(shape):
        return lax.broadcasted_iota(jnp.int32, shape, 0) % 8

    def send_act():
        everything = mods_all[...].reshape(count * 8, WIDTH)
        kind = which_mod((count * 8, act_all.shape[2]))
        total = jnp.zeros((count * 8, act_all.shape[2]), f32)
        for index in range(8):
            span = slice(index * WIDTH, (index + 1) * WIDTH)
            value = dot_t(everything, adaptive_low[:, span])
            total = total + jnp.where(kind == index, value, 0.0)
        act_all[here] = jnp.sum(total.reshape(count, 8, -1), axis=1)
        act_copy(0).start()

    def act_hop(position):
        act_copy(position - 1).wait_recv()
        if position < n_bits:
            act_copy(position).start()

    def grad_condition():
        grad = jnp.concatenate([act_all[number] for number in range(n_narrow)], axis=1)
        return grad * silu_slope(condition[...])

    def grad_time():
        low = grad_condition().astype(bf16)
        before = time_pre[...]
        return low, (dot_t(low, time_two[...]) * silu_slope(before)).astype(bf16)

    def upper_rows():
        low, first = grad_time()
        stage[0:PATCH, :] = small_total()[0:PATCH]
        stage[ROW_TIME_ONE:ROW_TIME_TWO, :] = dot_s(sheet[:, :FREQS].astype(bf16), first)
        act = jax.nn.silu(time_pre[...]).astype(bf16)
        stage[ROW_TIME_TWO:ROW_TABLE, :] = dot_s(act, low)
        rows_copy(0, ROW_TABLE, 0).start()

    def lower_rows():
        rows_copy(0, ROW_TABLE, 0).wait()
        grad = grad_condition()
        low, first = grad_time()
        labels = lax.broadcasted_iota(jnp.int32, (count, 1008), 1).astype(f32)
        pick = jnp.where(sheet[:, FREQS : FREQS + 1] == labels, 1.0, 0.0).astype(bf16)
        high, rest = halves(grad)
        rest = grad - high.astype(f32)
        middle, rest = halves(rest)
        table = dot_s(pick, high) + (dot_s(pick, middle) + dot_s(pick, rest))
        stage[0:1008, :] = table
        small = small_total()
        base = ROW_FINAL - ROW_TABLE
        stage[base : base + PATCH, :] = small[PATCH : 2 * PATCH]
        base = ROW_BIAS - ROW_TABLE
        bias = small[2 * PATCH : 2 * PATCH + 8]
        stage[base : base + 1, :] = bias[0:1]
        stage[base + 1 : base + 2, :] = jnp.sum(first.astype(f32), axis=0, keepdims=True)
        stage[base + 2 : base + 3, :] = jnp.sum(low.astype(f32), axis=0, keepdims=True)
        stage[base + 3 : base + 4, :] = bias[1:2]
        stage[base + 4 : base + 8, :] = bias[4:8]
        stage[base + 8 : base + 9, :] = bias[2:3]
        stage[base + 9 : base + 17, :] = jnp.sum(
            mods_all[...].astype(f32).reshape(count, 8, WIDTH), axis=0
        )
        lane = lax.broadcasted_iota(jnp.int32, (1, WIDTH), 1)
        stage[base + 17 : base + 18, :] = jnp.where(lane < PATCH, bias[3:4], 0.0)
        stage[base + 18 :, :] = jnp.zeros((stage.shape[0] - base - 18, WIDTH), f32)
        totals_out[...] = bias
        rows_copy(ROW_TABLE, stage.shape[0], 1).start()

    def adaptive_rows():
        everything = mods_all[...].reshape(count * 8, WIDTH)
        act = own_act[...].astype(f32)
        act = jnp.broadcast_to(act[:, None, :], (count, 8, act.shape[1]))
        act = act.reshape(count * 8, -1).astype(bf16)
        kind = which_mod(act.shape)
        for index in range(8):
            span = slice(index * WIDTH, (index + 1) * WIDTH)
            here_act = jnp.where(kind == index, act, jnp.zeros((), bf16))
            value = dot_s(here_act, everything)
            add_squares(value)
            adaptive_out[:, span] = value.astype(bf16)
        rows_copy(ROW_TABLE, stage.shape[0], 1).wait()
        window_copy().start()

    def window_squares():
        window_copy().wait()
        start = here * shard // (WIDTH * ALIGN) * ALIGN
        first = here * shard - start * WIDTH
        value = window_out[...]
        spot = (
            lax.broadcasted_iota(jnp.int32, value.shape, 0) * WIDTH
            + lax.broadcasted_iota(jnp.int32, value.shape, 1)
        )
        inside = jnp.logical_and(spot >= first, spot < first + shard)
        add_squares(jnp.where(inside, value, 0.0))

    asides = [partial(spread_hop, position) for position in range(hops)]

    def last_hop():
        spread_hop(hops)
        send_act()

    asides += [last_hop]
    asides += [partial(act_hop, position) for position in range(1, n_bits)]

    def last_act():
        act_hop(n_bits)
        upper_rows()

    asides += [last_act, lower_rows, adaptive_rows, window_squares]

    squares[...] = jnp.zeros_like(squares)
    greet(n_wide, n_narrow)
    first = 0
    for grad_ref in grad_refs:
        tiles = grad_ref.shape[1] // (2 * half)

        def begin(k, carry, grad_ref=grad_ref, first=first):
            give_copy(k, grad_ref, first).start()
            return carry

        lax.fori_loop(first, first + tiles, begin, 0)
        first = first + tiles
    for k in range(RING - 1):
        start_keep(jnp.int32(k))

    def wave(t, carry):
        for number, stage in enumerate(stages):
            k = t - number

            @pl.when(jnp.logical_and(k >= 0, k < chunks))
            def _(stage=stage, k=k):
                stage(k)

        for number, aside in enumerate(asides):

            @pl.when(t == number)
            def _(aside=aside):
                aside()

        return carry

    lax.fori_loop(0, max(chunks + len(stages) - 1, len(asides)), wave, 0)

    def finish(k, carry):
        give_copy(k, grad_refs[0], k).wait_send()
        for path in range(2):
            for step in range(n_bits):
                near_copy(path, k, step).wait_send()
        for step in range(far_steps):
            far_copy(k, step, gives[step]).wait_send()
            if traded[step]:
                back_copy(k, step, parts[step + 1]).wait_send()
        last_copy(k, core).wait_send()
        return carry

    lax.fori_loop(0, chunks, finish, 0)
    for position in range(hops):
        mods_copy(position).wait_send()
        small_copy(position).wait_send()
    for position in range(n_bits):
        act_copy(position).wait_send()

    total = jnp.sum(squares[...], axis=1, keepdims=True)
    value = jnp.broadcast_to(total, norm_out.shape[1:])
    for position in range(n_bits):
        norm_out[position] = value
        copy = beside(
            *places[position], norm_out.at[position], norm_in.at[position], norm_sem, position
        )
        copy.start()
        copy.wait()
        value = value + norm_in[position]
    norm = jnp.sqrt(value)
    row = lax.broadcasted_iota(jnp.int32, value.shape, 0)
    clip_out[...] = jnp.where(row == 0, norm, clip_limit / jnp.maximum(norm, clip_limit))


def reduce_all(n_wide, n_narrow, images, shard, grads, asides):
    rows = WIDTH // n_narrow
    chunks = sum(grad.shape[1] for grad in grads) // rows
    half = rows // 2
    far = bits_of(n_wide) - 1
    devices = n_wide * n_narrow
    hops = bits_of(devices)
    count = devices * images
    dma = pltpu.SemaphoreType.DMA
    any_space = pl.BlockSpec(memory_space=pl.ANY)
    vmem = pl.BlockSpec(memory_space=pltpu.VMEM)
    height = flat_rows(n_narrow, shard)
    out, adaptive, _, window, totals, clip = pl.pallas_call(
        partial(reduce_kernel, n_wide, n_narrow, images, shard),
        in_specs=[any_space] * 4 + [vmem] * len(asides),
        out_specs=[vmem, vmem, any_space, vmem, vmem, vmem],
        out_shape=[
            jax.ShapeDtypeStruct((chunks, 2, half, WIDTH), bf16),
            jax.ShapeDtypeStruct((rows, 8 * WIDTH), bf16),
            jax.ShapeDtypeStruct((height, WIDTH), f32),
            jax.ShapeDtypeStruct((shard_rows(shard), WIDTH), f32),
            jax.ShapeDtypeStruct((8, WIDTH), f32),
            jax.ShapeDtypeStruct((8, 128), f32),
        ],
        scratch_shapes=[
            pltpu.VMEM((RING, n_narrow, half, WIDTH), bf16),
            pltpu.VMEM((chunks, n_narrow, half, WIDTH), bf16),
            pltpu.VMEM((2, chunks, n_narrow - 1, half, WIDTH // 2), bf16),
            pltpu.VMEM((2, chunks, n_narrow - 1, half, WIDTH // 2), bf16),
            pltpu.VMEM((chunks, far, half, WIDTH), bf16),
            pltpu.VMEM((chunks, far, half, WIDTH), bf16),
            pltpu.VMEM((RING, n_narrow, half, WIDTH), f32),
            pltpu.VMEM((RING, half, WIDTH), f32),
            dma((chunks,)),
            dma((2, chunks)),
            dma((2, 2, chunks, bits_of(n_narrow))),
            dma((2, chunks, far)),
            dma((2, chunks, far)),
            dma((2, chunks)),
            pltpu.VMEM((devices, images * 8, WIDTH), bf16),
            pltpu.VMEM((hops, 2 * PATCH + 8, WIDTH), f32),
            pltpu.VMEM((hops, 2 * PATCH + 8, WIDTH), f32),
            pltpu.VMEM((n_narrow, count, rows), f32),
            pltpu.VMEM((height - ROW_TABLE, WIDTH), f32),
            pltpu.VMEM((bits_of(n_narrow), 8, 128), f32),
            pltpu.VMEM((bits_of(n_narrow), 8, 128), f32),
            pltpu.VMEM((1, WIDTH), f32),
            dma((2, hops)),
            dma((2, hops)),
            dma((2, bits_of(n_narrow))),
            dma((3,)),
            dma((2, bits_of(n_narrow))),
        ],
        compiler_params=pltpu.CompilerParams(
            collective_id=1, has_side_effects=True, vmem_limit_bytes=62 * 1024 * 1024
        ),
        cost_estimate=pl.CostEstimate(
            flops=10**8, bytes_accessed=300 * 10**6, transcendentals=0
        ),
        name="reduce_gradients",
    )(*grads, *asides)
    return out.reshape(chunks * rows, WIDTH), adaptive, window, totals, clip


def weight_kernel(left_ref, right_ref, out_ref):
    value = dot_s(left_ref[...], right_ref[...]).astype(bf16)
    out_ref[...] = value.reshape(out_ref.shape)


def weight_blocks(n_narrow, inputs, gradient):
    tokens, depth = inputs.shape
    across = gradient.shape[1] // WIDTH
    down = depth // WIDTH
    rows = WIDTH // n_narrow
    if down == 1:
        grid = across
        left = pl.BlockSpec((tokens, WIDTH), lambda i: (0, 0))
        right = pl.BlockSpec((tokens, WIDTH), lambda i: (0, i))
        out = pl.BlockSpec((n_narrow, rows, WIDTH), lambda i: (0, i, 0))
        shape = (n_narrow, across * rows, WIDTH)
    else:
        grid = down
        left = pl.BlockSpec((tokens, WIDTH), lambda i: (0, i))
        right = pl.BlockSpec((tokens, WIDTH), lambda i: (0, 0))
        out = pl.BlockSpec((WIDTH, WIDTH), lambda i: (i, 0))
        shape = (depth, WIDTH)
    result = pl.pallas_call(
        weight_kernel,
        grid=(grid,),
        in_specs=[left, right],
        out_specs=out,
        out_shape=jax.ShapeDtypeStruct(shape, bf16),
        compiler_params=pltpu.CompilerParams(vmem_limit_bytes=48 * 1024 * 1024),
        name="weight_gradient",
    )(inputs, gradient)
    return result.reshape(n_narrow, -1, WIDTH)


def dot_s(left, right):
    return lax.dot_general(left, right, (((0,), (0,)), ((), ())), preferred_element_type=f32)


def center(hidden):
    centered = hidden - jnp.mean(hidden, axis=-1, keepdims=True)
    scale = lax.rsqrt(jnp.mean(centered * centered, axis=-1, keepdims=True) + 1e-06)
    return centered * scale, scale


def center_back(grad, normal, scale):
    return (
        grad
        - jnp.mean(grad, axis=-1, keepdims=True)
        - normal * jnp.mean(grad * normal, axis=-1, keepdims=True)
    ) * scale


def gelu_pair(value):
    rate = math.sqrt(2.0 / math.pi)
    square = value * value
    bend = jnp.tanh(rate * value * (1.0 + 0.044715 * square))
    half = 0.5 * (1.0 + bend)
    slope = half + 0.5 * value * (1.0 - bend * bend) * (rate * (1.0 + 3.0 * 0.044715 * square))
    return value * half, slope


def layer_kernel(
    numbers,
    latent_ref,
    noise_ref,
    mods_ref,
    place_ref,
    patch_ref,
    final_ref,
    tail_ref,
    attend_ref,
    output_ref,
    expand_ref,
    shrink_ref,
    normed_ref,
    mixed_ref,
    normed_two_ref,
    act_ref,
    g_branch_two_ref,
    g_pre_ref,
    g_branch_ref,
    g_triple_ref,
    g_mods_ref,
    g_patch_ref,
    g_final_ref,
    g_bias_ref,
    triple,
    probs,
    slope,
    normal_one,
    normal_two,
    hidden,
    branch,
    g_mixed,
):
    image = pl.program_id(0)
    tokens = SEQUENCE
    wide = 256

    def bias(index):
        spot = ROW_BIAS - ROW_TAIL + index
        return tail_ref[spot : spot + 1, :]

    def bias_wide(ref, first, index):
        across = WIDTH // wide
        return (
            pl.ds(first + index // across, 1),
            pl.ds(pl.multiple_of(index % across * wide, wide), wide),
        )

    def row(index):
        return mods_ref[0, index : index + 1, :]

    @pl.when(image == 0)
    def _():
        for ref in (g_patch_ref, g_final_ref, g_bias_ref):
            ref[...] = jnp.zeros_like(ref)

    moment = numbers[0, image]
    blended = ((1.0 - moment) * latent_ref[0] + moment * noise_ref[0]).astype(bf16)
    target = noise_ref[0] - latent_ref[0]
    start = dot(blended, patch_ref[...]) + bias(0) + place_ref[...]
    hidden[...] = start
    normal, scale_one = center(start)
    normal_one[...] = normal
    normed_ref[...] = (normal * (1.0 + row(1)) + row(0)).astype(bf16)

    def project(index, carry):
        span = pl.ds(pl.multiple_of(index * wide, wide), wide)
        triple[:, span] = dot(normed_ref[...], attend_ref[:, span]).astype(bf16)
        return carry

    lax.fori_loop(0, 3 * WIDTH // wide, project, 0)

    lane = lax.broadcasted_iota(jnp.int32, (tokens, 2 * HEAD_DIM), 1)
    first_half = lane < HEAD_DIM
    zero = jnp.zeros((), bf16)
    rate = HEAD_DIM ** (-0.5)

    def spans_of(pair):
        return [
            pl.ds(pl.multiple_of(part * WIDTH + pair * 2 * HEAD_DIM, 2 * HEAD_DIM), 2 * HEAD_DIM)
            for part in range(3)
        ]

    def attend(pair, carry):
        query_span, key_span, value_span = spans_of(pair)
        query = triple[:, query_span]
        keys = triple[:, key_span]
        values = triple[:, value_span]
        results = []
        for side in range(2):
            mask = first_half if side == 0 else jnp.logical_not(first_half)
            scores = dot_t(jnp.where(mask, query, zero), keys) * rate
            scores = jnp.exp(scores - jnp.max(scores, axis=-1, keepdims=True))
            weights = scores * (1.0 / jnp.sum(scores, axis=-1, keepdims=True))
            probs[2 * pair + side] = weights
            results.append(dot(weights.astype(bf16), values))
        mixed_ref[:, query_span] = jnp.where(first_half, results[0], results[1]).astype(bf16)
        return carry

    lax.fori_loop(0, HEADS // 2, attend, 0)

    value = dot(mixed_ref[...], output_ref[...]) + bias(3)
    branch[...] = value
    value = hidden[...] + row(2) * value
    hidden[...] = value
    normal, scale_two = center(value)
    normal_two[...] = normal
    normed_two_ref[...] = (normal * (1.0 + row(4)) + row(3)).astype(bf16)

    def widen(index, carry):
        span = pl.ds(pl.multiple_of(index * wide, wide), wide)
        before = dot(normed_two_ref[...], expand_ref[:, span])
        before = before + tail_ref[bias_wide(tail_ref, ROW_BIAS - ROW_TAIL + 4, index)]
        after, steep = gelu_pair(before)
        act_ref[:, span] = after.astype(bf16)
        slope[:, span] = steep
        return carry

    lax.fori_loop(0, MLP_WIDTH // wide, widen, 0)

    branch_two = dot(act_ref[...], shrink_ref[...]) + bias(8)
    upper = hidden[...] + row(5) * branch_two
    normal, scale_three = center(upper)
    final = (normal * (1.0 + row(7)) + row(6)).astype(bf16)
    mismatch = dot(final, final_ref[...]) + bias(17)[:, :PATCH] - target
    loss = numbers[2, image] * jnp.sum(mismatch * mismatch)
    grad_out = (numbers[1, image] * mismatch).astype(bf16)

    g_final_ref[...] += dot_s(final, grad_out)
    sums = jnp.sum(grad_out.astype(f32), axis=0, keepdims=True)
    spot = lax.broadcasted_iota(jnp.int32, (1, WIDTH), 1)
    sums = jnp.concatenate([sums, jnp.zeros((1, WIDTH - PATCH), f32)], axis=1)
    g_bias_ref[3:4, :] += jnp.where(spot == PATCH, loss, sums)
    grad = dot_t(grad_out, final_ref[...])
    shift_f = jnp.sum(grad, axis=0, keepdims=True)
    scale_f = jnp.sum(grad * normal, axis=0, keepdims=True)
    grad_upper = center_back((1.0 + row(7)) * grad, normal, scale_three)
    gate_two = jnp.sum(branch_two * grad_upper, axis=0, keepdims=True)
    grad_branch = (row(5) * grad_upper).astype(bf16)
    g_branch_two_ref[...] = grad_branch
    g_bias_ref[2:3, :] += jnp.sum(grad_branch.astype(f32), axis=0, keepdims=True)
    hidden[...] = grad_upper

    def narrow(index, carry):
        span = pl.ds(pl.multiple_of(index * wide, wide), wide)
        grad_act = dot_t(g_branch_two_ref[...], shrink_ref[span, :])
        grad_pre = (grad_act * slope[:, span]).astype(bf16)
        g_pre_ref[:, span] = grad_pre
        g_bias_ref[bias_wide(g_bias_ref, 4, index)] += jnp.sum(grad_pre.astype(f32), axis=0, keepdims=True)
        return carry

    lax.fori_loop(0, MLP_WIDTH // wide, narrow, 0)

    grad = dot_t(g_pre_ref[...], expand_ref[...])
    normal = normal_two[...]
    shift_two = jnp.sum(grad, axis=0, keepdims=True)
    scale_mod_two = jnp.sum(grad * normal, axis=0, keepdims=True)
    grad_middle = hidden[...] + center_back((1.0 + row(4)) * grad, normal, scale_two)
    gate_one = jnp.sum(branch[...] * grad_middle, axis=0, keepdims=True)
    grad_branch = (row(2) * grad_middle).astype(bf16)
    g_branch_ref[...] = grad_branch
    g_bias_ref[1:2, :] += jnp.sum(grad_branch.astype(f32), axis=0, keepdims=True)
    hidden[...] = grad_middle
    g_mixed[...] = dot_t(grad_branch, output_ref[...]).astype(bf16)

    def attend_back(pair, carry):
        query_span, key_span, value_span = spans_of(pair)
        query = triple[:, query_span]
        keys = triple[:, key_span]
        values = triple[:, value_span]
        grad_mixed = g_mixed[:, query_span]
        results = []
        for side in range(2):
            mask = first_half if side == 0 else jnp.logical_not(first_half)
            weights = probs[2 * pair + side]
            grad_weights = dot_t(jnp.where(mask, grad_mixed, zero), values)
            grad_values = dot_s(weights.astype(bf16), grad_mixed)
            grad_scores = weights * (
                grad_weights - jnp.sum(weights * grad_weights, axis=-1, keepdims=True)
            )
            grad_scores = grad_scores.astype(bf16)
            grad_query = dot(grad_scores, keys)
            grad_keys = dot_s(grad_scores, query)
            results.append((grad_query, grad_keys, grad_values))
        for part, span in enumerate((query_span, key_span, value_span)):
            merged = jnp.where(first_half, results[0][part], results[1][part])
            if part < 2:
                merged = merged * rate
            g_triple_ref[:, span] = merged.astype(bf16)
        return carry

    lax.fori_loop(0, HEADS // 2, attend_back, 0)

    grad = dot_t(g_triple_ref[...], attend_ref[...])
    normal = normal_one[...]
    shift_one = jnp.sum(grad, axis=0, keepdims=True)
    scale_mod_one = jnp.sum(grad * normal, axis=0, keepdims=True)
    grad_start = hidden[...] + center_back((1.0 + row(1)) * grad, normal, scale_one)
    grad_start = grad_start.astype(bf16)
    g_patch_ref[...] += dot_s(blended, grad_start)
    g_bias_ref[0:1, :] += jnp.sum(grad_start.astype(f32), axis=0, keepdims=True)
    for index, value in enumerate(
        (shift_one, scale_mod_one, gate_one, shift_two, scale_mod_two, gate_two, shift_f, scale_f)
    ):
        g_mods_ref[0, index : index + 1, :] = value


def layer(numbers, latent, noisy, mods, patch_w, final_w, tail, weights):
    images = latent.shape[0]
    tokens = images * SEQUENCE
    once = pl.Buffered(1)

    def whole(array):
        return pl.BlockSpec(
            array.shape, lambda i: (0,) * len(array.shape), pipeline_mode=once
        )

    def fixed(shape, dtype=f32):
        return pl.BlockSpec(shape, lambda i: (0,) * len(shape)), jax.ShapeDtypeStruct(shape, dtype)

    def per_image(width):
        return (
            pl.BlockSpec((SEQUENCE, width), lambda i: (i, 0)),
            jax.ShapeDtypeStruct((tokens, width), bf16),
        )

    outs = [
        per_image(WIDTH),
        per_image(WIDTH),
        per_image(WIDTH),
        per_image(MLP_WIDTH),
        per_image(WIDTH),
        per_image(MLP_WIDTH),
        per_image(WIDTH),
        per_image(3 * WIDTH),
        (
            pl.BlockSpec((1, 8, WIDTH), lambda i: (i, 0, 0)),
            jax.ShapeDtypeStruct((images, 8, WIDTH), f32),
        ),
        fixed((PATCH, WIDTH)),
        fixed((WIDTH, PATCH)),
        fixed((8, WIDTH)),
    ]
    place = positions(SEQUENCE, WIDTH)
    fixed_args = (place, patch_w, final_w, tail) + tuple(weights)
    flops = 2 * 2 * 7078 * 1000 * tokens
    return pl.pallas_call(
        layer_kernel,
        grid=(images,),
        in_specs=[
            pl.BlockSpec(memory_space=pltpu.SMEM),
            pl.BlockSpec((1, SEQUENCE, PATCH), lambda i: (i, 0, 0)),
            pl.BlockSpec((1, SEQUENCE, PATCH), lambda i: (i, 0, 0)),
            pl.BlockSpec((1, 8, WIDTH), lambda i: (i, 0, 0)),
        ]
        + [whole(array) for array in fixed_args],
        out_specs=[spec for spec, _ in outs],
        out_shape=[shape for _, shape in outs],
        scratch_shapes=[
            pltpu.VMEM((SEQUENCE, 3 * WIDTH), bf16),
            pltpu.VMEM((HEADS, SEQUENCE, SEQUENCE), f32),
            pltpu.VMEM((SEQUENCE, MLP_WIDTH), f32),
            pltpu.VMEM((SEQUENCE, WIDTH), f32),
            pltpu.VMEM((SEQUENCE, WIDTH), f32),
            pltpu.VMEM((SEQUENCE, WIDTH), f32),
            pltpu.VMEM((SEQUENCE, WIDTH), f32),
            pltpu.VMEM((SEQUENCE, WIDTH), bf16),
        ],
        compiler_params=pltpu.CompilerParams(vmem_limit_bytes=56 * 1024 * 1024),
        cost_estimate=pl.CostEstimate(
            flops=flops, bytes_accessed=60 * 10**6, transcendentals=0
        ),
        name="layer",
    )(numbers, latent, noisy, mods, *fixed_args)


def local(
    n_wide,
    n_narrow,
    latents,
    noise_field,
    labels,
    label_drop,
    time_steps,
    loss_weights,
    attend_weight,
    attend_first,
    attend_second,
    attend_left,
    attend_right,
    output_weight,
    output_first,
    output_second,
    output_left,
    output_right,
    expand_weight,
    expand_first,
    expand_second,
    expand_left,
    expand_right,
    shrink_weight,
    shrink_first,
    shrink_second,
    shrink_left,
    shrink_right,
    adaptive_weight,
    adaptive_first,
    adaptive_second,
    adaptive_left,
    adaptive_right,
    shared_weight,
    shared_first,
    shared_second,
):
    column = lax.axis_index("narrow")
    images = labels.shape[0] * labels.shape[1]

    moment = (time_steps.reshape(images).astype(f32) + 0.5) / TIMESTEPS
    chosen = jnp.where(label_drop == 1, CLASSES - 1, labels).reshape(images, 1).astype(f32)
    weights_here = loss_weights.reshape(images)
    info = jnp.concatenate(
        [rounded(frequencies(moment, FREQS)).astype(f32), chosen, weights_here[:, None]], axis=1
    )
    info = jnp.pad(info, ((0, 8 - images), (0, SHEET - info.shape[1])))[None]

    shard = shared_weight.shape[0]
    rows = shard_rows(shard)
    row_start = column * shard // (WIDTH * ALIGN) * ALIGN
    offset = column * shard - row_start * WIDTH
    margin = (ALIGN + 1) * WIDTH
    own = jnp.concatenate(
        [jnp.zeros((margin,), f32), shared_weight, jnp.zeros((rows * WIDTH - shard,), f32)]
    )
    own = lax.dynamic_slice(own, (margin - offset,), (rows * WIDTH,)).reshape(rows, WIDTH)

    *full, flat, sheet, time_pre, condition, own_act, adaptive_low, mods, total = gather_all(
        n_wide,
        n_narrow,
        images,
        shard,
        (own, attend_weight, output_weight, expand_weight, shrink_weight),
        adaptive_weight,
        info,
    )
    weight_sum = total[0, 0]

    shape = (images,) + latents.shape[2:]
    entries = SEQUENCE * PATCH
    numbers = jnp.stack(
        [moment, 2.0 * weights_here / (entries * weight_sum), weights_here / entries]
    )
    (
        normed,
        mixed,
        normed_two,
        act,
        g_branch_two,
        g_pre,
        g_branch,
        g_triple,
        g_mods,
        g_patch,
        g_final,
        g_bias,
    ) = layer(
        numbers,
        latents.reshape(shape),
        noise_field.reshape(shape),
        mods,
        flat[ROW_PATCH:ROW_TIME_ONE],
        flat[ROW_FINAL:ROW_BIAS].reshape(WIDTH, PATCH),
        flat[ROW_TAIL : ROW_TAIL + TAIL].astype(f32),
        full,
    )

    joined, grad_adaptive, window, totals, clip = reduce_all(
        n_wide,
        n_narrow,
        images,
        shard,
        (
            weight_blocks(n_narrow, normed, g_triple),
            weight_blocks(n_narrow, mixed, g_branch),
            weight_blocks(n_narrow, normed_two, g_pre),
            weight_blocks(n_narrow, act, g_branch_two),
        ),
        (
            g_mods.reshape(images * 8, WIDTH),
            g_patch,
            g_final.reshape(PATCH, WIDTH),
            g_bias,
            adaptive_low,
            sheet,
            time_pre,
            condition,
            own_act,
            flat[ROW_TIME_TWO:ROW_TABLE],
        ),
    )
    loss_sum = totals[3, PATCH]
    clip_norm = clip[0, 0]
    factor = clip[1, 0]
    grad_shared = lax.dynamic_slice(window.reshape(-1), (offset,), (shard,))

    states = (
        (attend_weight, attend_first, attend_second, attend_left, attend_right),
        (output_weight, output_first, output_second, output_left, output_right),
        (expand_weight, expand_first, expand_second, expand_left, expand_right),
        (shrink_weight, shrink_first, shrink_second, shrink_left, shrink_right),
        (adaptive_weight, adaptive_first, adaptive_second, adaptive_left, adaptive_right),
    )
    tiles = (0, 3, 4, 8)
    results = []
    for number in range(5):
        weight, first, second, left, right = states[number]
        grad, base = (grad_adaptive, None) if number == 4 else (joined, tiles[number])
        results += rotated_update(
            weight, first, second, grad, base, left, right, factor, WIDTH // n_narrow
        )
    fresh = plain_update(shared_weight, shared_first, shared_second, grad_shared * factor)
    results += [fresh[0], fresh[1], fresh[2], fresh[0].astype(jnp.bfloat16)]
    return tuple(results) + (loss_sum, weight_sum, clip_norm)


def solution(mesh):
    data = P(None, ("wide", "narrow"))
    state = (P("narrow", None),) * 3 + (P("narrow", None, None), P())
    return jax.shard_map(
        partial(local, mesh.shape["wide"], mesh.shape["narrow"]),
        mesh=mesh,
        in_specs=(P(None, ("wide", "narrow"), None, None),) * 2
        + (data,) * 4
        + state * 5
        + (P("narrow"),) * 3,
        out_specs=(P("narrow", None),) * 20 + (P("narrow"),) * 4 + (P(),) * 3,
        check_vma=False,
    )
```

time: 2320 us -> 568 us (0.24)
  waiting for transfers between devices: 1070 us -> 0 us
  Pallas kernels: 0 us -> 504 us
  local copies, waits for them, and re-layouts: 538 us -> 45.4 us
  matrix products: 420 us -> 0 us
  other arithmetic: 180 us -> 9.37 us
  blocking collectives: 70.1 us -> 0 us
    reduce_scatter x10 -> x0, waiting for transfers between devices: 526 us -> none  [the longest x2 193 us: narrow_sums(): lax.psum_scatter(grads[4].astype(jnp.bfloat16), 'narrow', scatter_dimensi...]
    pallas_call x0 -> x12, Pallas kernels: none -> 504 us  [the longest x1 153 us: reduce_all(): pl.pallas_call(partial(reduce_kernel, n_wide, n_narrow, images, shard), i...]
    dot_general x84 -> x0, matrix products: 420 us -> none  [the longest x5 64.2 us: unrotate(): turned = jnp.einsum('iajd,jcd->iajc', turned, right, precision=highest)]
    psum x1 -> x0, waiting for transfers between devices: 250 us -> none  [local(): lax.psum((grad_totals[0], grad_totals[1], grad_totals[2], grad_totals[3],...]
    reshape x41 -> x4, local copies, waits for them, and re-layouts: 213 us -> 4.75 us  [the longest x1 1.57 us: local(): grad_shared = lax.dynamic_slice(window.reshape(-1), (offset,), (shard,))]
    all_gather x5 -> x0, waiting for transfers between devices: 187 us -> none  [the longest x1 75 us: local(): lax.all_gather(rounded(adaptive_weight), 'narrow', axis=0, tiled=True)]
    unnamed x556 -> x75, local copies, waits for them, and re-layouts: 134 us -> 20.3 us
    transpose x10 -> x0, local copies, waits for them, and re-layouts: 105 us -> none  [the longest x5 52.6 us: rotate(): turned = jnp.einsum('ibjc,jcd->ibjd', turned, right, precision=highest)]
  transfers between devices with their start and end apart: 18 -> 0, of which waited for: 15 -> 0; matrix products, arithmetic and copies ran while one was open for 14% -> 0% of each run, Pallas kernels for 0% -> 0%
where the time goes in v1:
time: 568 us; the launch traced here: 563 us
  Pallas kernels  504 us (89%)
  local copies, waits for them, and re-layouts  45.4 us (8%)
  other arithmetic  9.37 us (2%)
    pallas_call x1, Pallas kernels, reduce_all(): pl.pallas_call(partial(reduce_kernel, n_wide, n_narrow, images, shard), i...  153 us
    pallas_call x1, Pallas kernels, layer(): pl.pallas_call(layer_kernel, grid=(images,), in_specs=[pl.BlockSpec(memor...  127 us
    pallas_call x1, Pallas kernels, gather_all(): pl.pallas_call(partial(gather_kernel, n_wide, n_narrow, images, shard), i...  121 us
    pallas_call x5, Pallas kernels, rotated_update(): pl.pallas_call(adam_kernel, grid=(rows // tile_rows, cols // tile_cols),...  77.8 us
    pallas_call x4, Pallas kernels, weight_blocks(): pl.pallas_call(weight_kernel, grid=(grid,), in_specs=[left, right], out_s...  25.7 us
    unnamed x75, local copies, waits for them, and re-layouts  20.3 us
    concatenate x1, local copies, waits for them, and re-layouts, local(): jnp.concatenate([jnp.zeros((margin,), f32), shared_weight, jnp.zeros((row...  13.1 us

profile of v1, /device:TPU:0, one launch (start us, length us, event | category | flops | bytes accessed | tf_op | source)
XLA Modules:
  0.0 562.6 jit_solution(6961061524112668746)
XLA Ops:
  0.7 13.1 %concatenate.10 = f32[430848]{0:T(1024)S(1)} concatenate(f32[13056]{0:T(1024)S(1)} %broadcast_in_dim.15, f32[398212]{0:T(1024)} %param.66, f32[19580]{0:T(1024)S(1)} %broadcast_in_dim.16), dimensions={0} | concatenate | bytes 3446784 | tf_op jit(solution)/shard_map/concatenate | solution.py:1589
  14.4 1.5 reshape.162.refs_0_
  17.0 120.9 %gather_weights.1 = (bf16[768,2304]{1,0:T(8,128)(2,1)}, bf16[768,768]{1,0:T(8,128)(2,1)}, bf16[768,3072]{1,0:T(8,128)(2,1)}, bf16[3072,768]{1,0:T(8,128)(2,1)}, ...) custom-call(f32[544,768]{1,0:T(8,128)} %reshape.162.refs_0_, ...), custom_call_target="tpu_custom_call" | custom-call | tf_op jit(solution)/shard_map/gather_weights/pallas_call | solution.py:606
  139.3 1.0 copy.71
  141.3 1.4 fusion.7
  143.6 1.4 slice_convert_fusion.tail_ref
  145.0 126.9 %layer.1 = (bf16[1024,768]{1,0:T(8,128)(2,1)}, bf16[1024,768]{1,0:T(8,128)(2,1)}, bf16[1024,768]{1,0:T(8,128)(2,1)}, bf16[1024,3072]{1,0:T(8,128)(2,1)}, bf16[10...) custom-call(f32[3,4]{1,0:T(4,128)} %pad_maximum_fusion.numbers, ...), custom_call_target="tpu_custom_call" | custom-call | flops 28991488000 | bytes 60000000 | tf_op jit(solution)/shard_map/layer/pallas_call | solution.py:1505
  271.9 1.4 copy-done.13
  273.3 6.1 %weight_gradient.4.refs_0_ = bf16[4,576,768]{2,1,0:T(8,128)(2,1)S(1)} custom-call(bf16[1024,768]{1,0:T(8,128)(2,1)S(1)} %copy-done.13, bf16[1024,2304]{1,0:T(8,128)(2,1)} %get-tuple-element.84.right_ref), custom_call_target="tpu_custom_call" | custom-call | tf_op jit(solution)/shard_map/weight_gradient/pallas_call | solution.py:1219
  279.4 1.8 copy-done.1
  281.2 1.4 weight_gradient.5.refs_1_
  282.7 9.1 %weight_gradient.6.refs_2_ = bf16[4,768,768]{2,1,0:T(8,128)(2,1)} custom-call(bf16[1024,768]{1,0:T(8,128)(2,1)S(1)} %copy-done.12, bf16[1024,3072]{1,0:T(8,128)(2,1)} %get-tuple-element.88.right_ref), custom_call_target="tpu_custom_call" | custom-call | tf_op jit(solution)/shard_map/weight_gradient/pallas_call | solution.py:1219
  291.8 9.1 %weight_gradient.7 = bf16[3072,768]{1,0:T(8,128)(2,1)} custom-call(bf16[1024,3072]{1,0:T(8,128)(2,1)} %get-tuple-element.89.left_ref, bf16[1024,768]{1,0:T(8,128)(2,1)S(1)} %copy-done.11), custom_call_target="tpu_custom_call" | custom-call | tf_op jit(solution)/shard_map/weight_gradient/pallas_call | solution.py:1219
  301.7 2.4 slice.24.refs_13_
  304.1 153.0 %reduce_gradients.1 = (bf16[12,2,96,768]{3,2,1,0:T(8,128)(2,1)}, bf16[192,6144]{1,0:T(8,128)(2,1)}, f32[2112,768]{1,0:T(8,128)}, f32[544,768]{1,0:T(8,128)}, f32[8,768]{1,0:T(8,128)}, /*index=5*/f32[8,128]{1,0:T(8,128)}) custom-call(bf16[4,576,768]{2,1,0:T(8,128)(2,1)} %copy-done.1, bf16[4,192,768]{2,1,0:T(8,128)(2,1)} %copy-done.6, ...), custom_call_target="tpu_custom_call" | custom-call | flops 100000000 | bytes 300000000 | tf_op jit(solution)/shard_map/reduce_gradients/pallas_call | solution.py:1145
  457.1 1.3 fusion.8
  458.4 1.9 copy.73.right_ref
  460.2 1.5 copy-done.4
  461.7 1.3 copy-done.5
  463.0 1.5 copy-done.10
  465.4 13.3 %rotated_adam.5 = (f32[192,2304]{1,0:T(8,128)}, f32[192,2304]{1,0:T(8,128)}, f32[192,2304]{1,0:T(8,128)}, bf16[192,2304]{1,0:T(8,128)(2,1)}) custom-call(f32[1]{0:T(128)} %bitcast.6.factor_ref, f32[192,2304]{1,0:T(8,128)S(1)} %copy-done.4, f32[192,2304]{1,0:T(8,128)S(1)} %copy-done.10, f32[192,2304]{1,0:T(8,128)} %second_ref.5, bf16[2304,768]{1,0:T(8,128)(2,1)} %bitcast.12, ...), custom_call_target="tpu_custom_call" | custom-call | tf_op jit(solution)/shard_map/rotated_adam/pallas_call | solution.py:206
  478.8 4.8 rotated_adam.6
  483.6 1.4 copy.74.right_ref
  485.0 1.7 copy-done.2
  486.6 16.3 %rotated_adam.7 = (f32[192,3072]{1,0:T(8,128)}, f32[192,3072]{1,0:T(8,128)}, f32[192,3072]{1,0:T(8,128)}, bf16[192,3072]{1,0:T(8,128)(2,1)}) custom-call(f32[1]{0:T(128)} %bitcast.6.factor_ref, f32[192,3072]{1,0:T(8,128)S(1)} %copy-done.2, f32[192,3072]{1,0:T(8,128)} %first_ref.7, f32[192,3072]{1,0:T(8,128)} %second_ref.7, bf16[2304,768]{1,0:T(8,128)(2,1)} %bitcast.13, ...), custom_call_target="tpu_custom_call" | custom-call | tf_op jit(solution)/shard_map/rotated_adam/pallas_call | solution.py:206
  503.0 15.3 %rotated_adam.8 = (f32[768,768]{1,0:T(8,128)}, f32[768,768]{1,0:T(8,128)}, f32[768,768]{1,0:T(8,128)}, bf16[768,768]{1,0:T(8,128)(2,1)}) custom-call(f32[1]{0:T(128)} %bitcast.6.factor_ref, f32[768,768]{1,0:T(8,128)S(1)} %copy-done.3, f32[768,768]{1,0:T(8,128)S(1)} %copy-done.8, f32[768,768]{1,0:T(8,128)} %second_ref.8, bf16[2304,768]{1,0:T(8,128)(2,1)} %bitcast.14, ...), custom_call_target="tpu_custom_call" | custom-call | tf_op jit(solution)/shard_map/rotated_adam/pallas_call | solution.py:206
  518.2 3.0 copy.75.right_ref
  521.2 1.7 copy-done.9
  522.9 28.1 %rotated_adam.9 = (f32[192,6144]{1,0:T(8,128)}, f32[192,6144]{1,0:T(8,128)}, f32[192,6144]{1,0:T(8,128)}, bf16[192,6144]{1,0:T(8,128)(2,1)}) custom-call(f32[1]{0:T(128)} %bitcast.6.factor_ref, f32[192,6144]{1,0:T(8,128)} %weight_ref.9, f32[192,6144]{1,0:T(8,128)} %first_ref.9, f32[192,6144]{1,0:T(8,128)} %second_ref.9, bf16[192,6144]{1,0:T(8,128)(2,1)S(1)} %copy-done.9, ...), custom_call_target="tpu_custom_call" | custom-call | tf_op jit(solution)/shard_map/rotated_adam/pallas_call | solution.py:206
  551.0 1.6 reshape.170
  552.9 6.5 %fusion.5 = (bf16[398212]{0:T(1024)(128)(2,1)}, f32[398212]{0:T(1024)}, f32[398212]{0:T(1024)}, f32[398212]{0:T(1024)}) fusion(f32[398212]{0:T(1024)S(1)} %copy-done.25, f32[]{:T(128)} %bitcast.8, f32[417792]{0:T(1024)S(1)} %reshape.170, s32[]{:T(128)S(6)} %select_n.18, f32[398212]{0:T(1024)} %param.67, f32[398212]{0:T(1024)} %param.68), kind=kLoop, calls=%fused_computation.24 | loop fusion | flops 6769604 | bytes 11946368 | tf_op jit(solution)/shard_map/convert_element_type | solution.py:1679
  559.4 1.3 slice.26
  (83 shorter events, 6.5 us)
Async XLA Ops:
  14.3 1.5 copy-start.31
  14.4 1.6 copy-start.32
  14.4 1.6 copy-start.33
  14.4 1.7 copy-start.34
  17.0 122.3 %copy-start.29 = (f32[2,2,256,16]{2,3,1,0:T(8,128)S(1)}, f32[2,2,256,16]{2,3,1,0:T(8,128)}, u32[]{:S(2)}) copy-start(f32[2,2,256,16]{2,3,1,0:T(8,128)} %param.35) | copy-start | bytes 196612
  17.0 123.3 %copy-start.30 = (f32[2,2,256,16]{2,3,1,0:T(8,128)S(1)}, f32[2,2,256,16]{2,3,1,0:T(8,128)}, u32[]{:S(2)}) copy-start(f32[2,2,256,16]{2,3,1,0:T(8,128)} %param.36) | copy-start | bytes 196612
  271.9 1.4 copy-start.13
  273.3 7.9 %copy-start.14 = (bf16[1024,768]{1,0:T(8,128)(2,1)S(1)}, bf16[1024,768]{1,0:T(8,128)(2,1)}, u32[]{:S(2)}) copy-start(bf16[1024,768]{1,0:T(8,128)(2,1)} %get-tuple-element.85.left_ref) | copy-start | bytes 4718596
  273.3 7.9 %copy-start.15 = (bf16[1024,768]{1,0:T(8,128)(2,1)S(1)}, bf16[1024,768]{1,0:T(8,128)(2,1)}, u32[]{:S(2)}) copy-start(bf16[1024,768]{1,0:T(8,128)(2,1)} %get-tuple-element.86.right_ref) | copy-start | bytes 4718596
  279.4 1.8 copy-start.1
  281.2 1.5 copy-start.12
  282.7 9.2 %copy-start.6 = (bf16[4,192,768]{2,1,0:T(8,128)(2,1)}, bf16[4,192,768]{2,1,0:T(8,128)(2,1)S(1)}, u32[]{:S(2)}) copy-start(bf16[4,192,768]{2,1,0:T(8,128)(2,1)S(1)} %weight_gradient.5.refs_1_) | copy-start | bytes 3538948
  282.7 9.1 %copy-start.11 = (bf16[1024,768]{1,0:T(8,128)(2,1)S(1)}, bf16[1024,768]{1,0:T(8,128)(2,1)}, u32[]{:S(2)}) copy-start(bf16[1024,768]{1,0:T(8,128)(2,1)} %get-tuple-element.90.right_ref) | copy-start | bytes 4718596
  291.8 9.1 %copy-start.28 = (f32[768,16]{1,0:T(8,128)S(1)}, f32[768,16]{1,0:T(8,128)}, u32[]{:S(2)}) copy-start(f32[768,16]{1,0:T(8,128)} %get-tuple-element.93) | copy-start | bytes 147460
  304.1 154.3 %copy-start.26 = (f32[72,32,32]{0,2,1:T(8,128)S(1)}, f32[72,32,32]{0,2,1:T(8,128)}, u32[]{:S(2)}) copy-start(f32[72,32,32]{0,2,1:T(8,128)} %param.45) | copy-start | bytes 884740
  460.2 1.5 copy-start.4
  463.0 1.5 copy-start.10
  465.4 13.4 %copy-start = (bf16[12,2,96,768]{3,2,1,0:T(8,128)(2,1)S(1)}, bf16[12,2,96,768]{3,2,1,0:T(8,128)(2,1)}, u32[]{:S(2)}) copy-start(bf16[12,2,96,768]{3,2,1,0:T(8,128)(2,1)} %get-tuple-element.101) | copy-start | bytes 10616836
  465.4 13.4 %copy-start.7 = (f32[192,768]{1,0:T(8,128)S(1)}, f32[192,768]{1,0:T(8,128)}, u32[]{:S(2)}) copy-start(f32[192,768]{1,0:T(8,128)} %weight_ref.6) | copy-start | bytes 1769476
  465.4 13.4 %copy-start.16 = (f32[192,768]{1,0:T(8,128)S(1)}, f32[192,768]{1,0:T(8,128)}, u32[]{:S(2)}) copy-start(f32[192,768]{1,0:T(8,128)} %first_ref.6) | copy-start | bytes 1769476
  465.4 13.4 %copy-start.17 = (f32[192,768]{1,0:T(8,128)S(1)}, f32[192,768]{1,0:T(8,128)}, u32[]{:S(2)}) copy-start(f32[192,768]{1,0:T(8,128)} %second_ref.6) | copy-start | bytes 1769476
  465.4 13.4 %copy-start.20 = (f32[24,32,32]{2,1,0:T(8,128)S(1)}, f32[24,32,32]{2,1,0:T(8,128)}, u32[]{:S(2)}) copy-start(f32[24,32,32]{2,1,0:T(8,128)} %right_ref.5) | copy-start | bytes 294916
  465.4 13.4 %copy-start.24 = (f32[6,32,32]{2,1,0:T(8,128)S(1)}, f32[6,32,32]{2,1,0:T(8,128)}, u32[]{:S(2)}) copy-start(f32[6,32,32]{2,1,0:T(8,128)} %left_ref.6) | copy-start | bytes 73732
  478.8 4.8 copy-start.27
  484.9 1.7 copy-start.2
  486.6 16.3 %copy-start.3 = (f32[768,768]{1,0:T(8,128)S(1)}, f32[768,768]{1,0:T(8,128)}, u32[]{:S(2)}) copy-start(f32[768,768]{1,0:T(8,128)} %weight_ref.8) | copy-start | bytes 7077892
  486.6 16.3 %copy-start.8 = (f32[768,768]{1,0:T(8,128)S(1)}, f32[768,768]{1,0:T(8,128)}, u32[]{:S(2)}) copy-start(f32[768,768]{1,0:T(8,128)} %first_ref.8) | copy-start | bytes 7077892
  486.6 16.3 %copy-start.18 = (f32[24,32,32]{2,1,0:T(8,128)S(1)}, f32[24,32,32]{2,1,0:T(8,128)}, u32[]{:S(2)}) copy-start(f32[24,32,32]{2,1,0:T(8,128)} %left_ref.8) | copy-start | bytes 294916
  486.6 16.3 %copy-start.19 = (f32[24,32,32]{2,1,0:T(8,128)S(1)}, f32[24,32,32]{2,1,0:T(8,128)}, u32[]{:S(2)}) copy-start(f32[24,32,32]{2,1,0:T(8,128)} %right_ref.6) | copy-start | bytes 294916
  518.2 3.0 copy-start.23
  521.2 1.7 copy-start.9
  551.0 1.9 copy-start.25
  (3 other events, 3.6 us)

commit v2 on v1

--- a/solution.py
+++ b/solution.py
@@ -68,10 +68,8 @@
 
 
 def adam_direction(first, second):
-    return (
-        first
-        / (1.0 - beta_one**STEP_COUNT)
-        / (jnp.sqrt(second / (1.0 - beta_two**STEP_COUNT)) + epsilon_adam)
+    return (first * (1.0 / (1.0 - beta_one**STEP_COUNT))) / (
+        jnp.sqrt(second * (1.0 / (1.0 - beta_two**STEP_COUNT))) + epsilon_adam
     )
 
 
@@ -111,19 +109,37 @@
     return high, (value - high.astype(f32)).astype(bf16)
 
 
-def spread_blocks(blocks):
-    count = blocks.shape[0]
-    size = count * BLOCK
-    high, low = halves(blocks.reshape(size, BLOCK))
+def spread_left(blocks):
+    size = blocks.shape[0]
     place = lax.broadcasted_iota(jnp.int32, (BLOCK, size), 0)
     column = lax.broadcasted_iota(jnp.int32, (BLOCK, size), 1)
     repeat = (place == column % BLOCK).astype(bf16)
     row_block = lax.broadcasted_iota(jnp.int32, (size, size), 0) // BLOCK
     col_block = lax.broadcasted_iota(jnp.int32, (size, size), 1) // BLOCK
+    return tuple(
+        jnp.where(
+            row_block == col_block, jnp.dot(part, repeat, preferred_element_type=f32), 0.0
+        ).astype(bf16)
+        for part in halves(blocks)
+    )
+
+
+def spread_right(first, second):
+    size = 4 * BLOCK
+    row_block = lax.broadcasted_iota(jnp.int32, (size, size), 0) // BLOCK
+    col_block = lax.broadcasted_iota(jnp.int32, (size, size), 1) // BLOCK
     inside = row_block == col_block
-    high = jnp.dot(high, repeat, preferred_element_type=f32)
-    low = jnp.dot(low, repeat, preferred_element_type=f32)
-    return jnp.where(inside, high, 0.0), jnp.where(inside, low, 0.0)
+    corners = [
+        jnp.where(inside, jnp.concatenate([row] * 4, axis=0), 0.0) for row in (first, second)
+    ]
+    empty = jnp.zeros((size, size), f32)
+    return jnp.concatenate(
+        [
+            jnp.concatenate([corners[0], empty], axis=1),
+            jnp.concatenate([empty, corners[1]], axis=1),
+        ],
+        axis=0,
+    )
 
 
 def dot(left, right):
@@ -134,94 +150,137 @@
     return lax.dot_general(left, right, (((1,), (1,)), ((), ())), preferred_element_type=f32)
 
 
-def adam_kernel(
-    factor_ref,
-    weight_ref,
-    first_ref,
-    second_ref,
-    grad_ref,
-    left_ref,
-    right_ref,
-    new_ref,
-    mean_ref,
-    square_ref,
-    copy_ref,
-    left_high,
-    turn_high,
-    turn_low,
-):
-    @pl.when(pl.program_id(1) == 0)
-    def _():
-        high, low = spread_blocks(left_ref[...])
-        left_high[...] = high.astype(bf16)
-        turn_high[...] = high.T.astype(bf16)
-        turn_low[...] = low.T.astype(bf16)
-
-    factor = factor_ref[0]
-    chunk = 256
-    for start in range(0, weight_ref.shape[1], chunk):
-        span = pl.ds(start, chunk)
-        right_high, right_low = spread_blocks(
-            right_ref[start // BLOCK : (start + chunk) // BLOCK]
-        )
-        right_high = right_high.astype(bf16)
-        right_low = right_low.astype(bf16)
-        if grad_ref.dtype == bf16:
-            grad = grad_ref[:, span]
-            turned = dot(grad, right_high) + dot(grad, right_low)
-        else:
-            grad_high, grad_low = halves(grad_ref[:, span])
-            turned = dot(grad_high, right_high) + (
-                dot(grad_high, right_low) + dot(grad_low, right_high)
-            )
-        high, low = halves(turned)
-        turned = dot(turn_high[...], high) + (
-            dot(turn_low[...], high) + dot(turn_high[...], low)
-        )
-        turned = turned * factor
-        first = beta_one * first_ref[:, span] + (1.0 - beta_one) * turned
-        second = beta_two * second_ref[:, span] + (1.0 - beta_two) * turned * turned
-        mean_ref[:, span] = first
-        square_ref[:, span] = second
-        step = adam_direction(first, second)
-        step = dot_t(step.astype(bf16), right_high)
-        step = dot(left_high[...], step.astype(bf16))
-        weight = weight_ref[:, span]
-        weight = weight - learn_rate * (step + decay_rate * weight)
-        new_ref[:, span] = weight
-        copy_ref[:, span] = weight.astype(bf16)
-
-
-def rotated_update(weight, first, second, grad, base, left, right, factor, tile_rows):
-    rows, cols = weight.shape
-    tile_cols = WIDTH
-    tile = pl.BlockSpec((tile_rows, tile_cols), lambda i, j: (i, j))
-    if base is None:
-        grad_tile = tile
-    else:
-        across = cols // tile_cols
-        grad_tile = pl.BlockSpec(
-            (tile_rows, tile_cols), lambda i, j: (base + i * across + j, 0)
-        )
+STRIP = 256
+TILES = ((3, 1), (1, 1), (4, 1), (1, 4), (8, 1))
+
+
+def tile_places():
+    places = []
+    for matrix, (across, down) in enumerate(TILES):
+        for number in range(across * down):
+            places.append((matrix, number // across, number % across))
+    return places
+
+
+def left_number(tile):
+    return (tile + 9) // 12 + (tile + 8) // 12 + (tile + 4) // 12 * (tile - 7)
+
+
+def adam_kernel(count, *refs):
+    factor_ref, turned, lefts, rights = refs[:4]
+    states = [refs[4 + 3 * matrix : 7 + 3 * matrix] for matrix in range(5)]
+    outs = [refs[19 + 4 * matrix : 23 + 4 * matrix] for matrix in range(5)]
+    taken, given, low, take_sem, give_sem = refs[39:]
+    rows = taken.shape[2]
+    places = tile_places()
+    factor = factor_ref[1, 0]
+
+    def window(number):
+        _, down, across = places[number]
+        return (pl.ds(down * rows, rows), pl.ds(across * WIDTH, WIDTH))
+
+    def takes(number):
+        slot = number % 3
+        arrays = [ref.at[window(number)] for ref in states[places[number][0]]]
+        arrays.append(turned.at[number])
+        return [
+            pltpu.make_async_copy(array, taken.at[slot, part], take_sem.at[slot, part])
+            for part, array in enumerate(arrays)
+        ]
+
+    def gives(number):
+        slot = number % 2
+        arrays = [ref.at[window(number)] for ref in outs[places[number][0]]]
+        sources = [given.at[slot, part] for part in range(3)] + [low.at[slot]]
+        return [
+            pltpu.make_async_copy(source, array, give_sem.at[slot, part])
+            for part, (source, array) in enumerate(zip(sources, arrays))
+        ]
+
+    def given_out(slot):
+        for part in range(4):
+            buffer = low.at[slot] if part == 3 else given.at[slot, part]
+            pltpu.make_async_copy(buffer, buffer, give_sem.at[slot, part]).wait()
+
+    for number in range(2):
+        for copy in takes(number):
+            copy.start()
+
+    def body(tile, carry):
+        for number in range(2, count):
+
+            @pl.when(tile + 2 == number)
+            def _(number=number):
+                for copy in takes(number):
+                    copy.start()
+
+        slot = tile % 3
+        out = tile % 2
+        for part in range(4):
+            buffer = taken.at[slot, part]
+            pltpu.make_async_copy(buffer, buffer, take_sem.at[slot, part]).wait()
+
+        @pl.when(tile >= 2)
+        def _():
+            given_out(out)
+
+        stack = jnp.where(tile < 12, left_number(jnp.minimum(tile, 11)), 7)
+        left = spread_left(lefts[stack])[0]
+        for start in range(0, WIDTH, STRIP):
+            span = slice(start, start + STRIP)
+            group = tile * (WIDTH // BLOCK // 4) + start // BLOCK // 4
+            right = spread_right(rights[group], rights[group + 1]).astype(bf16)
+            grad = taken[slot, 3, :, span] * factor
+            first = beta_one * taken[slot, 1, :, span] + (1.0 - beta_one) * grad
+            second = beta_two * taken[slot, 2, :, span] + (1.0 - beta_two) * grad * grad
+            given[out, 1, :, span] = first
+            given[out, 2, :, span] = second
+            step = adam_direction(first, second)
+            step = dot_t(step.astype(bf16), right)
+            step = dot(left, step.astype(bf16))
+            weight = taken[slot, 0, :, span]
+            weight = weight - learn_rate * (step + decay_rate * weight)
+            given[out, 0, :, span] = weight
+            low[out, :, span] = weight.astype(bf16)
+        for number in range(count):
+
+            @pl.when(tile == number)
+            def _(number=number):
+                for copy in gives(number):
+                    copy.start()
+
+        return carry
+
+    lax.fori_loop(0, count, body, 0)
+    for slot in range(2):
+        given_out(slot)
+
+
+def rotated_update(clip, turned, lefts, rights, states):
+    count, rows, _ = turned.shape
+    any_space = pl.BlockSpec(memory_space=pl.ANY)
+    vmem = pl.BlockSpec(memory_space=pltpu.VMEM)
+    shapes = []
+    for weight, _, _ in states:
+        shapes += [jax.ShapeDtypeStruct(weight.shape, f32)] * 3
+        shapes += [jax.ShapeDtypeStruct(weight.shape, bf16)]
+    dma = pltpu.SemaphoreType.DMA
     return pl.pallas_call(
-        adam_kernel,
-        grid=(rows // tile_rows, cols // tile_cols),
-        in_specs=[
-            pl.BlockSpec(memory_space=pltpu.SMEM),
-            tile,
-            tile,
-            tile,
-            grad_tile,
-            pl.BlockSpec((tile_rows // BLOCK, BLOCK, BLOCK), lambda i, j: (i, 0, 0)),
-            pl.BlockSpec((tile_cols // BLOCK, BLOCK, BLOCK), lambda i, j: (j, 0, 0)),
+        partial(adam_kernel, count),
+        in_specs=[pl.BlockSpec(memory_space=pltpu.SMEM), any_space, vmem, vmem]
+        + [any_space] * 15,
+        out_specs=[any_space] * 20,
+        out_shape=shapes,
+        scratch_shapes=[
+            pltpu.VMEM((3, 4, rows, WIDTH), f32),
+            pltpu.VMEM((2, 3, rows, WIDTH), f32),
+            pltpu.VMEM((2, rows, WIDTH), bf16),
+            dma((3, 4)),
+            dma((2, 4)),
         ],
-        out_specs=[tile] * 4,
-        out_shape=[jax.ShapeDtypeStruct((rows, cols), f32)] * 3
-        + [jax.ShapeDtypeStruct((rows, cols), bf16)],
-        scratch_shapes=[pltpu.VMEM((tile_rows, tile_rows), bf16)] * 3,
-        compiler_params=pltpu.CompilerParams(vmem_limit_bytes=48 * 1024 * 1024),
+        compiler_params=pltpu.CompilerParams(vmem_limit_bytes=60 * 1024 * 1024),
         name="rotated_adam",
-    )(factor.reshape(1), weight, first, second, grad, left, right)
+    )(clip, turned, lefts, rights, *[array for state in states for array in state])
 
 
 def bits_of(extent):
@@ -262,6 +321,20 @@
     )
 
 
+def slot_of(n_wide, n_narrow):
+    here = lax.axis_index("narrow")
+    there = lax.axis_index("wide")
+    return there // 2 + n_wide // 2 * (here + n_narrow * (there % 2))
+
+
+def hop_order(n_wide, n_narrow):
+    n_bits = bits_of(n_narrow)
+    w_bits = bits_of(n_wide)
+    places = [("wide", bit, w_bits) for bit in range(1, w_bits)]
+    places += [("narrow", bit, n_bits) for bit in range(n_bits)]
+    return places + [("wide", 0, w_bits)]
+
+
 def route(path, step, count):
     return (step + path) % count
 
@@ -284,6 +357,10 @@
 def flat_rows(n_narrow, shard):
     last = shard_start(n_narrow - 1, shard) + shard_rows(shard)
     return max(-(-last // ALIGN) * ALIGN, 2112)
+
+
+def bases_along_lanes(shape):
+    return shape[0] == BLOCK and shape[2] > BLOCK
 
 
 def silu_slope(value):
@@ -306,16 +383,33 @@
     count = 5
     shards = refs[:count]
     adaptive_ref, info_ref = refs[count : count + 2]
-    outs = refs[count + 2 : count + 14]
-    flat, sheet, time_pre, condition, own_act, adaptive_low, mods_ref, total_ref = outs[4:12]
-    scratch = refs[count + 14 :]
+    left_refs = refs[count + 2 : count + 7]
+    right_refs = refs[count + 7 : count + 12]
+    outs = refs[count + 12 : count + 29]
+    scratch = refs[count + 29 :]
+    (
+        patch_out,
+        final_out,
+        tail_out,
+        time_two_out,
+        sheet,
+        time_pre,
+        condition,
+        own_act,
+        adaptive_low,
+        mods_ref,
+        total_ref,
+        lefts_out,
+        rights_out,
+    ) = outs[4:17]
     gathered = scratch[0]
     wides = scratch[1 : count + 1]
     lows = scratch[count + 1 : 2 * count + 1]
     (
+        flat,
+        turned,
         adaptive_wide,
         info_all,
-        lined,
         part,
         part_in,
         load_sem,
@@ -345,7 +439,7 @@
     loads.append(pltpu.make_async_copy(adaptive_ref, adaptive_wide, load_sem.at[count]))
     for load in loads:
         load.start()
-    slot = there * n_narrow + here
+    slot = slot_of(n_wide, n_narrow)
     info_own = pltpu.make_async_copy(info_ref, info_all.at[pl.ds(slot, 1)], info_sem)
     info_own.start()
     greet(n_wide, n_narrow)
@@ -358,13 +452,13 @@
             pl.ds(path * (cols // 2), cols // 2),
         )
 
-    def narrow_step(number, step):
+    def narrow_step(number, step, own):
         for path in range(2):
             bit = route(path, step, n_bits)
             peer = flipped(here, 1 << bit, n_bits)
             done = sum(1 << route(path, earlier, n_bits) for earlier in range(step))
             for mask in range(n_narrow):
-                if mask & ~done:
+                if mask & ~done or own != (mask == 0):
                     continue
                 place = region(number, flipped(here, mask, n_bits), core, path)
                 arrives = mask | 1 << bit
@@ -449,10 +543,10 @@
         )
         keep.start()
         keeps.append(keep)
-        narrow_step(number, 0)
-
-    places = [("narrow", bit, n_bits) for bit in range(n_bits)]
-    places += [("wide", bit, w_bits) for bit in range(w_bits)]
+        for step in range(n_bits):
+            narrow_step(number, step, True)
+
+    places = hop_order(n_wide, n_narrow)
 
     def info_copy(position):
         axis, bit, bits = places[position]
@@ -474,13 +568,19 @@
         info_copy(position).wait()
         if position + 1 < len(places):
             info_copy(position + 1).start()
-    begin(1)
+        if position + 1 < count:
+            begin(position + 1)
+    for number in range(len(places) + 1, count):
+        begin(number)
+
+    def pass_on(numbers, step):
+        for number in numbers:
+            arrive(number, step)
+            if step + 1 < n_bits:
+                narrow_step(number, step + 1, False)
+
     for step in range(n_bits):
-        arrive(0, step)
-        if step + 1 < n_bits:
-            narrow_step(0, step + 1)
-    for number in range(2, count):
-        begin(number)
+        pass_on([0], step)
     from_sibling(0)
     keeps[0].wait()
 
@@ -506,6 +606,11 @@
     weights = sheet[:, FREQS + 1 : FREQS + 2]
     total_ref[...] = jnp.sum(weights, axis=0, keepdims=True)
     tail = flat[ROW_TAIL : ROW_TAIL + TAIL, :].astype(f32)
+    tail_out[...] = tail
+    patch_out[...] = flat[ROW_PATCH:ROW_TIME_ONE, :]
+    time_two_out[...] = flat[ROW_TIME_TWO:ROW_TABLE, :]
+    last = flat[ROW_FINAL - 9 : ROW_FINAL + 23, :].astype(f32)
+    final_out[...] = last[9 : 9 + PATCH]
     tail_row = ROW_BIAS - ROW_TAIL
     value = dot(sheet[:, :FREQS].astype(bf16), flat[ROW_TIME_ONE:ROW_TIME_TWO, :])
     value = value + tail[tail_row + 1 : tail_row + 2]
@@ -517,23 +622,42 @@
     value = value + dot(pick, flat[ROW_TABLE : ROW_TABLE + 1008, :])
     condition[...] = value
     act = own_columns(jax.nn.silu(value), n_narrow)
-    own_act[...] = act.astype(bf16)
-    lined[...] = act
+    act = act.astype(bf16)
+    own_act[...] = act
 
     loads[count].wait()
     cast_rows(adaptive_wide, adaptive_low)
-    group = n_narrow * images
-    near = lined[pl.ds(pl.multiple_of(there * group, 8), group), :]
-    blocks = []
-    for number in range(n_narrow):
-        blocks.append(near[number * images : (number + 1) * images])
-        blocks.append(jnp.zeros((8 - images, near.shape[1]), f32))
-    near = jnp.concatenate(blocks, axis=0).astype(bf16)
+    row = lax.broadcasted_iota(jnp.int32, (8 * n_narrow, act.shape[0]), 0)
+    column = lax.broadcasted_iota(jnp.int32, (8 * n_narrow, act.shape[0]), 1)
+    owner = there // 2 + n_wide // 2 * (row // 8 + n_narrow * core)
+    chosen = jnp.logical_and(column == owner * images + row % 8, row % 8 < images)
+    near = dot(jnp.where(chosen, 1.0, 0.0).astype(bf16), act).astype(bf16)
     for index in range(8):
         span = slice(index * WIDTH, (index + 1) * WIDTH)
         value = dot(near, adaptive_low[:, span])
         for number in range(n_narrow):
             part[0, number, :, span] = value[8 * number : 8 * number + 8]
+
+    def lay_bases():
+        place = 0
+        for ref in left_refs:
+            blocks = ref.shape[0]
+            lefts_out[place : place + blocks * BLOCK, :] = ref[...].reshape(-1, BLOCK)
+            place = place + blocks * BLOCK
+        place = 0
+        for matrix, ref in enumerate(right_refs):
+            turning = bases_along_lanes(ref.shape)
+            blocks = ref.shape[2] if turning else ref.shape[0]
+            copies = TILES[matrix][1]
+            for row in range(BLOCK):
+                turned[0:blocks, :] = ref[row].T if turning else ref[:, row, :]
+                value = jnp.concatenate(
+                    [turned[pl.ds(spot, blocks // 4, stride=4), :] for spot in range(4)], axis=1
+                )
+                for copy in range(copies):
+                    start = place + copy * blocks // 4 * BLOCK + row
+                    rights_out[pl.ds(start, blocks // 4, stride=BLOCK), :] = value
+            place = place + copies * blocks // 4 * BLOCK
 
     def part_copy(step, mask):
         bit = 1 << step
@@ -567,6 +691,9 @@
             copy = part_copy(step, mask)
             copy.start()
             sends.append(copy)
+        pass_on(range(1, count), step)
+        if step == 0:
+            lay_bases()
         for mask in masks:
             back, owner = part_back(step, mask)
             back.wait_recv()
@@ -581,11 +708,6 @@
                             + tail[tail_row + 9 + index : tail_row + 10 + index]
                         )
 
-    for step in range(n_bits):
-        for number in range(1, count):
-            arrive(number, step)
-            if step + 1 < n_bits:
-                narrow_step(number, step + 1)
     for number in range(1, count):
         from_sibling(number)
     for keep in keeps[1:]:
@@ -594,7 +716,7 @@
         copy.wait_send()
 
 
-def gather_all(n_wide, n_narrow, images, shard, shards, adaptive, info):
+def gather_all(n_wide, n_narrow, images, shard, shards, adaptive, info, lefts, rights):
     count = len(shards)
     any_space = pl.BlockSpec(memory_space=pl.ANY)
     vmem = pl.BlockSpec(memory_space=pltpu.VMEM)
@@ -605,14 +727,17 @@
     total = devices * images
     return pl.pallas_call(
         partial(gather_kernel, n_wide, n_narrow, images, shard),
-        in_specs=[any_space] * (count + 2),
-        out_specs=[any_space] * (count - 1) + [vmem] * 8,
+        in_specs=[any_space] * (count + 2) + [vmem] * 10,
+        out_specs=[any_space] * (count - 1) + [vmem] * 13,
         out_shape=[
             jax.ShapeDtypeStruct((piece.shape[0] * n_narrow, piece.shape[1]), bf16)
             for piece in shards[1:]
         ]
         + [
-            jax.ShapeDtypeStruct((flat_rows(n_narrow, shard), WIDTH), bf16),
+            jax.ShapeDtypeStruct((PATCH, WIDTH), bf16),
+            jax.ShapeDtypeStruct((PATCH, WIDTH), f32),
+            jax.ShapeDtypeStruct((TAIL, WIDTH), f32),
+            jax.ShapeDtypeStruct((WIDTH, WIDTH), bf16),
             jax.ShapeDtypeStruct((total, SHEET), f32),
             jax.ShapeDtypeStruct((total, WIDTH), f32),
             jax.ShapeDtypeStruct((total, WIDTH), f32),
@@ -620,14 +745,17 @@
             jax.ShapeDtypeStruct(adaptive.shape, bf16),
             jax.ShapeDtypeStruct((images, 8, WIDTH), f32),
             jax.ShapeDtypeStruct((1, 1), f32),
+            jax.ShapeDtypeStruct((8 * rows, BLOCK), f32),
+            jax.ShapeDtypeStruct((len(tile_places()) * 6 * BLOCK, 4 * BLOCK), f32),
         ],
         scratch_shapes=[pltpu.VMEM((shards[0].shape[0] * n_narrow, WIDTH), bf16)]
         + [pltpu.VMEM(piece.shape, f32) for piece in shards]
         + [pltpu.VMEM(piece.shape, bf16) for piece in shards]
         + [
+            pltpu.VMEM((flat_rows(n_narrow, shard), WIDTH), bf16),
+            pltpu.VMEM((8 * WIDTH // BLOCK, BLOCK), f32),
             pltpu.VMEM(adaptive.shape, f32),
             pltpu.VMEM((devices,) + info.shape[1:], f32),
-            pltpu.VMEM((total, rows), f32),
             pltpu.VMEM((n_bits, n_narrow, 8, 8 * WIDTH), f32),
             pltpu.VMEM((n_bits, n_narrow, 8, 8 * WIDTH), f32),
             dma((count + 1,)),
@@ -646,7 +774,7 @@
             collective_id=0, has_side_effects=True, vmem_limit_bytes=56 * 1024 * 1024
         ),
         name="gather_weights",
-    )(*shards, adaptive, info)
+    )(*shards, adaptive, info, *lefts, *rights)
 
 
 RING = 4
@@ -665,25 +793,36 @@
         condition,
         own_act,
         time_two,
-    ) = refs[4:14]
-    out_ref, adaptive_out, rows_out, window_out, totals_out, clip_out = refs[14:20]
-    scratch = refs[20:]
+        lefts,
+        rights,
+    ) = refs[4:16]
+    turned_out, rows_out, window_out, totals_out, clip_out = refs[16:21]
+    out_ref = refs[21]
+    scratch = refs[22:]
     own, from_core, to_near, from_near, to_far, from_far, acc, acc_far = scratch[:8]
     load_sem, core_sem, near_sem, far_sem, back_sem, last_sem = scratch[8:14]
     (
         mods_all,
+        by_mod,
+        product_parts,
+        first_part,
+        biases,
         small_out,
         small_in,
+        small_all,
         act_all,
         stage,
         norm_out,
         norm_in,
         squares,
+        ring,
         mods_sem,
+        mods_near_sem,
         small_sem,
         act_sem,
         rows_sem,
         norm_sem,
+        ring_sem,
     ) = scratch[14:]
     here = lax.axis_index("narrow")
     there = lax.axis_index("wide")
@@ -766,7 +905,7 @@
         bit, masks = leaving[path][step]
         spots = pl.ds(min(masks.values()), len(masks))
         return remote(
-            to_near.at[path, k, spots],
+            to_near.at[path, k % RING, spots],
             from_near.at[path, k, spots],
             near_sem.at[0, path, k, step],
             near_sem.at[1, path, k, step],
@@ -776,7 +915,7 @@
 
     def far_copy(k, step, part):
         return remote(
-            to_far.at[(k, step) + window(part)],
+            to_far.at[(k % RING, step) + window(part)],
             from_far.at[(k, step) + window(part)],
             far_sem.at[0, k, step],
             far_sem.at[1, k, step],
@@ -807,18 +946,24 @@
 
     def place_near(path, k, step, mask, total):
         columns = pl.ds(path * side, side)
-        ring = k % RING
+        ring_slot = k % RING
         if step == n_bits:
-            acc_far[ring, :, columns] = total
+            acc_far[ring_slot, :, columns] = total
         elif mask in leaving[path][step][1]:
-            to_near[path, k, leaving[path][step][1][mask]] = total.astype(bf16)
+            to_near[path, ring_slot, leaving[path][step][1][mask]] = total.astype(bf16)
         else:
-            acc[ring, mask, :, columns] = total
+            acc[ring_slot, mask, :, columns] = total
+
+    def before(k, wait):
+        @pl.when(k >= RING)
+        def _():
+            wait()
 
     def stage_core(k):
         keep_copy(k, grad_refs[0], k).wait()
         give_copy(k, grad_refs[0], k).wait_recv()
         for path in range(2):
+            before(k, lambda path=path: near_copy(path, k - RING, 0).wait_send())
             columns = pl.ds(path * side, side)
             for mask in range(n_narrow):
                 owner = flipped(here, mask, n_bits)
@@ -830,13 +975,15 @@
         start_keep(k + RING - 1)
 
     def stage_near(step, k):
-        ring = k % RING
+        ring_slot = k % RING
         for path in range(2):
             columns = pl.ds(path * side, side)
             near_copy(path, k, step).wait_recv()
+            if step + 1 < n_bits:
+                before(k, lambda path=path: near_copy(path, k - RING, step + 1).wait_send())
             bit, masks = leaving[path][step]
             for mask, spot in masks.items():
-                total = acc[ring, mask - bit, :, columns] + from_near[path, k, spot].astype(f32)
+                total = acc[ring_slot, mask - bit, :, columns] + from_near[path, k, spot].astype(f32)
                 place_near(path, k, step + 1, mask - bit, total)
             if step + 1 < n_bits:
                 near_copy(path, k, step + 1).start()
@@ -844,25 +991,26 @@
             start_far(0, k)
 
     def start_far(step, k):
-        ring = k % RING
+        ring_slot = k % RING
         if step < far_steps:
             place = window(gives[step])
-            to_far[(k, step) + place] = acc_far[(ring,) + place].astype(bf16)
+            before(k, lambda: far_copy(k - RING, step, gives[step]).wait_send())
+            to_far[(ring_slot, step) + place] = acc_far[(ring_slot,) + place].astype(bf16)
             far_copy(k, step, gives[step]).start()
         else:
             place = window(parts[step])
-            out_ref[(k, core) + place] = acc_far[(ring,) + place].astype(bf16)
+            out_ref[(k, core) + place] = acc_far[(ring_slot,) + place].astype(bf16)
             start_back(far_steps - 1, k)
 
     def stage_far(step, k):
-        ring = k % RING
+        ring_slot = k % RING
         far_copy(k, step, parts[step + 1]).wait_recv()
         place = window(parts[step + 1])
         if traded[step]:
-            mine = acc_far[(ring,) + place]
+            mine = acc_far[(ring_slot,) + place]
         else:
-            mine = to_far[(k, step) + place].astype(f32)
-        acc_far[(ring,) + place] = mine + from_far[(k, step) + place].astype(f32)
+            mine = to_far[(ring_slot, step) + place].astype(f32)
+        acc_far[(ring_slot,) + place] = mine + from_far[(k, step) + place].astype(f32)
         start_far(step + 1, k)
 
     def start_back(step, k):
@@ -880,10 +1028,34 @@
     def add_squares(value):
         squares[...] += jnp.sum(value * value, axis=0, keepdims=True)
 
+    def turned_copy(slot, tile):
+        return pltpu.make_async_copy(ring.at[slot], turned_out.at[tile], ring_sem.at[slot])
+
+    def turn(high, rest, stack, tile, slot, used):
+        @pl.when(used)
+        def _():
+            turned_copy(slot, tile).wait()
+
+        left, left_rest = spread_left(lefts[stack])
+        for start in range(0, WIDTH, STRIP):
+            span = slice(start, start + STRIP)
+            group = tile * (WIDTH // BLOCK // 4) + start // BLOCK // 4
+            right, right_rest = halves(spread_right(rights[group], rights[group + 1]))
+            value = dot(high[:, span], right) + dot(high[:, span], right_rest)
+            if rest is not None:
+                value = value + dot(rest[:, span], right)
+            part, part_rest = halves(value)
+            ring[slot, :, span] = dot_s(left, part) + (
+                dot_s(left_rest, part) + dot_s(left, part_rest)
+            )
+        turned_copy(slot, tile).start()
+
     def stage_last(k):
         last_copy(k, 1 - core).wait_recv()
         for number in range(2):
             add_squares(out_ref[k, number].astype(f32))
+        value = out_ref[k].reshape(2 * half, width)
+        turn(value, None, left_number(k), k, k % 2, k >= 2)
 
     stages = [stage_core]
     stages += [partial(stage_near, step) for step in range(n_bits)]
@@ -891,11 +1063,10 @@
     stages += [partial(stage_back, step) for step in reversed(range(far_steps)) if traded[step]]
     stages += [stage_last]
 
-    places = [("narrow", bit, n_bits) for bit in range(n_bits)]
-    places += [("wide", bit, w_bits) for bit in range(w_bits)]
+    places = hop_order(n_wide, n_narrow)
+    near_places = [("narrow", bit, n_bits) for bit in range(n_bits)]
     hops = len(places)
-    slot = there * n_narrow + here
-    per = images * 8
+    slot = slot_of(n_wide, n_narrow)
     count = n_wide * n_narrow * images
 
     def beside(axis, bit, bits, source, target, sem, position):
@@ -908,23 +1079,61 @@
             flipped(lax.axis_index(axis), 1 << bit, bits),
         )
 
+    column_bits = n_wide // 2
+    half_rows = small_out.shape[1] // 2
+    own_rows = pl.ds(pl.multiple_of(half_rows * core, 8), half_rows)
+    small_places = places[hops - 1 :] + places[: hops - 1]
+
     def mods_copy(position):
         width = 1 << position
         block = mods_all.at[pl.ds(slot // width * width, width)]
         return beside(*places[position], block, block, mods_sem, position)
 
+    def mods_near(path, step, mask, arrived):
+        owner = flipped(here, arrived if mask is None else mask, n_bits)
+        bit = 1 << route(path, step, n_bits)
+        block = mods_all.at[
+            pl.ds(column_bits * (owner + n_narrow * core), column_bits),
+            :,
+            pl.ds(path * side, side),
+        ]
+        return remote(
+            block,
+            block,
+            mods_near_sem.at[0, path, arrived - 1],
+            mods_near_sem.at[1, path, arrived - 1],
+            "narrow",
+            flipped(here, bit, n_bits),
+        )
+
+    def near_masks(path, step):
+        done = sum(1 << route(path, earlier, n_bits) for earlier in range(step))
+        bit = 1 << route(path, step, n_bits)
+        return [(mask, mask | bit) for mask in range(n_narrow) if not mask & ~done]
+
     def small_copy(position):
+        if position == 0:
+            return beside(
+                *small_places[0], small_out.at[0], small_in.at[0], small_sem, position
+            )
+        if position == hops:
+            block = small_all.at[own_rows]
+            return beside(*small_places[0], block, block, small_sem, position)
         return beside(
-            *places[position], small_out.at[position], small_in.at[position], small_sem, position
+            *small_places[position],
+            small_out.at[position, own_rows],
+            small_in.at[position, own_rows],
+            small_sem,
+            position,
         )
 
     def act_copy(position):
         width = 1 << position
         block = act_all.at[pl.ds(here // width * width, width)]
-        return beside(*places[position], block, block, act_sem, position)
+        return beside(*near_places[position], block, block, act_sem, position)
 
     def small_total():
-        return small_out[hops - 1] + small_in[hops - 1]
+        return small_all[...]
 
     def rows_copy(start, rows, position):
         return pltpu.make_async_copy(
@@ -939,33 +1148,68 @@
             rows_out.at[pl.ds(pl.multiple_of(start, ALIGN), height)], window_out, rows_sem.at[2]
         )
 
-    def spread_hop(position):
+    def mods_hop(position):
         if position == 0:
             mods_all[slot] = g_mods_ref[...].astype(bf16)
+        elif position <= far_steps or position == hops:
+            mods_copy(position - 1).wait_recv()
+        else:
+            step = position - 1 - far_steps
+            for path in range(2):
+                for _, arrived in near_masks(path, step):
+                    mods_near(path, step, None, arrived).wait_recv()
+        if position < far_steps or position == hops - 1:
+            mods_copy(position).start()
+        elif position < hops:
+            step = position - far_steps
+            for path in range(2):
+                for mask, arrived in near_masks(path, step):
+                    mods_near(path, step, mask, arrived).start()
+
+    def small_hop(position):
+        if position == 0:
             small_out[0, 0:PATCH] = g_patch_ref[...]
             small_out[0, PATCH : 2 * PATCH] = g_final_ref[...]
             small_out[0, 2 * PATCH : 2 * PATCH + 8] = g_bias_ref[...]
+            small_out[0, 2 * PATCH + 8 :] = jnp.zeros(
+                (small_out.shape[1] - 2 * PATCH - 8, WIDTH), f32
+            )
         else:
-            mods_copy(position - 1).wait_recv()
             small_copy(position - 1).wait_recv()
+            total = small_out[position - 1, own_rows] + small_in[position - 1, own_rows]
             if position < hops:
-                small_out[position] = small_out[position - 1] + small_in[position - 1]
-        if position < hops:
-            mods_copy(position).start()
-            small_copy(position).start()
-
-    def which_mod(shape):
-        return lax.broadcasted_iota(jnp.int32, shape, 0) % 8
+                small_out[position, own_rows] = total
+            else:
+                small_all[own_rows] = total
+        small_copy(position).start()
+
+    def small_end():
+        other = pl.ds(pl.multiple_of(half_rows * (1 - core), 8), half_rows)
+        block = small_all.at[other]
+        beside(*small_places[0], block, block, small_sem, hops).wait_recv()
+
+    def sort_mods():
+        together = 8
+        size = together * images * 8
+        row = lax.broadcasted_iota(jnp.int32, (size, size), 0)
+        column = lax.broadcasted_iota(jnp.int32, (size, size), 1)
+        span = together * images
+        order = jnp.where(column == row % span * 8 + row // span, 1.0, 0.0).astype(bf16)
+        for block in range(mods_all.shape[0] // together):
+            value = mods_all[block * together : (block + 1) * together].reshape(size, WIDTH)
+            value = dot(order, value).astype(bf16)
+            for index in range(8):
+                by_mod[index, block * span : (block + 1) * span, :] = value[
+                    index * span : (index + 1) * span
+                ]
 
     def send_act():
-        everything = mods_all[...].reshape(count * 8, WIDTH)
-        kind = which_mod((count * 8, act_all.shape[2]))
-        total = jnp.zeros((count * 8, act_all.shape[2]), f32)
+        sort_mods()
+        total = jnp.zeros(act_all.shape[1:], f32)
         for index in range(8):
             span = slice(index * WIDTH, (index + 1) * WIDTH)
-            value = dot_t(everything, adaptive_low[:, span])
-            total = total + jnp.where(kind == index, value, 0.0)
-        act_all[here] = jnp.sum(total.reshape(count, 8, -1), axis=1)
+            total = total + dot_t(by_mod[index], adaptive_low[:, span])
+        act_all[here] = total
         act_copy(0).start()
 
     def act_hop(position):
@@ -973,66 +1217,67 @@
         if position < n_bits:
             act_copy(position).start()
 
-    def grad_condition():
+    def start_rows():
         grad = jnp.concatenate([act_all[number] for number in range(n_narrow)], axis=1)
-        return grad * silu_slope(condition[...])
-
-    def grad_time():
-        low = grad_condition().astype(bf16)
+        grad = grad * silu_slope(condition[...])
+        high, rest = halves(grad)
         before = time_pre[...]
-        return low, (dot_t(low, time_two[...]) * silu_slope(before)).astype(bf16)
+        first = (dot_t(high, time_two[...]) * silu_slope(before)).astype(bf16)
+        product_parts[0:count] = high
+        product_parts[count : 2 * count] = rest
+        first_part[...] = first
+        biases[0:1, :] = jnp.sum(first.astype(f32), axis=0, keepdims=True)
+        biases[1:2, :] = jnp.sum(high.astype(f32), axis=0, keepdims=True)
 
     def upper_rows():
-        low, first = grad_time()
         stage[0:PATCH, :] = small_total()[0:PATCH]
-        stage[ROW_TIME_ONE:ROW_TIME_TWO, :] = dot_s(sheet[:, :FREQS].astype(bf16), first)
+        stage[ROW_TIME_ONE:ROW_TIME_TWO, :] = dot_s(
+            sheet[:, :FREQS].astype(bf16), first_part[...]
+        )
         act = jax.nn.silu(time_pre[...]).astype(bf16)
-        stage[ROW_TIME_TWO:ROW_TABLE, :] = dot_s(act, low)
+        stage[ROW_TIME_TWO:ROW_TABLE, :] = dot_s(act, product_parts[0:count])
         rows_copy(0, ROW_TABLE, 0).start()
 
+    def table_rows(half_of):
+        if half_of == 0:
+            rows_copy(0, ROW_TABLE, 0).wait()
+        size = 504
+        labels = lax.broadcasted_iota(jnp.int32, (count, size), 1) + half_of * size
+        pick = jnp.where(sheet[:, FREQS : FREQS + 1] == labels.astype(f32), 1.0, 0.0)
+        pick = pick.astype(bf16)
+        pick = jnp.concatenate([pick, pick], axis=0)
+        stage[half_of * size : (half_of + 1) * size, :] = dot_s(pick, product_parts[...])
+
     def lower_rows():
-        rows_copy(0, ROW_TABLE, 0).wait()
-        grad = grad_condition()
-        low, first = grad_time()
-        labels = lax.broadcasted_iota(jnp.int32, (count, 1008), 1).astype(f32)
-        pick = jnp.where(sheet[:, FREQS : FREQS + 1] == labels, 1.0, 0.0).astype(bf16)
-        high, rest = halves(grad)
-        rest = grad - high.astype(f32)
-        middle, rest = halves(rest)
-        table = dot_s(pick, high) + (dot_s(pick, middle) + dot_s(pick, rest))
-        stage[0:1008, :] = table
         small = small_total()
         base = ROW_FINAL - ROW_TABLE
         stage[base : base + PATCH, :] = small[PATCH : 2 * PATCH]
         base = ROW_BIAS - ROW_TABLE
         bias = small[2 * PATCH : 2 * PATCH + 8]
         stage[base : base + 1, :] = bias[0:1]
-        stage[base + 1 : base + 2, :] = jnp.sum(first.astype(f32), axis=0, keepdims=True)
-        stage[base + 2 : base + 3, :] = jnp.sum(low.astype(f32), axis=0, keepdims=True)
+        stage[base + 1 : base + 3, :] = biases[0:2, :]
         stage[base + 3 : base + 4, :] = bias[1:2]
         stage[base + 4 : base + 8, :] = bias[4:8]
         stage[base + 8 : base + 9, :] = bias[2:3]
-        stage[base + 9 : base + 17, :] = jnp.sum(
-            mods_all[...].astype(f32).reshape(count, 8, WIDTH), axis=0
-        )
+        for index in range(8):
+            stage[base + 9 + index : base + 10 + index, :] = jnp.sum(
+                by_mod[index].astype(f32), axis=0, keepdims=True
+            )
         lane = lax.broadcasted_iota(jnp.int32, (1, WIDTH), 1)
         stage[base + 17 : base + 18, :] = jnp.where(lane < PATCH, bias[3:4], 0.0)
         stage[base + 18 :, :] = jnp.zeros((stage.shape[0] - base - 18, WIDTH), f32)
         totals_out[...] = bias
         rows_copy(ROW_TABLE, stage.shape[0], 1).start()
 
-    def adaptive_rows():
-        everything = mods_all[...].reshape(count * 8, WIDTH)
-        act = own_act[...].astype(f32)
-        act = jnp.broadcast_to(act[:, None, :], (count, 8, act.shape[1]))
-        act = act.reshape(count * 8, -1).astype(bf16)
-        kind = which_mod(act.shape)
-        for index in range(8):
-            span = slice(index * WIDTH, (index + 1) * WIDTH)
-            here_act = jnp.where(kind == index, act, jnp.zeros((), bf16))
-            value = dot_s(here_act, everything)
-            add_squares(value)
-            adaptive_out[:, span] = value.astype(bf16)
+    first_turn = chunks
+
+    def adaptive_columns(index):
+        value = dot_s(own_act[...], by_mod[index])
+        add_squares(value)
+        high, rest = halves(value)
+        turn(high, rest, lefts.shape[0] - 1, first_turn + index, 2 + index % 2, index >= 2)
+
+    def start_window():
         rows_copy(ROW_TABLE, stage.shape[0], 1).wait()
         window_copy().start()
 
@@ -1048,20 +1293,26 @@
         inside = jnp.logical_and(spot >= first, spot < first + shard)
         add_squares(jnp.where(inside, value, 0.0))
 
-    asides = [partial(spread_hop, position) for position in range(hops)]
-
-    def last_hop():
-        spread_hop(hops)
-        send_act()
-
-    asides += [last_hop]
+    def together(*steps):
+        return lambda: [step() for step in steps]
+
+    asides = [
+        together(partial(mods_hop, position), partial(small_hop, position))
+        for position in range(hops)
+    ]
+    asides += [together(partial(mods_hop, hops), partial(small_hop, hops), send_act)]
+    first_act = len(asides)
     asides += [partial(act_hop, position) for position in range(1, n_bits)]
-
-    def last_act():
-        act_hop(n_bits)
-        upper_rows()
-
-    asides += [last_act, lower_rows, adaptive_rows, window_squares]
+    asides[-1] = together(asides[-1], small_end)
+    asides += [
+        together(partial(act_hop, n_bits), start_rows),
+        upper_rows,
+        partial(table_rows, 0),
+        partial(table_rows, 1),
+        lower_rows,
+        start_window,
+        window_squares,
+    ]
 
     squares[...] = jnp.zeros_like(squares)
     greet(n_wide, n_narrow)
@@ -1092,35 +1343,58 @@
             def _(aside=aside):
                 aside()
 
+        index = t - first_act
+
+        @pl.when(jnp.logical_and(index >= 0, index < 8))
+        def _():
+            adaptive_columns(index)
+
         return carry
 
-    lax.fori_loop(0, max(chunks + len(stages) - 1, len(asides)), wave, 0)
+    lax.fori_loop(0, max(chunks + len(stages) - 1, len(asides), first_act + 8), wave, 0)
 
     def finish(k, carry):
         give_copy(k, grad_refs[0], k).wait_send()
+        for step in range(far_steps):
+            if traded[step]:
+                back_copy(k, step, parts[step + 1]).wait_send()
+        last_copy(k, core).wait_send()
+        return carry
+
+    lax.fori_loop(0, chunks, finish, 0)
+
+    def finish_ring(k, carry):
         for path in range(2):
             for step in range(n_bits):
                 near_copy(path, k, step).wait_send()
         for step in range(far_steps):
             far_copy(k, step, gives[step]).wait_send()
-            if traded[step]:
-                back_copy(k, step, parts[step + 1]).wait_send()
-        last_copy(k, core).wait_send()
         return carry
 
-    lax.fori_loop(0, chunks, finish, 0)
-    for position in range(hops):
+    lax.fori_loop(chunks - RING, chunks, finish_ring, 0)
+    for position in [*range(far_steps), hops - 1]:
         mods_copy(position).wait_send()
+    for path in range(2):
+        for step in range(n_bits):
+            for mask, arrived in near_masks(path, step):
+                mods_near(path, step, mask, arrived).wait_send()
+    for position in range(hops + 1):
         small_copy(position).wait_send()
     for position in range(n_bits):
         act_copy(position).wait_send()
+    for slot_of_ring in range(4):
+        turned_copy(slot_of_ring, 0).wait()
 
     total = jnp.sum(squares[...], axis=1, keepdims=True)
     value = jnp.broadcast_to(total, norm_out.shape[1:])
     for position in range(n_bits):
         norm_out[position] = value
         copy = beside(
-            *places[position], norm_out.at[position], norm_in.at[position], norm_sem, position
+            *near_places[position],
+            norm_out.at[position],
+            norm_in.at[position],
+            norm_sem,
+            position,
         )
         copy.start()
         copy.wait()
@@ -1142,24 +1416,24 @@
     any_space = pl.BlockSpec(memory_space=pl.ANY)
     vmem = pl.BlockSpec(memory_space=pltpu.VMEM)
     height = flat_rows(n_narrow, shard)
-    out, adaptive, _, window, totals, clip = pl.pallas_call(
+    turned, _, window, totals, clip = pl.pallas_call(
         partial(reduce_kernel, n_wide, n_narrow, images, shard),
         in_specs=[any_space] * 4 + [vmem] * len(asides),
-        out_specs=[vmem, vmem, any_space, vmem, vmem, vmem],
+        out_specs=[any_space, any_space, vmem, vmem, vmem],
         out_shape=[
-            jax.ShapeDtypeStruct((chunks, 2, half, WIDTH), bf16),
-            jax.ShapeDtypeStruct((rows, 8 * WIDTH), bf16),
+            jax.ShapeDtypeStruct((chunks + 8, rows, WIDTH), f32),
             jax.ShapeDtypeStruct((height, WIDTH), f32),
             jax.ShapeDtypeStruct((shard_rows(shard), WIDTH), f32),
             jax.ShapeDtypeStruct((8, WIDTH), f32),
             jax.ShapeDtypeStruct((8, 128), f32),
         ],
         scratch_shapes=[
+            pltpu.VMEM((chunks, 2, half, WIDTH), bf16),
             pltpu.VMEM((RING, n_narrow, half, WIDTH), bf16),
             pltpu.VMEM((chunks, n_narrow, half, WIDTH), bf16),
+            pltpu.VMEM((2, RING, n_narrow - 1, half, WIDTH // 2), bf16),
             pltpu.VMEM((2, chunks, n_narrow - 1, half, WIDTH // 2), bf16),
-            pltpu.VMEM((2, chunks, n_narrow - 1, half, WIDTH // 2), bf16),
-            pltpu.VMEM((chunks, far, half, WIDTH), bf16),
+            pltpu.VMEM((RING, far, half, WIDTH), bf16),
             pltpu.VMEM((chunks, far, half, WIDTH), bf16),
             pltpu.VMEM((RING, n_narrow, half, WIDTH), f32),
             pltpu.VMEM((RING, half, WIDTH), f32),
@@ -1170,18 +1444,26 @@
             dma((2, chunks, far)),
             dma((2, chunks)),
             pltpu.VMEM((devices, images * 8, WIDTH), bf16),
-            pltpu.VMEM((hops, 2 * PATCH + 8, WIDTH), f32),
-            pltpu.VMEM((hops, 2 * PATCH + 8, WIDTH), f32),
+            pltpu.VMEM((8, count, WIDTH), bf16),
+            pltpu.VMEM((2 * count, WIDTH), bf16),
+            pltpu.VMEM((count, WIDTH), bf16),
+            pltpu.VMEM((8, WIDTH), f32),
+            pltpu.VMEM((hops, 3 * PATCH, WIDTH), f32),
+            pltpu.VMEM((hops, 3 * PATCH, WIDTH), f32),
+            pltpu.VMEM((3 * PATCH, WIDTH), f32),
             pltpu.VMEM((n_narrow, count, rows), f32),
             pltpu.VMEM((height - ROW_TABLE, WIDTH), f32),
             pltpu.VMEM((bits_of(n_narrow), 8, 128), f32),
             pltpu.VMEM((bits_of(n_narrow), 8, 128), f32),
             pltpu.VMEM((1, WIDTH), f32),
+            pltpu.VMEM((4, rows, WIDTH), f32),
             dma((2, hops)),
-            dma((2, hops)),
+            dma((2, 2, n_narrow - 1)),
+            dma((2, hops + 1)),
             dma((2, bits_of(n_narrow))),
             dma((3,)),
             dma((2, bits_of(n_narrow))),
+            dma((4,)),
         ],
         compiler_params=pltpu.CompilerParams(
             collective_id=1, has_side_effects=True, vmem_limit_bytes=62 * 1024 * 1024
@@ -1191,41 +1473,105 @@
         ),
         name="reduce_gradients",
     )(*grads, *asides)
-    return out.reshape(chunks * rows, WIDTH), adaptive, window, totals, clip
-
-
-def weight_kernel(left_ref, right_ref, out_ref):
-    value = dot_s(left_ref[...], right_ref[...]).astype(bf16)
-    out_ref[...] = value.reshape(out_ref.shape)
-
-
-def weight_blocks(n_narrow, inputs, gradient):
-    tokens, depth = inputs.shape
-    across = gradient.shape[1] // WIDTH
-    down = depth // WIDTH
+    return turned, window, totals, clip
+
+
+def weight_kernel(*refs):
+    lefts, rights, outs = refs[0:4], refs[4:8], refs[8:12]
+    taken, given, take_sem, give_sem = refs[12:]
+    _, pieces, rows, _ = given.shape
+    units = [
+        (matrix, number)
+        for matrix in range(4)
+        for number in range(max(lefts[matrix].shape[1], rights[matrix].shape[1]) // WIDTH)
+    ]
+
+    def takes(unit):
+        matrix, number = units[unit]
+        copies = []
+        for side, ref in enumerate((lefts[matrix], rights[matrix])):
+            start = number * WIDTH if ref.shape[1] > WIDTH else 0
+            copies.append(
+                pltpu.make_async_copy(
+                    ref.at[:, pl.ds(start, WIDTH)],
+                    taken.at[unit % 3, side],
+                    take_sem.at[unit % 3, side],
+                )
+            )
+        return copies
+
+    def give(unit):
+        matrix, number = units[unit]
+        if matrix < 3:
+            target = outs[matrix].at[:, pl.ds(number * rows, rows), :]
+        else:
+            target = outs[3].at[pl.ds(number * pieces, pieces)]
+        return pltpu.make_async_copy(given.at[unit % 2], target, give_sem.at[unit % 2])
+
+    def given_out(slot):
+        pltpu.make_async_copy(given.at[slot], given.at[slot], give_sem.at[slot]).wait()
+
+    for unit in range(2):
+        for copy in takes(unit):
+            copy.start()
+
+    def body(step, carry):
+        for unit in range(2, len(units)):
+
+            @pl.when(step + 2 == unit)
+            def _(unit=unit):
+                for copy in takes(unit):
+                    copy.start()
+
+        slot = step % 3
+        out = step % 2
+        for side in range(2):
+            buffer = taken.at[slot, side]
+            pltpu.make_async_copy(buffer, buffer, take_sem.at[slot, side]).wait()
+
+        @pl.when(step >= 2)
+        def _():
+            given_out(out)
+
+        for start in range(0, WIDTH, STRIP):
+            span = slice(start, start + STRIP)
+            value = dot_s(taken[slot, 0], taken[slot, 1, :, span]).astype(bf16)
+            given[out, :, :, span] = value.reshape(pieces, rows, STRIP)
+        for unit in range(len(units)):
+
+            @pl.when(step == unit)
+            def _(unit=unit):
+                give(unit).start()
+
+        return carry
+
+    lax.fori_loop(0, len(units), body, 0)
+    for slot in range(2):
+        given_out(slot)
+
+
+def weight_blocks(n_narrow, inputs, gradients):
     rows = WIDTH // n_narrow
-    if down == 1:
-        grid = across
-        left = pl.BlockSpec((tokens, WIDTH), lambda i: (0, 0))
-        right = pl.BlockSpec((tokens, WIDTH), lambda i: (0, i))
-        out = pl.BlockSpec((n_narrow, rows, WIDTH), lambda i: (0, i, 0))
-        shape = (n_narrow, across * rows, WIDTH)
-    else:
-        grid = down
-        left = pl.BlockSpec((tokens, WIDTH), lambda i: (0, i))
-        right = pl.BlockSpec((tokens, WIDTH), lambda i: (0, 0))
-        out = pl.BlockSpec((WIDTH, WIDTH), lambda i: (i, 0))
-        shape = (depth, WIDTH)
-    result = pl.pallas_call(
+    tokens = inputs[0].shape[0]
+    any_space = pl.BlockSpec(memory_space=pl.ANY)
+    shapes = [(n_narrow, gradient.shape[1] // n_narrow, WIDTH) for gradient in gradients[:3]]
+    shapes.append((inputs[3].shape[1] // rows, rows, WIDTH))
+    dma = pltpu.SemaphoreType.DMA
+    results = pl.pallas_call(
         weight_kernel,
-        grid=(grid,),
-        in_specs=[left, right],
-        out_specs=out,
-        out_shape=jax.ShapeDtypeStruct(shape, bf16),
-        compiler_params=pltpu.CompilerParams(vmem_limit_bytes=48 * 1024 * 1024),
+        in_specs=[any_space] * 8,
+        out_specs=[any_space] * 4,
+        out_shape=[jax.ShapeDtypeStruct(shape, bf16) for shape in shapes],
+        scratch_shapes=[
+            pltpu.VMEM((3, 2, tokens, WIDTH), bf16),
+            pltpu.VMEM((2, n_narrow, rows, WIDTH), bf16),
+            dma((3, 2)),
+            dma((2,)),
+        ],
+        compiler_params=pltpu.CompilerParams(vmem_limit_bytes=60 * 1024 * 1024),
         name="weight_gradient",
-    )(inputs, gradient)
-    return result.reshape(n_narrow, -1, WIDTH)
+    )(*inputs, *gradients)
+    return [result.reshape(n_narrow, -1, WIDTH) for result in results]
 
 
 def dot_s(left, right):
@@ -1326,7 +1672,7 @@
         triple[:, span] = dot(normed_ref[...], attend_ref[:, span]).astype(bf16)
         return carry
 
-    lax.fori_loop(0, 3 * WIDTH // wide, project, 0)
+    lax.fori_loop(0, 3 * WIDTH // wide, project, 0, unroll=True)
 
     lane = lax.broadcasted_iota(jnp.int32, (tokens, 2 * HEAD_DIM), 1)
     first_half = lane < HEAD_DIM
@@ -1355,7 +1701,7 @@
         mixed_ref[:, query_span] = jnp.where(first_half, results[0], results[1]).astype(bf16)
         return carry
 
-    lax.fori_loop(0, HEADS // 2, attend, 0)
+    lax.fori_loop(0, HEADS // 2, attend, 0, unroll=True)
 
     value = dot(mixed_ref[...], output_ref[...]) + bias(3)
     branch[...] = value
@@ -1374,7 +1720,7 @@
         slope[:, span] = steep
         return carry
 
-    lax.fori_loop(0, MLP_WIDTH // wide, widen, 0)
+    lax.fori_loop(0, MLP_WIDTH // wide, widen, 0, unroll=True)
 
     branch_two = dot(act_ref[...], shrink_ref[...]) + bias(8)
     upper = hidden[...] + row(5) * branch_two
@@ -1407,7 +1753,7 @@
         g_bias_ref[bias_wide(g_bias_ref, 4, index)] += jnp.sum(grad_pre.astype(f32), axis=0, keepdims=True)
         return carry
 
-    lax.fori_loop(0, MLP_WIDTH // wide, narrow, 0)
+    lax.fori_loop(0, MLP_WIDTH // wide, narrow, 0, unroll=True)
 
     grad = dot_t(g_pre_ref[...], expand_ref[...])
     normal = normal_two[...]
@@ -1447,7 +1793,7 @@
             g_triple_ref[:, span] = merged.astype(bf16)
         return carry
 
-    lax.fori_loop(0, HEADS // 2, attend_back, 0)
+    lax.fori_loop(0, HEADS // 2, attend_back, 0, unroll=True)
 
     grad = dot_t(g_triple_ref[...], attend_ref[...])
     normal = normal_one[...]
@@ -1585,13 +1931,26 @@
     rows = shard_rows(shard)
     row_start = column * shard // (WIDTH * ALIGN) * ALIGN
     offset = column * shard - row_start * WIDTH
-    margin = (ALIGN + 1) * WIDTH
-    own = jnp.concatenate(
-        [jnp.zeros((margin,), f32), shared_weight, jnp.zeros((rows * WIDTH - shard,), f32)]
-    )
+    margin = -(-(ALIGN + 1) * WIDTH // 1024) * 1024
+    own = lax.pad(shared_weight, f32(0.0), [(margin, rows * WIDTH - shard, 0)])
     own = lax.dynamic_slice(own, (margin - offset,), (rows * WIDTH,)).reshape(rows, WIDTH)
 
-    *full, flat, sheet, time_pre, condition, own_act, adaptive_low, mods, total = gather_all(
+    (
+        *full,
+        patch_w,
+        final_rows,
+        tail,
+        time_two,
+        sheet,
+        time_pre,
+        condition,
+        own_act,
+        adaptive_low,
+        mods,
+        total,
+        lefts,
+        rights,
+    ) = gather_all(
         n_wide,
         n_narrow,
         images,
@@ -1599,7 +1958,14 @@
         (own, attend_weight, output_weight, expand_weight, shrink_weight),
         adaptive_weight,
         info,
+        (attend_left, output_left, expand_left, shrink_left, adaptive_left),
+        [
+            blocks.transpose(1, 2, 0) if blocks.shape[0] > BLOCK else blocks
+            for blocks in (attend_right, output_right, expand_right, shrink_right, adaptive_right)
+        ],
     )
+    lefts = lefts.reshape(8, -1, BLOCK)
+    rights = rights.reshape(-1, BLOCK, 4 * BLOCK)
     weight_sum = total[0, 0]
 
     shape = (images,) + latents.shape[2:]
@@ -1625,22 +1991,21 @@
         latents.reshape(shape),
         noise_field.reshape(shape),
         mods,
-        flat[ROW_PATCH:ROW_TIME_ONE],
-        flat[ROW_FINAL:ROW_BIAS].reshape(WIDTH, PATCH),
-        flat[ROW_TAIL : ROW_TAIL + TAIL].astype(f32),
+        patch_w,
+        final_rows.astype(bf16).reshape(WIDTH, PATCH),
+        tail,
         full,
     )
 
-    joined, grad_adaptive, window, totals, clip = reduce_all(
+    turned, window, totals, clip = reduce_all(
         n_wide,
         n_narrow,
         images,
         shard,
-        (
-            weight_blocks(n_narrow, normed, g_triple),
-            weight_blocks(n_narrow, mixed, g_branch),
-            weight_blocks(n_narrow, normed_two, g_pre),
-            weight_blocks(n_narrow, act, g_branch_two),
+        weight_blocks(
+            n_narrow,
+            (normed, mixed, normed_two, act),
+            (g_triple, g_branch, g_pre, g_branch_two),
         ),
         (
             g_mods.reshape(images * 8, WIDTH),
@@ -1652,7 +2017,9 @@
             time_pre,
             condition,
             own_act,
-            flat[ROW_TIME_TWO:ROW_TABLE],
+            time_two,
+            lefts,
+            rights,
         ),
     )
     loss_sum = totals[3, PATCH]
@@ -1660,23 +2027,21 @@
     factor = clip[1, 0]
     grad_shared = lax.dynamic_slice(window.reshape(-1), (offset,), (shard,))
 
-    states = (
-        (attend_weight, attend_first, attend_second, attend_left, attend_right),
-        (output_weight, output_first, output_second, output_left, output_right),
-        (expand_weight, expand_first, expand_second, expand_left, expand_right),
-        (shrink_weight, shrink_first, shrink_second, shrink_left, shrink_right),
-        (adaptive_weight, adaptive_first, adaptive_second, adaptive_left, adaptive_right),
+    results = rotated_update(
+        clip,
+        turned,
+        lefts,
+        rights,
+        (
+            (attend_weight, attend_first, attend_second),
+            (output_weight, output_first, output_second),
+            (expand_weight, expand_first, expand_second),
+            (shrink_weight, shrink_first, shrink_second),
+            (adaptive_weight, adaptive_first, adaptive_second),
+        ),
     )
-    tiles = (0, 3, 4, 8)
-    results = []
-    for number in range(5):
-        weight, first, second, left, right = states[number]
-        grad, base = (grad_adaptive, None) if number == 4 else (joined, tiles[number])
-        results += rotated_update(
-            weight, first, second, grad, base, left, right, factor, WIDTH // n_narrow
-        )
     fresh = plain_update(shared_weight, shared_first, shared_second, grad_shared * factor)
-    results += [fresh[0], fresh[1], fresh[2], fresh[0].astype(jnp.bfloat16)]
+    results = [*results, fresh[0], fresh[1], fresh[2], fresh[0].astype(jnp.bfloat16)]
     return tuple(results) + (loss_sum, weight_sum, clip_norm)
 
 

time: 568 us -> 378 us (0.67)
  Pallas kernels: 504 us -> 354 us
  local copies, waits for them, and re-layouts: 45.4 us -> 12.1 us
    pallas_call x9 -> x2, Pallas kernels: 103 us -> 54.1 us  [the longest x1 33.5 us: rotated_update(): pl.pallas_call(partial(adam_kernel, count), in_specs=[pl.BlockSpec(memory...]
    pallas_call x1, Pallas kernels: 127 us -> 81.8 us  [layer(): pl.pallas_call(layer_kernel, grid=(images,), in_specs=[pl.BlockSpec(memor...]
    pallas_call x1, Pallas kernels: 153 us -> 114 us  [reduce_all(): pl.pallas_call(partial(reduce_kernel, n_wide, n_narrow, images, shard), i...]
    unnamed x75 -> x18, local copies, waits for them, and re-layouts: 20.3 us -> 2.37 us
    pallas_call x1, Pallas kernels: 121 us -> 103 us  [gather_all(): pl.pallas_call(partial(gather_kernel, n_wide, n_narrow, images, shard), i...]
    concatenate x1 -> x0, local copies, waits for them, and re-layouts: 13.1 us -> none  [local(): jnp.concatenate([jnp.zeros((margin,), f32), shared_weight, jnp.zeros((row...]
where the time goes in v2:
time: 378 us
  Pallas kernels  354 us (94%)
  local copies, waits for them, and re-layouts  12.1 us (3%)
  other arithmetic  8.73 us (2%)
    pallas_call x1, Pallas kernels, reduce_all(): pl.pallas_call(partial(reduce_kernel, n_wide, n_narrow, images, shard), i...  114 us
    pallas_call x1, Pallas kernels, gather_all(): pl.pallas_call(partial(gather_kernel, n_wide, n_narrow, images, shard), i...  103 us
    pallas_call x1, Pallas kernels, layer(): pl.pallas_call(layer_kernel, grid=(images,), in_specs=[pl.BlockSpec(memor...  81.8 us
    pallas_call x1, Pallas kernels, rotated_update(): pl.pallas_call(partial(adam_kernel, count), in_specs=[pl.BlockSpec(memory...  33.5 us
    pallas_call x1, Pallas kernels, weight_blocks(): pl.pallas_call(weight_kernel, in_specs=[any_space] * 8, out_specs=[any_sp...  20.6 us

profile of v2, /device:TPU:0, one launch (start us, length us, event | category | flops | bytes accessed | tf_op | source)
XLA Modules:
  0.0 377.7 jit_solution(4616374662320457909)
XLA Ops:
  0.7 2.0 pad_dynamic-slice_fusion
  2.7 0.0 copy-start.4
  2.7 0.0 copy-start.5
  2.7 0.0 copy-start.6
  2.7 0.0 copy-start.7
  2.7 1.5 reshape.165.refs_0_
  4.2 0.0 copy-done.4
  4.2 0.1 broadcast_in_dim_reshape.4
  4.3 0.1 convert_element_type.48
  4.4 0.1 add.47
  4.5 0.1 fusion.2
  4.6 0.7 fusion.1.refs_6_
  5.3 103.5 %gather_weights.1 = (bf16[768,2304]{1,0:T(8,128)(2,1)}, bf16[768,768]{1,0:T(8,128)(2,1)}, bf16[768,3072]{1,0:T(8,128)(2,1)}, bf16[3072,768]{1,0:T(8,128)(2,1)}, ...) custom-call(f32[544,768]{1,0:T(8,128)} %reshape.165.refs_0_, ...), custom_call_target="tpu_custom_call" | custom-call | tf_op jit(solution)/shard_map/gather_weights/pallas_call | solution.py:728
  109.5 0.1 div.48
  109.5 0.1 div.46
  109.6 0.1 div.40
  109.7 0.6 pad_maximum_fusion.numbers
  110.3 1.0 copy.68
  111.3 1.0 copy.69
  112.3 0.8 convert_element_type.46
  113.1 0.9 reshape.168.final_ref
  114.0 81.8 %layer.1 = (bf16[1024,768]{1,0:T(8,128)(2,1)}, bf16[1024,768]{1,0:T(8,128)(2,1)}, bf16[1024,768]{1,0:T(8,128)(2,1)}, bf16[1024,3072]{1,0:T(8,128)(2,1)}, bf16[10...) custom-call(f32[3,4]{1,0:T(4,128)} %pad_maximum_fusion.numbers, ...), custom_call_target="tpu_custom_call" | custom-call | flops 28991488000 | bytes 60000000 | tf_op jit(solution)/shard_map/layer/pallas_call | solution.py:1851
  195.8 0.0 copy-start.1
  195.8 20.6 %weight_gradient.1 = (bf16[4,576,768]{2,1,0:T(8,128)(2,1)}, bf16[4,192,768]{2,1,0:T(8,128)(2,1)}, bf16[4,768,768]{2,1,0:T(8,128)(2,1)}, bf16[16,192,768]{2,1,0:T(8,128)(2,1)}) custom-call(bf16[1024,768]{1,0:T(8,128)(2,1)} %get-tuple-element.93.refs_0_, bf16[1024,768]{1,0:T(8,128)(2,1)} %get-tuple-element.94.refs_1_, ...), custom_call_target="tpu_custom_call" | custom-call | tf_op jit(solution)/shard_map/weight_gradient/pallas_call | solution.py:1560
  216.4 0.8 reshape.171.refs_6_
  217.2 114.2 %reduce_gradients.1 = (f32[20,192,768]{2,1,0:T(8,128)}, f32[2112,768]{1,0:T(8,128)}, f32[544,768]{1,0:T(8,128)}, f32[8,768]{1,0:T(8,128)}, f32[8,128]{1,0:T(8,128)}) custom-call(bf16[4,576,768]{2,1,0:T(8,128)(2,1)} %get-tuple-element.101.refs_0_, bf16[4,192,768]{2,1,0:T(8,128)(2,1)} %get-tuple-element.102.refs_1_, ...), custom_call_target="tpu_custom_call" | custom-call | flops 100000000 | bytes 300000000 | tf_op jit(solution)/shard_map/reduce_gradients/pallas_call | solution.py:1419
  331.4 33.5 %rotated_adam.1 = (f32[192,2304]{1,0:T(8,128)}, f32[192,2304]{1,0:T(8,128)}, f32[192,2304]{1,0:T(8,128)}, bf16[192,2304]{1,0:T(8,128)(2,1)}, f32[192,768]{1,0:T(...) custom-call(f32[8,128]{1,0:T(8,128)} %get-tuple-element.117.refs_0_,, ...), custom_call_target="tpu_custom_call" | custom-call | tf_op jit(solution)/shard_map/rotated_adam/pallas_call | solution.py:268
  364.9 1.3 fusion.7
  366.2 1.6 reshape.174
  367.8 0.3 copy-done
  368.1 6.5 %fusion.5 = (bf16[398212]{0:T(1024)(128)(2,1)}, f32[398212]{0:T(1024)}, f32[398212]{0:T(1024)}, f32[398212]{0:T(1024)}) fusion(f32[398212]{0:T(1024)S(1)} %copy-done, f32[]{:T(128)} %bitcast.11, f32[417792]{0:T(1024)S(1)} %reshape.174, s32[]{:T(128)S(6)} %select_n.18, f32[398212]{0:T(1024)} %param.67, f32[398212]{0:T(1024)} %param.68), kind=kLoop, calls=%fused_computation.24 | loop fusion | flops 6769604 | bytes 11946368 | tf_op jit(solution)/shard_map/convert_element_type | solution.py:2044
  374.6 1.3 slice.10
  (14 shorter events, 0.1 us)
Async XLA Ops:
  2.7 1.5 copy-start.4
  2.7 1.6 copy-start.5
  2.7 1.6 copy-start.6
  2.7 1.7 copy-start.7
  5.3 105.0 %copy-start.2 = (f32[2,2,256,16]{2,3,1,0:T(8,128)S(1)}, f32[2,2,256,16]{2,3,1,0:T(8,128)}, u32[]{:S(2)}) copy-start(f32[2,2,256,16]{2,3,1,0:T(8,128)} %param.35) | copy-start | bytes 196612
  5.3 106.0 %copy-start.3 = (f32[2,2,256,16]{2,3,1,0:T(8,128)S(1)}, f32[2,2,256,16]{2,3,1,0:T(8,128)}, u32[]{:S(2)}) copy-start(f32[2,2,256,16]{2,3,1,0:T(8,128)} %param.36) | copy-start | bytes 196612
  195.8 20.6 %copy-start.1 = (f32[768,16]{1,0:T(8,128)S(1)}, f32[768,16]{1,0:T(8,128)}, u32[]{:S(2)}) copy-start(f32[768,16]{1,0:T(8,128)} %get-tuple-element.107) | copy-start | bytes 147460
  366.2 1.9 copy-start

commit v3 on v2

--- a/solution.py
+++ b/solution.py
@@ -359,6 +359,24 @@
     return max(-(-last // ALIGN) * ALIGN, 2112)
 
 
+def center(hidden):
+    centered = hidden - jnp.mean(hidden, axis=-1, keepdims=True)
+    scale = lax.rsqrt(jnp.mean(centered * centered, axis=-1, keepdims=True) + 1e-06)
+    return centered * scale, scale
+
+
+def pair_spans(pair):
+    return [
+        pl.ds(pl.multiple_of(part * WIDTH + pair * 2 * HEAD_DIM, 2 * HEAD_DIM), 2 * HEAD_DIM)
+        for part in range(3)
+    ]
+
+
+def head_masks(tokens):
+    lane = lax.broadcasted_iota(jnp.int32, (tokens, 2 * HEAD_DIM), 1)
+    return lane < HEAD_DIM, lane >= HEAD_DIM
+
+
 def bases_along_lanes(shape):
     return shape[0] == BLOCK and shape[2] > BLOCK
 
@@ -385,8 +403,9 @@
     adaptive_ref, info_ref = refs[count : count + 2]
     left_refs = refs[count + 2 : count + 7]
     right_refs = refs[count + 7 : count + 12]
-    outs = refs[count + 12 : count + 29]
-    scratch = refs[count + 29 :]
+    moment_ref, latent_ref, noise_ref, place_ref = refs[count + 12 : count + 16]
+    outs = refs[count + 16 : count + 37]
+    scratch = refs[count + 37 :]
     (
         patch_out,
         final_out,
@@ -401,13 +420,22 @@
         total_ref,
         lefts_out,
         rights_out,
-    ) = outs[4:17]
+        normed_out,
+        triple_out,
+        mixed_out,
+        probs_out,
+    ) = outs[4:21]
     gathered = scratch[0]
     wides = scratch[1 : count + 1]
     lows = scratch[count + 1 : 2 * count + 1]
     (
         flat,
         turned,
+        attend_full,
+        normed,
+        triple,
+        mixed,
+        probs,
         adaptive_wide,
         info_all,
         part,
@@ -423,8 +451,10 @@
         info_recv,
         part_send,
         part_recv,
+        attend_sem,
+        image_sem,
     ) = scratch[2 * count + 1 :]
-    fulls = (gathered,) + tuple(outs[:4])
+    fulls = (gathered, attend_full) + tuple(outs[1:4])
     here = lax.axis_index("narrow")
     there = lax.axis_index("wide")
     core = there % 2
@@ -543,7 +573,10 @@
         )
         keep.start()
         keeps.append(keep)
-        for step in range(n_bits):
+        narrow_step(number, 0, True)
+
+    def begin_rest(number):
+        for step in range(1, n_bits):
             narrow_step(number, step, True)
 
     places = hop_order(n_wide, n_narrow)
@@ -561,26 +594,28 @@
             flipped(lax.axis_index(axis), 1 << bit, bits),
         )
 
-    info_own.wait()
-    info_copy(0).start()
-    begin(0)
-    for position in range(len(places)):
-        info_copy(position).wait()
-        if position + 1 < len(places):
-            info_copy(position + 1).start()
-        if position + 1 < count:
-            begin(position + 1)
-    for number in range(len(places) + 1, count):
-        begin(number)
-
     def pass_on(numbers, step):
         for number in numbers:
             arrive(number, step)
             if step + 1 < n_bits:
                 narrow_step(number, step + 1, False)
 
-    for step in range(n_bits):
-        pass_on([0], step)
+    info_own.wait()
+    info_copy(0).start()
+    begin(0)
+    begin_rest(0)
+    waiting = [lambda step=step: pass_on([0], step) for step in range(n_bits - 1)]
+    waiting += [lambda: (begin(1), begin_rest(1)), lambda: (begin(2), begin_rest(2))]
+    waiting += [lambda: begin(3), lambda: begin(4)]
+    for position in range(len(places)):
+        info_copy(position).wait()
+        if position + 1 < len(places):
+            info_copy(position + 1).start()
+        if waiting:
+            waiting.pop(0)()
+    for step in waiting:
+        step()
+    pass_on([0], n_bits - 1)
     from_sibling(0)
     keeps[0].wait()
 
@@ -630,13 +665,21 @@
     row = lax.broadcasted_iota(jnp.int32, (8 * n_narrow, act.shape[0]), 0)
     column = lax.broadcasted_iota(jnp.int32, (8 * n_narrow, act.shape[0]), 1)
     owner = there // 2 + n_wide // 2 * (row // 8 + n_narrow * core)
-    chosen = jnp.logical_and(column == owner * images + row % 8, row % 8 < images)
+    chosen = column == owner * images + row % images
     near = dot(jnp.where(chosen, 1.0, 0.0).astype(bf16), act).astype(bf16)
+    across = images
+
+    def piece(index):
+        first = index // across * images
+        start = index % across * WIDTH
+        return slice(first, first + images), slice(start, start + WIDTH)
+
     for index in range(8):
-        span = slice(index * WIDTH, (index + 1) * WIDTH)
-        value = dot(near, adaptive_low[:, span])
+        value = dot(near, adaptive_low[:, index * WIDTH : (index + 1) * WIDTH])
+        rows_of, span = piece(index)
         for number in range(n_narrow):
-            part[0, number, :, span] = value[8 * number : 8 * number + 8]
+            start = 8 * number + rows_of.start
+            part[0, number, rows_of, span] = value[start : start + images]
 
     def lay_bases():
         place = 0
@@ -691,9 +734,7 @@
             copy = part_copy(step, mask)
             copy.start()
             sends.append(copy)
-        pass_on(range(1, count), step)
-        if step == 0:
-            lay_bases()
+        pass_on([1, 2] if step + 1 < n_bits else [], step)
         for mask in masks:
             back, owner = part_back(step, mask)
             back.wait_recv()
@@ -701,22 +742,96 @@
                 part[step + 1, owner] = part[step, owner] + part_in[step, owner]
             else:
                 value = part[step, owner] + part_in[step, owner]
-                for image in range(images):
-                    for index in range(8):
+                for index in range(8):
+                    rows_of, span = piece(index)
+                    for image in range(images):
+                        start = rows_of.start + image
                         mods_ref[image, index : index + 1, :] = (
-                            value[image : image + 1, index * WIDTH : (index + 1) * WIDTH]
+                            value[start : start + 1, span]
                             + tail[tail_row + 9 + index : tail_row + 10 + index]
                         )
 
-    for number in range(1, count):
+    begin_rest(3)
+    begin_rest(4)
+    for step in range(n_bits - 1):
+        pass_on([3, 4], step)
+    pass_on([1], n_bits - 1)
+    lay_bases()
+
+    from_sibling(1)
+    keeps[1].wait()
+    attend_out = pltpu.make_async_copy(attend_full, outs[0], attend_sem)
+    attend_out.start()
+    masks = head_masks(SEQUENCE)
+    rate = HEAD_DIM ** (-0.5)
+
+    def image_copies(image):
+        slot = image % 2
+        tokens = pl.ds(pl.multiple_of(image * SEQUENCE, SEQUENCE), SEQUENCE)
+        heads = pl.ds(image * HEADS, HEADS)
+        pairs = (
+            (normed, normed_out.at[tokens]),
+            (triple, triple_out.at[tokens]),
+            (mixed, mixed_out.at[tokens]),
+            (probs, probs_out.at[heads]),
+        )
+        return [
+            pltpu.make_async_copy(source.at[slot], target, image_sem.at[slot, number])
+            for number, (source, target) in enumerate(pairs)
+        ]
+
+    def one_image(image, carry):
+        slot = image % 2
+
+        @pl.when(image >= 2)
+        def _():
+            for copy in image_copies(image - 2):
+                copy.wait()
+
+        moment = moment_ref[image]
+        blended = (1.0 - moment) * latent_ref[image] + moment * noise_ref[image]
+        start = dot(blended.astype(bf16), patch_out[...]) + tail_out[tail_row : tail_row + 1, :]
+        normal, _ = center(start + place_ref[...])
+        shift = mods_ref[image, 0:1, :]
+        scale = mods_ref[image, 1:2, :]
+        normed[slot] = (normal * (1.0 + scale) + shift).astype(bf16)
+
+        for index in range(3 * WIDTH // STRIP):
+            span = slice(index * STRIP, (index + 1) * STRIP)
+            triple[slot, :, span] = dot(normed[slot], attend_full[:, span]).astype(bf16)
+        for pair in range(HEADS // 2):
+            query_span, key_span, value_span = pair_spans(pair)
+            query = triple[slot, :, query_span]
+            keys = triple[slot, :, key_span]
+            values = triple[slot, :, value_span]
+            results = []
+            for side, mask in enumerate(masks):
+                scores = dot_t(jnp.where(mask, query, jnp.zeros((), bf16)), keys) * rate
+                scores = jnp.exp(scores - jnp.max(scores, axis=-1, keepdims=True))
+                shares = scores * (1.0 / jnp.sum(scores, axis=-1, keepdims=True))
+                shares = shares.astype(bf16)
+                probs[slot, 2 * pair + side] = shares
+                results.append(dot(shares, values))
+            mixed[slot, :, query_span] = jnp.where(masks[0], results[0], results[1]).astype(bf16)
+        for copy in image_copies(image):
+            copy.start()
+        return carry
+
+    lax.fori_loop(0, images, one_image, 0)
+    pass_on(range(2, count), n_bits - 1)
+    for number in range(2, count):
         from_sibling(number)
-    for keep in keeps[1:]:
+    for keep in keeps[2:]:
         keep.wait()
     for copy in sends:
         copy.wait_send()
-
-
-def gather_all(n_wide, n_narrow, images, shard, shards, adaptive, info, lefts, rights):
+    for image in range(max(images - 2, 0), images):
+        for copy in image_copies(image):
+            copy.wait()
+    attend_out.wait()
+
+
+def gather_all(n_wide, n_narrow, images, shard, shards, adaptive, info, lefts, rights, data):
     count = len(shards)
     any_space = pl.BlockSpec(memory_space=pl.ANY)
     vmem = pl.BlockSpec(memory_space=pltpu.VMEM)
@@ -727,8 +842,11 @@
     total = devices * images
     return pl.pallas_call(
         partial(gather_kernel, n_wide, n_narrow, images, shard),
-        in_specs=[any_space] * (count + 2) + [vmem] * 10,
-        out_specs=[any_space] * (count - 1) + [vmem] * 13,
+        in_specs=[any_space] * (count + 2)
+        + [vmem] * 10
+        + [pl.BlockSpec(memory_space=pltpu.SMEM)]
+        + [vmem] * 3,
+        out_specs=[any_space] * (count - 1) + [vmem] * 13 + [any_space] * 4,
         out_shape=[
             jax.ShapeDtypeStruct((piece.shape[0] * n_narrow, piece.shape[1]), bf16)
             for piece in shards[1:]
@@ -747,6 +865,10 @@
             jax.ShapeDtypeStruct((1, 1), f32),
             jax.ShapeDtypeStruct((8 * rows, BLOCK), f32),
             jax.ShapeDtypeStruct((len(tile_places()) * 6 * BLOCK, 4 * BLOCK), f32),
+            jax.ShapeDtypeStruct((images * SEQUENCE, WIDTH), bf16),
+            jax.ShapeDtypeStruct((images * SEQUENCE, 3 * WIDTH), bf16),
+            jax.ShapeDtypeStruct((images * SEQUENCE, WIDTH), bf16),
+            jax.ShapeDtypeStruct((images * HEADS, SEQUENCE, SEQUENCE), bf16),
         ],
         scratch_shapes=[pltpu.VMEM((shards[0].shape[0] * n_narrow, WIDTH), bf16)]
         + [pltpu.VMEM(piece.shape, f32) for piece in shards]
@@ -754,10 +876,15 @@
         + [
             pltpu.VMEM((flat_rows(n_narrow, shard), WIDTH), bf16),
             pltpu.VMEM((8 * WIDTH // BLOCK, BLOCK), f32),
+            pltpu.VMEM((WIDTH, 3 * WIDTH), bf16),
+            pltpu.VMEM((2, SEQUENCE, WIDTH), bf16),
+            pltpu.VMEM((2, SEQUENCE, 3 * WIDTH), bf16),
+            pltpu.VMEM((2, SEQUENCE, WIDTH), bf16),
+            pltpu.VMEM((2, HEADS, SEQUENCE, SEQUENCE), bf16),
             pltpu.VMEM(adaptive.shape, f32),
             pltpu.VMEM((devices,) + info.shape[1:], f32),
-            pltpu.VMEM((n_bits, n_narrow, 8, 8 * WIDTH), f32),
-            pltpu.VMEM((n_bits, n_narrow, 8, 8 * WIDTH), f32),
+            pltpu.VMEM((n_bits, n_narrow, 8, images * WIDTH), f32),
+            pltpu.VMEM((n_bits, n_narrow, 8, images * WIDTH), f32),
             dma((count + 1,)),
             dma((count,)),
             dma((count, 2, n_narrow - 1)),
@@ -769,12 +896,14 @@
             dma((bits_of(devices),)),
             dma((n_bits, n_narrow)),
             dma((n_bits, n_narrow)),
+            dma,
+            dma((2, 4)),
         ],
         compiler_params=pltpu.CompilerParams(
-            collective_id=0, has_side_effects=True, vmem_limit_bytes=56 * 1024 * 1024
+            collective_id=0, has_side_effects=True, vmem_limit_bytes=60 * 1024 * 1024
         ),
         name="gather_weights",
-    )(*shards, adaptive, info, *lefts, *rights)
+    )(*shards, adaptive, info, *lefts, *rights, *data)
 
 
 RING = 4
@@ -1578,12 +1707,6 @@
     return lax.dot_general(left, right, (((0,), (0,)), ((), ())), preferred_element_type=f32)
 
 
-def center(hidden):
-    centered = hidden - jnp.mean(hidden, axis=-1, keepdims=True)
-    scale = lax.rsqrt(jnp.mean(centered * centered, axis=-1, keepdims=True) + 1e-06)
-    return centered * scale, scale
-
-
 def center_back(grad, normal, scale):
     return (
         grad
@@ -1606,6 +1729,9 @@
     latent_ref,
     noise_ref,
     mods_ref,
+    triple,
+    mixed_ref,
+    probs,
     place_ref,
     patch_ref,
     final_ref,
@@ -1614,8 +1740,6 @@
     output_ref,
     expand_ref,
     shrink_ref,
-    normed_ref,
-    mixed_ref,
     normed_two_ref,
     act_ref,
     g_branch_two_ref,
@@ -1626,8 +1750,6 @@
     g_patch_ref,
     g_final_ref,
     g_bias_ref,
-    triple,
-    probs,
     slope,
     normal_one,
     normal_two,
@@ -1665,43 +1787,10 @@
     hidden[...] = start
     normal, scale_one = center(start)
     normal_one[...] = normal
-    normed_ref[...] = (normal * (1.0 + row(1)) + row(0)).astype(bf16)
-
-    def project(index, carry):
-        span = pl.ds(pl.multiple_of(index * wide, wide), wide)
-        triple[:, span] = dot(normed_ref[...], attend_ref[:, span]).astype(bf16)
-        return carry
-
-    lax.fori_loop(0, 3 * WIDTH // wide, project, 0, unroll=True)
-
-    lane = lax.broadcasted_iota(jnp.int32, (tokens, 2 * HEAD_DIM), 1)
-    first_half = lane < HEAD_DIM
     zero = jnp.zeros((), bf16)
+    masks = head_masks(tokens)
+    first_half = masks[0]
     rate = HEAD_DIM ** (-0.5)
-
-    def spans_of(pair):
-        return [
-            pl.ds(pl.multiple_of(part * WIDTH + pair * 2 * HEAD_DIM, 2 * HEAD_DIM), 2 * HEAD_DIM)
-            for part in range(3)
-        ]
-
-    def attend(pair, carry):
-        query_span, key_span, value_span = spans_of(pair)
-        query = triple[:, query_span]
-        keys = triple[:, key_span]
-        values = triple[:, value_span]
-        results = []
-        for side in range(2):
-            mask = first_half if side == 0 else jnp.logical_not(first_half)
-            scores = dot_t(jnp.where(mask, query, zero), keys) * rate
-            scores = jnp.exp(scores - jnp.max(scores, axis=-1, keepdims=True))
-            weights = scores * (1.0 / jnp.sum(scores, axis=-1, keepdims=True))
-            probs[2 * pair + side] = weights
-            results.append(dot(weights.astype(bf16), values))
-        mixed_ref[:, query_span] = jnp.where(first_half, results[0], results[1]).astype(bf16)
-        return carry
-
-    lax.fori_loop(0, HEADS // 2, attend, 0, unroll=True)
 
     value = dot(mixed_ref[...], output_ref[...]) + bias(3)
     branch[...] = value
@@ -1768,17 +1857,17 @@
     g_mixed[...] = dot_t(grad_branch, output_ref[...]).astype(bf16)
 
     def attend_back(pair, carry):
-        query_span, key_span, value_span = spans_of(pair)
+        query_span, key_span, value_span = pair_spans(pair)
         query = triple[:, query_span]
         keys = triple[:, key_span]
         values = triple[:, value_span]
         grad_mixed = g_mixed[:, query_span]
         results = []
         for side in range(2):
-            mask = first_half if side == 0 else jnp.logical_not(first_half)
-            weights = probs[2 * pair + side]
-            grad_weights = dot_t(jnp.where(mask, grad_mixed, zero), values)
-            grad_values = dot_s(weights.astype(bf16), grad_mixed)
+            low_weights = probs[2 * pair + side]
+            weights = low_weights.astype(f32)
+            grad_weights = dot_t(jnp.where(masks[side], grad_mixed, zero), values)
+            grad_values = dot_s(low_weights, grad_mixed)
             grad_scores = weights * (
                 grad_weights - jnp.sum(weights * grad_weights, axis=-1, keepdims=True)
             )
@@ -1809,7 +1898,7 @@
         g_mods_ref[0, index : index + 1, :] = value
 
 
-def layer(numbers, latent, noisy, mods, patch_w, final_w, tail, weights):
+def layer(numbers, latent, noisy, mods, attention, patch_w, final_w, tail, weights):
     images = latent.shape[0]
     tokens = images * SEQUENCE
     once = pl.Buffered(1)
@@ -1829,8 +1918,6 @@
         )
 
     outs = [
-        per_image(WIDTH),
-        per_image(WIDTH),
         per_image(WIDTH),
         per_image(MLP_WIDTH),
         per_image(WIDTH),
@@ -1856,13 +1943,14 @@
             pl.BlockSpec((1, SEQUENCE, PATCH), lambda i: (i, 0, 0)),
             pl.BlockSpec((1, SEQUENCE, PATCH), lambda i: (i, 0, 0)),
             pl.BlockSpec((1, 8, WIDTH), lambda i: (i, 0, 0)),
+            pl.BlockSpec((SEQUENCE, 3 * WIDTH), lambda i: (i, 0)),
+            pl.BlockSpec((SEQUENCE, WIDTH), lambda i: (i, 0)),
+            pl.BlockSpec((HEADS, SEQUENCE, SEQUENCE), lambda i: (i, 0, 0)),
         ]
         + [whole(array) for array in fixed_args],
         out_specs=[spec for spec, _ in outs],
         out_shape=[shape for _, shape in outs],
         scratch_shapes=[
-            pltpu.VMEM((SEQUENCE, 3 * WIDTH), bf16),
-            pltpu.VMEM((HEADS, SEQUENCE, SEQUENCE), f32),
             pltpu.VMEM((SEQUENCE, MLP_WIDTH), f32),
             pltpu.VMEM((SEQUENCE, WIDTH), f32),
             pltpu.VMEM((SEQUENCE, WIDTH), f32),
@@ -1875,7 +1963,7 @@
             flops=flops, bytes_accessed=60 * 10**6, transcendentals=0
         ),
         name="layer",
-    )(numbers, latent, noisy, mods, *fixed_args)
+    )(numbers, latent, noisy, mods, *attention, *fixed_args)
 
 
 def local(
@@ -1927,6 +2015,8 @@
     )
     info = jnp.pad(info, ((0, 8 - images), (0, SHEET - info.shape[1])))[None]
 
+    shape = (images,) + latents.shape[2:]
+
     shard = shared_weight.shape[0]
     rows = shard_rows(shard)
     row_start = column * shard // (WIDTH * ALIGN) * ALIGN
@@ -1950,6 +2040,10 @@
         total,
         lefts,
         rights,
+        normed,
+        triple,
+        mixed,
+        probs,
     ) = gather_all(
         n_wide,
         n_narrow,
@@ -1963,19 +2057,22 @@
             blocks.transpose(1, 2, 0) if blocks.shape[0] > BLOCK else blocks
             for blocks in (attend_right, output_right, expand_right, shrink_right, adaptive_right)
         ],
+        (
+            moment,
+            latents.reshape(shape),
+            noise_field.reshape(shape),
+            positions(SEQUENCE, WIDTH),
+        ),
     )
     lefts = lefts.reshape(8, -1, BLOCK)
     rights = rights.reshape(-1, BLOCK, 4 * BLOCK)
     weight_sum = total[0, 0]
 
-    shape = (images,) + latents.shape[2:]
     entries = SEQUENCE * PATCH
     numbers = jnp.stack(
         [moment, 2.0 * weights_here / (entries * weight_sum), weights_here / entries]
     )
     (
-        normed,
-        mixed,
         normed_two,
         act,
         g_branch_two,
@@ -1991,6 +2088,7 @@
         latents.reshape(shape),
         noise_field.reshape(shape),
         mods,
+        (triple, mixed, probs),
         patch_w,
         final_rows.astype(bf16).reshape(WIDTH, PATCH),
         tail,

time: 378 us -> 359 us (0.950)
  Pallas kernels: 354 us -> 334 us
    pallas_call x1, Pallas kernels: 81.8 us -> 70.2 us  [layer(): pl.pallas_call(layer_kernel, grid=(images,), in_specs=[pl.BlockSpec(memor...]
    pallas_call x1, Pallas kernels: 103 us -> 93.9 us  [gather_all(): pl.pallas_call(partial(gather_kernel, n_wide, n_narrow, images, shard), i...]
where the time goes in v3:
time: 359 us; the launch traced here: 358 us
  Pallas kernels  334 us (93%)
  local copies, waits for them, and re-layouts  12.1 us (3%)
  other arithmetic  9.24 us (3%)
    pallas_call x1, Pallas kernels, reduce_all(): pl.pallas_call(partial(reduce_kernel, n_wide, n_narrow, images, shard), i...  116 us
    pallas_call x1, Pallas kernels, gather_all(): pl.pallas_call(partial(gather_kernel, n_wide, n_narrow, images, shard), i...  93.9 us
    pallas_call x1, Pallas kernels, layer(): pl.pallas_call(layer_kernel, grid=(images,), in_specs=[pl.BlockSpec(memor...  70.2 us
    pallas_call x1, Pallas kernels, rotated_update(): pl.pallas_call(partial(adam_kernel, count), in_specs=[pl.BlockSpec(memory...  33.5 us
    pallas_call x1, Pallas kernels, weight_blocks(): pl.pallas_call(weight_kernel, in_specs=[any_space] * 8, out_specs=[any_sp...  20.6 us

profile of v3, /device:TPU:0, one launch (start us, length us, event | category | flops | bytes accessed | tf_op | source)
XLA Modules:
  0.0 358.2 jit_solution(6348898600267755895)
XLA Ops:
  0.7 2.0 pad_dynamic-slice_fusion
  2.7 0.0 copy-start.4
  2.7 0.0 copy-start.5
  2.7 0.0 copy-start.6
  2.7 0.0 copy-start.3
  2.8 1.5 reshape.167.refs_0_
  4.3 0.1 broadcast_in_dim_reshape.4
  4.4 0.1 convert_element_type.48
  4.5 0.1 add.47
  4.5 0.1 fusion.2
  4.7 0.7 fusion.1.refs_6_
  5.3 0.5 broadcast_multiply_fusion.2.refs_17_
  5.9 1.0 copy.69
  6.9 1.0 copy.70
  7.9 93.9 %gather_weights.1 = (bf16[768,2304]{1,0:T(8,128)(2,1)}, bf16[768,768]{1,0:T(8,128)(2,1)}, bf16[768,3072]{1,0:T(8,128)(2,1)}, bf16[3072,768]{1,0:T(8,128)(2,1)}, ...) custom-call(f32[544,768]{1,0:T(8,128)} %reshape.167.refs_0_, ...), custom_call_target="tpu_custom_call" | custom-call | tf_op jit(solution)/shard_map/gather_weights/pallas_call | solution.py:843
  102.4 0.1 div.51
  102.4 0.1 div.49
  102.5 0.1 div.46
  102.6 0.6 pad_maximum_fusion.numbers
  103.2 0.8 convert_element_type.46
  104.0 0.9 reshape.170.final_ref
  104.9 70.2 %layer.1 = (bf16[1024,768]{1,0:T(8,128)(2,1)}, bf16[1024,3072]{1,0:T(8,128)(2,1)}, bf16[1024,768]{1,0:T(8,128)(2,1)}, bf16[1024,3072]{1,0:T(8,128)(2,1)}, bf16[1...) custom-call(f32[3,4]{1,0:T(4,128)} %pad_maximum_fusion.numbers, ...), custom_call_target="tpu_custom_call" | custom-call | flops 28991488000 | bytes 60000000 | tf_op jit(solution)/shard_map/layer/pallas_call | solution.py:1938
  175.1 0.0 copy-start.1
  175.1 20.6 %weight_gradient.1 = (bf16[4,576,768]{2,1,0:T(8,128)(2,1)}, bf16[4,192,768]{2,1,0:T(8,128)(2,1)}, bf16[4,768,768]{2,1,0:T(8,128)(2,1)}, bf16[16,192,768]{2,1,0:T(8,128)(2,1)}) custom-call(bf16[1024,768]{1,0:T(8,128)(2,1)} %get-tuple-element.86.refs_0_, bf16[1024,768]{1,0:T(8,128)(2,1)} %get-tuple-element.87.mixed_ref.refs_1_, ...), custom_call_target="tpu_custom_call" | custom-call | tf_op jit(solution)/shard_map/weight_gradient/pallas_call | solution.py:1689
  195.7 0.8 reshape.173.refs_6_
  196.5 115.6 %reduce_gradients.1 = (f32[20,192,768]{2,1,0:T(8,128)}, f32[2112,768]{1,0:T(8,128)}, f32[544,768]{1,0:T(8,128)}, f32[8,768]{1,0:T(8,128)}, f32[8,128]{1,0:T(8,128)}) custom-call(bf16[4,576,768]{2,1,0:T(8,128)(2,1)} %get-tuple-element.105.refs_0_, bf16[4,192,768]{2,1,0:T(8,128)(2,1)} %get-tuple-element.106.refs_1_, ...), custom_call_target="tpu_custom_call" | custom-call | flops 100000000 | bytes 300000000 | tf_op jit(solution)/shard_map/reduce_gradients/pallas_call | solution.py:1548
  312.1 33.5 %rotated_adam.1 = (f32[192,2304]{1,0:T(8,128)}, f32[192,2304]{1,0:T(8,128)}, f32[192,2304]{1,0:T(8,128)}, bf16[192,2304]{1,0:T(8,128)(2,1)}, f32[192,768]{1,0:T(...) custom-call(f32[8,128]{1,0:T(8,128)} %get-tuple-element.121.refs_0_,, ...), custom_call_target="tpu_custom_call" | custom-call | tf_op jit(solution)/shard_map/rotated_adam/pallas_call | solution.py:268
  345.6 1.3 fusion.7
  346.8 1.6 reshape.176
  348.4 0.3 copy-done
  348.8 6.5 %fusion.5 = (bf16[398212]{0:T(1024)(128)(2,1)}, f32[398212]{0:T(1024)}, f32[398212]{0:T(1024)}, f32[398212]{0:T(1024)}) fusion(f32[398212]{0:T(1024)S(1)} %copy-done, f32[]{:T(128)} %bitcast.11, f32[417792]{0:T(1024)S(1)} %reshape.176, s32[]{:T(128)S(6)} %select_n.18, f32[398212]{0:T(1024)} %param.68, f32[398212]{0:T(1024)} %param.69), kind=kLoop, calls=%fused_computation.25 | loop fusion | flops 6769604 | bytes 11946368 | tf_op jit(solution)/shard_map/convert_element_type | solution.py:2142
  355.3 1.3 slice.10
  (15 shorter events, 0.1 us)
Async XLA Ops:
  2.7 1.6 copy-start.4
  2.7 1.6 copy-start.5
  2.7 1.6 copy-start.6
  2.7 1.7 copy-start.7
  2.7 3.1 copy-start.2
  2.7 4.1 %copy-start.3 = (f32[2,2,256,16]{2,3,1,0:T(8,128)S(1)}, f32[2,2,256,16]{2,3,1,0:T(8,128)}, u32[]{:S(2)}) copy-start(f32[2,2,256,16]{2,3,1,0:T(8,128)} %param.37) | copy-start | bytes 196612
  175.1 20.6 %copy-start.1 = (f32[768,16]{1,0:T(8,128)S(1)}, f32[768,16]{1,0:T(8,128)}, u32[]{:S(2)}) copy-start(f32[768,16]{1,0:T(8,128)} %get-tuple-element.111) | copy-start | bytes 147460
  346.8 1.9 copy-start

commit v4 on v3

--- a/solution.py
+++ b/solution.py
@@ -910,7 +910,7 @@
 
 
 def reduce_kernel(n_wide, n_narrow, images, shard, *refs):
-    grad_refs = refs[:4]
+    input_refs, gradient_refs = refs[0:4], refs[4:8]
     (
         g_mods_ref,
         g_patch_ref,
@@ -924,10 +924,10 @@
         time_two,
         lefts,
         rights,
-    ) = refs[4:16]
-    turned_out, rows_out, window_out, totals_out, clip_out = refs[16:21]
-    out_ref = refs[21]
-    scratch = refs[22:]
+    ) = refs[8:20]
+    turned_out, rows_out, window_out, totals_out, clip_out = refs[20:25]
+    out_ref, pair, act_in, last_in, blocks, to_core = refs[25:31]
+    scratch = refs[31:]
     own, from_core, to_near, from_near, to_far, from_far, acc, acc_far = scratch[:8]
     load_sem, core_sem, near_sem, far_sem, back_sem, last_sem = scratch[8:14]
     (
@@ -936,6 +936,7 @@
         product_parts,
         first_part,
         biases,
+        small_first,
         small_out,
         small_in,
         small_all,
@@ -1002,40 +1003,107 @@
             left = pl.multiple_of(left, 128)
         return (pl.ds(low, rows), pl.ds(left, cols))
 
-    def keep_copy(k, grad_ref, first):
-        start = pl.multiple_of((k - first) * 2 * half + core * half, 16)
-        return pltpu.make_async_copy(
-            grad_ref.at[:, pl.ds(start, half), :], own.at[k % RING], load_sem.at[k]
-        )
-
-    def start_keep(k):
-        first = 0
-        for grad_ref in grad_refs:
-            tiles = grad_ref.shape[1] // (2 * half)
-
-            @pl.when(jnp.logical_and(k >= first, k < first + tiles))
-            def _(grad_ref=grad_ref, first=first):
-                keep_copy(k, grad_ref, first).start()
-
-            first = first + tiles
-
-    def give_copy(k, grad_ref, first):
-        start = pl.multiple_of((k - first) * 2 * half + (1 - core) * half, 16)
+    def give_copy(k):
         return remote(
-            grad_ref.at[:, pl.ds(start, half), :],
-            from_core.at[k],
+            to_core.at[k % 2],
+            from_core.at[k % RING],
             core_sem.at[0, k],
             core_sem.at[1, k],
             "wide",
             sibling,
         )
 
+    products = [(0, 0), (0, 1), (0, 2), (1, 0), (2, 0), (2, 1), (2, 2), (2, 3)]
+    lasting = act_in.shape[1]
+
+    def start_pair(k):
+        for number, (matrix, across) in enumerate(products):
+
+            @pl.when(k == number)
+            def _(number=number, matrix=matrix, across=across):
+                slot_of = number % 2
+                pltpu.make_async_copy(
+                    input_refs[matrix], pair.at[slot_of, 0], load_sem.at[slot_of, 0]
+                ).start()
+                pltpu.make_async_copy(
+                    gradient_refs[matrix].at[:, pl.ds(across * WIDTH, WIDTH)],
+                    pair.at[slot_of, 1],
+                    load_sem.at[slot_of, 1],
+                ).start()
+
+    def act_load(number):
+        return pltpu.make_async_copy(
+            input_refs[3].at[:, pl.ds(pl.multiple_of(number * lasting, lasting), lasting)],
+            act_in,
+            load_sem.at[2, 0],
+        )
+
+    def last_load():
+        return pltpu.make_async_copy(gradient_refs[3], last_in, load_sem.at[2, 1])
+
+    def put_halves(k, owner, span, lower, upper):
+        own[k % 2, owner, :, span] = jnp.where(core == 0, lower, upper).astype(f32)
+        to_core[k % 2, owner, :, span] = jnp.where(core == 0, upper, lower).astype(bf16)
+
+    def stage_product(k):
+        start_pair(k + 1)
+
+        @pl.when(k >= 2)
+        def _():
+            give_copy(k - 2).wait_send()
+
+        @pl.when(k < len(products))
+        def _():
+            slot_of = k % 2
+            for side_of in range(2):
+                buffer = pair.at[slot_of, side_of]
+                pltpu.make_async_copy(buffer, buffer, load_sem.at[slot_of, side_of]).wait()
+            for start in range(0, WIDTH, STRIP):
+                span = slice(start, start + STRIP)
+                value = dot_s(pair[slot_of, 0], pair[slot_of, 1, :, span])
+                for owner in range(n_narrow):
+                    top = owner * 2 * half
+                    put_halves(
+                        k,
+                        owner,
+                        span,
+                        value[top : top + half],
+                        value[top + half : top + 2 * half],
+                    )
+
+        @pl.when(k >= len(products))
+        def _():
+            for owner in range(n_narrow):
+                block = owner * 4 + k - len(products)
+                put_halves(
+                    k,
+                    owner,
+                    slice(None),
+                    blocks[block, 0:half, :].astype(f32),
+                    blocks[block, half : 2 * half, :].astype(f32),
+                )
+
+        give_copy(k).start()
+
+    def last_product(number):
+        act_load(number).wait()
+        for start in range(0, WIDTH, STRIP):
+            span = slice(start, start + STRIP)
+            value = dot_s(act_in[...], last_in[:, span]).astype(bf16)
+            for piece in range(n_narrow):
+                top = piece * 2 * half
+                blocks[number * n_narrow + piece, :, span] = value[top : top + 2 * half]
+
+        @pl.when(number < 3)
+        def _():
+            act_load(number + 1).start()
+
     def near_copy(path, k, step):
         bit, masks = leaving[path][step]
         spots = pl.ds(min(masks.values()), len(masks))
         return remote(
             to_near.at[path, k % RING, spots],
-            from_near.at[path, k, spots],
+            from_near.at[path, k % RING, spots],
             near_sem.at[0, path, k, step],
             near_sem.at[1, path, k, step],
             "narrow",
@@ -1045,7 +1113,7 @@
     def far_copy(k, step, part):
         return remote(
             to_far.at[(k % RING, step) + window(part)],
-            from_far.at[(k, step) + window(part)],
+            from_far.at[(k % RING, step) + window(part)],
             far_sem.at[0, k, step],
             far_sem.at[1, k, step],
             "wide",
@@ -1089,19 +1157,17 @@
             wait()
 
     def stage_core(k):
-        keep_copy(k, grad_refs[0], k).wait()
-        give_copy(k, grad_refs[0], k).wait_recv()
+        give_copy(k).wait_recv()
         for path in range(2):
             before(k, lambda path=path: near_copy(path, k - RING, 0).wait_send())
             columns = pl.ds(path * side, side)
             for mask in range(n_narrow):
                 owner = flipped(here, mask, n_bits)
-                total = own[k % RING, owner, :, columns].astype(f32) + from_core[
-                    k, owner, :, columns
+                total = own[k % 2, owner, :, columns] + from_core[
+                    k % RING, owner, :, columns
                 ].astype(f32)
                 place_near(path, k, 0, mask, total)
             near_copy(path, k, 0).start()
-        start_keep(k + RING - 1)
 
     def stage_near(step, k):
         ring_slot = k % RING
@@ -1112,7 +1178,7 @@
                 before(k, lambda path=path: near_copy(path, k - RING, step + 1).wait_send())
             bit, masks = leaving[path][step]
             for mask, spot in masks.items():
-                total = acc[ring_slot, mask - bit, :, columns] + from_near[path, k, spot].astype(f32)
+                total = acc[ring_slot, mask - bit, :, columns] + from_near[path, ring_slot, spot].astype(f32)
                 place_near(path, k, step + 1, mask - bit, total)
             if step + 1 < n_bits:
                 near_copy(path, k, step + 1).start()
@@ -1139,7 +1205,7 @@
             mine = acc_far[(ring_slot,) + place]
         else:
             mine = to_far[(ring_slot, step) + place].astype(f32)
-        acc_far[(ring_slot,) + place] = mine + from_far[(k, step) + place].astype(f32)
+        acc_far[(ring_slot,) + place] = mine + from_far[(ring_slot, step) + place].astype(f32)
         start_far(step + 1, k)
 
     def start_back(step, k):
@@ -1186,7 +1252,7 @@
         value = out_ref[k].reshape(2 * half, width)
         turn(value, None, left_number(k), k, k % 2, k >= 2)
 
-    stages = [stage_core]
+    stages = [stage_product, stage_core]
     stages += [partial(stage_near, step) for step in range(n_bits)]
     stages += [partial(stage_far, step) for step in range(far_steps)]
     stages += [partial(stage_back, step) for step in reversed(range(far_steps)) if traded[step]]
@@ -1209,7 +1275,7 @@
         )
 
     column_bits = n_wide // 2
-    half_rows = small_out.shape[1] // 2
+    half_rows = small_out.shape[1]
     own_rows = pl.ds(pl.multiple_of(half_rows * core, 8), half_rows)
     small_places = places[hops - 1 :] + places[: hops - 1]
 
@@ -1243,15 +1309,15 @@
     def small_copy(position):
         if position == 0:
             return beside(
-                *small_places[0], small_out.at[0], small_in.at[0], small_sem, position
+                *small_places[0], small_first.at[0], small_first.at[1], small_sem, position
             )
         if position == hops:
             block = small_all.at[own_rows]
             return beside(*small_places[0], block, block, small_sem, position)
         return beside(
             *small_places[position],
-            small_out.at[position, own_rows],
-            small_in.at[position, own_rows],
+            small_out.at[position],
+            small_in.at[position],
             small_sem,
             position,
         )
@@ -1271,11 +1337,13 @@
 
     height = window_out.shape[0]
 
-    def window_copy():
+    def window_copies():
         start = here * shard // (WIDTH * ALIGN) * ALIGN
-        return pltpu.make_async_copy(
-            rows_out.at[pl.ds(pl.multiple_of(start, ALIGN), height)], window_out, rows_sem.at[2]
-        )
+        source = rows_out.at[pl.ds(pl.multiple_of(start, ALIGN), height)]
+        return [
+            pltpu.make_async_copy(source, stage.at[pl.ds(0, height)], rows_sem.at[2]),
+            pltpu.make_async_copy(stage.at[pl.ds(0, height)], window_out, rows_sem.at[3]),
+        ]
 
     def mods_hop(position):
         if position == 0:
@@ -1297,17 +1365,20 @@
 
     def small_hop(position):
         if position == 0:
-            small_out[0, 0:PATCH] = g_patch_ref[...]
-            small_out[0, PATCH : 2 * PATCH] = g_final_ref[...]
-            small_out[0, 2 * PATCH : 2 * PATCH + 8] = g_bias_ref[...]
-            small_out[0, 2 * PATCH + 8 :] = jnp.zeros(
-                (small_out.shape[1] - 2 * PATCH - 8, WIDTH), f32
+            small_first[0, 0:PATCH] = g_patch_ref[...]
+            small_first[0, PATCH : 2 * PATCH] = g_final_ref[...]
+            small_first[0, 2 * PATCH : 2 * PATCH + 8] = g_bias_ref[...]
+            small_first[0, 2 * PATCH + 8 :] = jnp.zeros(
+                (small_first.shape[1] - 2 * PATCH - 8, WIDTH), f32
             )
         else:
             small_copy(position - 1).wait_recv()
-            total = small_out[position - 1, own_rows] + small_in[position - 1, own_rows]
+            if position == 1:
+                total = small_first[0, own_rows] + small_first[1, own_rows]
+            else:
+                total = small_out[position - 1] + small_in[position - 1]
             if position < hops:
-                small_out[position, own_rows] = total
+                small_out[position] = total
             else:
                 small_all[own_rows] = total
         small_copy(position).start()
@@ -1408,13 +1479,14 @@
 
     def start_window():
         rows_copy(ROW_TABLE, stage.shape[0], 1).wait()
-        window_copy().start()
+        window_copies()[0].start()
 
     def window_squares():
-        window_copy().wait()
+        window_copies()[0].wait()
+        window_copies()[1].start()
         start = here * shard // (WIDTH * ALIGN) * ALIGN
         first = here * shard - start * WIDTH
-        value = window_out[...]
+        value = stage[0:height, :]
         spot = (
             lax.broadcasted_iota(jnp.int32, value.shape, 0) * WIDTH
             + lax.broadcasted_iota(jnp.int32, value.shape, 1)
@@ -1445,27 +1517,26 @@
 
     squares[...] = jnp.zeros_like(squares)
     greet(n_wide, n_narrow)
-    first = 0
-    for grad_ref in grad_refs:
-        tiles = grad_ref.shape[1] // (2 * half)
-
-        def begin(k, carry, grad_ref=grad_ref, first=first):
-            give_copy(k, grad_ref, first).start()
-            return carry
-
-        lax.fori_loop(first, first + tiles, begin, 0)
-        first = first + tiles
-    for k in range(RING - 1):
-        start_keep(jnp.int32(k))
+    start_pair(jnp.int32(0))
+    last_load().start()
+    act_load(0).start()
 
     def wave(t, carry):
-        for number, stage in enumerate(stages):
+        for number, stage in [*enumerate(stages)][1:] + [(0, stages[0])]:
             k = t - number
 
             @pl.when(jnp.logical_and(k >= 0, k < chunks))
             def _(stage=stage, k=k):
                 stage(k)
 
+        @pl.when(t == 1)
+        def _():
+            last_load().wait()
+
+        @pl.when(jnp.logical_and(t % 2 == 1, t < 8))
+        def _():
+            last_product(t // 2)
+
         for number, aside in enumerate(asides):
 
             @pl.when(t == number)
@@ -1483,7 +1554,6 @@
     lax.fori_loop(0, max(chunks + len(stages) - 1, len(asides), first_act + 8), wave, 0)
 
     def finish(k, carry):
-        give_copy(k, grad_refs[0], k).wait_send()
         for step in range(far_steps):
             if traded[step]:
                 back_copy(k, step, parts[step + 1]).wait_send()
@@ -1491,6 +1561,8 @@
         return carry
 
     lax.fori_loop(0, chunks, finish, 0)
+    for k in range(chunks - 2, chunks):
+        give_copy(k).wait_send()
 
     def finish_ring(k, carry):
         for path in range(2):
@@ -1513,6 +1585,7 @@
         act_copy(position).wait_send()
     for slot_of_ring in range(4):
         turned_copy(slot_of_ring, 0).wait()
+    window_copies()[1].wait()
 
     total = jnp.sum(squares[...], axis=1, keepdims=True)
     value = jnp.broadcast_to(total, norm_out.shape[1:])
@@ -1533,9 +1606,10 @@
     clip_out[...] = jnp.where(row == 0, norm, clip_limit / jnp.maximum(norm, clip_limit))
 
 
-def reduce_all(n_wide, n_narrow, images, shard, grads, asides):
+def reduce_all(n_wide, n_narrow, images, shard, inputs, gradients, asides):
     rows = WIDTH // n_narrow
-    chunks = sum(grad.shape[1] for grad in grads) // rows
+    chunks = 12
+    tokens = inputs[0].shape[0]
     half = rows // 2
     far = bits_of(n_wide) - 1
     devices = n_wide * n_narrow
@@ -1547,8 +1621,8 @@
     height = flat_rows(n_narrow, shard)
     turned, _, window, totals, clip = pl.pallas_call(
         partial(reduce_kernel, n_wide, n_narrow, images, shard),
-        in_specs=[any_space] * 4 + [vmem] * len(asides),
-        out_specs=[any_space, any_space, vmem, vmem, vmem],
+        in_specs=[any_space] * 8 + [vmem] * len(asides),
+        out_specs=[any_space, any_space, any_space, vmem, vmem],
         out_shape=[
             jax.ShapeDtypeStruct((chunks + 8, rows, WIDTH), f32),
             jax.ShapeDtypeStruct((height, WIDTH), f32),
@@ -1558,15 +1632,20 @@
         ],
         scratch_shapes=[
             pltpu.VMEM((chunks, 2, half, WIDTH), bf16),
+            pltpu.VMEM((2, 2, tokens, WIDTH), bf16),
+            pltpu.VMEM((tokens, WIDTH), bf16),
+            pltpu.VMEM((tokens, WIDTH), bf16),
+            pltpu.VMEM((4 * n_narrow, rows, WIDTH), bf16),
+            pltpu.VMEM((2, n_narrow, half, WIDTH), bf16),
+            pltpu.VMEM((2, n_narrow, half, WIDTH), f32),
             pltpu.VMEM((RING, n_narrow, half, WIDTH), bf16),
-            pltpu.VMEM((chunks, n_narrow, half, WIDTH), bf16),
             pltpu.VMEM((2, RING, n_narrow - 1, half, WIDTH // 2), bf16),
-            pltpu.VMEM((2, chunks, n_narrow - 1, half, WIDTH // 2), bf16),
+            pltpu.VMEM((2, RING, n_narrow - 1, half, WIDTH // 2), bf16),
             pltpu.VMEM((RING, far, half, WIDTH), bf16),
-            pltpu.VMEM((chunks, far, half, WIDTH), bf16),
+            pltpu.VMEM((RING, far, half, WIDTH), bf16),
             pltpu.VMEM((RING, n_narrow, half, WIDTH), f32),
             pltpu.VMEM((RING, half, WIDTH), f32),
-            dma((chunks,)),
+            dma((3, 2)),
             dma((2, chunks)),
             dma((2, 2, chunks, bits_of(n_narrow))),
             dma((2, chunks, far)),
@@ -1577,8 +1656,9 @@
             pltpu.VMEM((2 * count, WIDTH), bf16),
             pltpu.VMEM((count, WIDTH), bf16),
             pltpu.VMEM((8, WIDTH), f32),
-            pltpu.VMEM((hops, 3 * PATCH, WIDTH), f32),
-            pltpu.VMEM((hops, 3 * PATCH, WIDTH), f32),
+            pltpu.VMEM((2, 3 * PATCH, WIDTH), f32),
+            pltpu.VMEM((hops, 3 * PATCH // 2, WIDTH), f32),
+            pltpu.VMEM((hops, 3 * PATCH // 2, WIDTH), f32),
             pltpu.VMEM((3 * PATCH, WIDTH), f32),
             pltpu.VMEM((n_narrow, count, rows), f32),
             pltpu.VMEM((height - ROW_TABLE, WIDTH), f32),
@@ -1590,117 +1670,19 @@
             dma((2, 2, n_narrow - 1)),
             dma((2, hops + 1)),
             dma((2, bits_of(n_narrow))),
-            dma((3,)),
+            dma((4,)),
             dma((2, bits_of(n_narrow))),
             dma((4,)),
         ],
         compiler_params=pltpu.CompilerParams(
-            collective_id=1, has_side_effects=True, vmem_limit_bytes=62 * 1024 * 1024
+            collective_id=1, has_side_effects=True, vmem_limit_bytes=63 * 1024 * 1024
         ),
         cost_estimate=pl.CostEstimate(
             flops=10**8, bytes_accessed=300 * 10**6, transcendentals=0
         ),
         name="reduce_gradients",
-    )(*grads, *asides)
+    )(*inputs, *gradients, *asides)
     return turned, window, totals, clip
-
-
-def weight_kernel(*refs):
-    lefts, rights, outs = refs[0:4], refs[4:8], refs[8:12]
-    taken, given, take_sem, give_sem = refs[12:]
-    _, pieces, rows, _ = given.shape
-    units = [
-        (matrix, number)
-        for matrix in range(4)
-        for number in range(max(lefts[matrix].shape[1], rights[matrix].shape[1]) // WIDTH)
-    ]
-
-    def takes(unit):
-        matrix, number = units[unit]
-        copies = []
-        for side, ref in enumerate((lefts[matrix], rights[matrix])):
-            start = number * WIDTH if ref.shape[1] > WIDTH else 0
-            copies.append(
-                pltpu.make_async_copy(
-                    ref.at[:, pl.ds(start, WIDTH)],
-                    taken.at[unit % 3, side],
-                    take_sem.at[unit % 3, side],
-                )
-            )
-        return copies
-
-    def give(unit):
-        matrix, number = units[unit]
-        if matrix < 3:
-            target = outs[matrix].at[:, pl.ds(number * rows, rows), :]
-        else:
-            target = outs[3].at[pl.ds(number * pieces, pieces)]
-        return pltpu.make_async_copy(given.at[unit % 2], target, give_sem.at[unit % 2])
-
-    def given_out(slot):
-        pltpu.make_async_copy(given.at[slot], given.at[slot], give_sem.at[slot]).wait()
-
-    for unit in range(2):
-        for copy in takes(unit):
-            copy.start()
-
-    def body(step, carry):
-        for unit in range(2, len(units)):
-
-            @pl.when(step + 2 == unit)
-            def _(unit=unit):
-                for copy in takes(unit):
-                    copy.start()
-
-        slot = step % 3
-        out = step % 2
-        for side in range(2):
-            buffer = taken.at[slot, side]
-            pltpu.make_async_copy(buffer, buffer, take_sem.at[slot, side]).wait()
-
-        @pl.when(step >= 2)
-        def _():
-            given_out(out)
-
-        for start in range(0, WIDTH, STRIP):
-            span = slice(start, start + STRIP)
-            value = dot_s(taken[slot, 0], taken[slot, 1, :, span]).astype(bf16)
-            given[out, :, :, span] = value.reshape(pieces, rows, STRIP)
-        for unit in range(len(units)):
-
-            @pl.when(step == unit)
-            def _(unit=unit):
-                give(unit).start()
-
-        return carry
-
-    lax.fori_loop(0, len(units), body, 0)
-    for slot in range(2):
-        given_out(slot)
-
-
-def weight_blocks(n_narrow, inputs, gradients):
-    rows = WIDTH // n_narrow
-    tokens = inputs[0].shape[0]
-    any_space = pl.BlockSpec(memory_space=pl.ANY)
-    shapes = [(n_narrow, gradient.shape[1] // n_narrow, WIDTH) for gradient in gradients[:3]]
-    shapes.append((inputs[3].shape[1] // rows, rows, WIDTH))
-    dma = pltpu.SemaphoreType.DMA
-    results = pl.pallas_call(
-        weight_kernel,
-        in_specs=[any_space] * 8,
-        out_specs=[any_space] * 4,
-        out_shape=[jax.ShapeDtypeStruct(shape, bf16) for shape in shapes],
-        scratch_shapes=[
-            pltpu.VMEM((3, 2, tokens, WIDTH), bf16),
-            pltpu.VMEM((2, n_narrow, rows, WIDTH), bf16),
-            dma((3, 2)),
-            dma((2,)),
-        ],
-        compiler_params=pltpu.CompilerParams(vmem_limit_bytes=60 * 1024 * 1024),
-        name="weight_gradient",
-    )(*inputs, *gradients)
-    return [result.reshape(n_narrow, -1, WIDTH) for result in results]
 
 
 def dot_s(left, right):
@@ -1809,7 +1791,7 @@
         slope[:, span] = steep
         return carry
 
-    lax.fori_loop(0, MLP_WIDTH // wide, widen, 0, unroll=True)
+    lax.fori_loop(0, MLP_WIDTH // wide, widen, 0, unroll=6)
 
     branch_two = dot(act_ref[...], shrink_ref[...]) + bias(8)
     upper = hidden[...] + row(5) * branch_two
@@ -1842,7 +1824,7 @@
         g_bias_ref[bias_wide(g_bias_ref, 4, index)] += jnp.sum(grad_pre.astype(f32), axis=0, keepdims=True)
         return carry
 
-    lax.fori_loop(0, MLP_WIDTH // wide, narrow, 0, unroll=True)
+    lax.fori_loop(0, MLP_WIDTH // wide, narrow, 0, unroll=6)
 
     grad = dot_t(g_pre_ref[...], expand_ref[...])
     normal = normal_two[...]
@@ -1882,7 +1864,7 @@
             g_triple_ref[:, span] = merged.astype(bf16)
         return carry
 
-    lax.fori_loop(0, HEADS // 2, attend_back, 0, unroll=True)
+    lax.fori_loop(0, HEADS // 2, attend_back, 0, unroll=3)
 
     grad = dot_t(g_triple_ref[...], attend_ref[...])
     normal = normal_one[...]
@@ -2100,11 +2082,8 @@
         n_narrow,
         images,
         shard,
-        weight_blocks(
-            n_narrow,
-            (normed, mixed, normed_two, act),
-            (g_triple, g_branch, g_pre, g_branch_two),
-        ),
+        (normed, mixed, normed_two, act),
+        (g_triple, g_branch, g_pre, g_branch_two),
         (
             g_mods.reshape(images * 8, WIDTH),
             g_patch,

time: 359 us -> 354 us (0.986)
  Pallas kernels: 334 us -> 328 us
    pallas_call x1 -> x0, Pallas kernels: 20.6 us -> none  [weight_blocks(): pl.pallas_call(weight_kernel, in_specs=[any_space] * 8, out_specs=[any_sp...]
    pallas_call x1, Pallas kernels: 116 us -> 123 us  [reduce_all(): pl.pallas_call(partial(reduce_kernel, n_wide, n_narrow, images, shard), i...]
    pallas_call x1, Pallas kernels: 70.2 us -> 77.3 us  [layer(): pl.pallas_call(layer_kernel, grid=(images,), in_specs=[pl.BlockSpec(memor...]
where the time goes in v4:
time: 354 us; the launch traced here: 353 us
  Pallas kernels  328 us (93%)
  local copies, waits for them, and re-layouts  13.1 us (4%)
  other arithmetic  9.24 us (3%)
    pallas_call x1, Pallas kernels, reduce_all(): pl.pallas_call(partial(reduce_kernel, n_wide, n_narrow, images, shard), i...  123 us
    pallas_call x1, Pallas kernels, gather_all(): pl.pallas_call(partial(gather_kernel, n_wide, n_narrow, images, shard), i...  93.9 us
    pallas_call x1, Pallas kernels, layer(): pl.pallas_call(layer_kernel, grid=(images,), in_specs=[pl.BlockSpec(memor...  77.3 us
    pallas_call x1, Pallas kernels, rotated_update(): pl.pallas_call(partial(adam_kernel, count), in_specs=[pl.BlockSpec(memory...  33.5 us

profile of v4, /device:TPU:0, one launch (start us, length us, event | category | flops | bytes accessed | tf_op | source)
XLA Modules:
  0.0 353.4 jit_solution(8820707048471030143)
XLA Ops:
  0.7 2.0 pad_dynamic-slice_fusion
  2.7 0.0 copy-start.3
  2.7 0.0 copy-start.4
  2.7 0.0 copy-start.5
  2.7 0.0 copy-start.6
  2.7 0.0 copy-start.1
  2.7 0.0 copy-start.2
  2.8 1.5 reshape.164.refs_0_
  4.3 0.1 broadcast_in_dim_reshape.4
  4.4 0.1 convert_element_type.48
  4.5 0.1 add.47
  4.5 0.1 fusion.2
  4.7 0.7 fusion.1.refs_6_
  5.3 0.5 broadcast_multiply_fusion.2.refs_17_
  5.9 1.0 copy.69
  6.9 1.0 copy.70
  7.9 93.9 %gather_weights.1 = (bf16[768,2304]{1,0:T(8,128)(2,1)}, bf16[768,768]{1,0:T(8,128)(2,1)}, bf16[768,3072]{1,0:T(8,128)(2,1)}, bf16[3072,768]{1,0:T(8,128)(2,1)}, ...) custom-call(f32[544,768]{1,0:T(8,128)} %reshape.164.refs_0_, ...), custom_call_target="tpu_custom_call" | custom-call | tf_op jit(solution)/shard_map/gather_weights/pallas_call | solution.py:843
  102.4 0.1 div.51
  102.5 0.1 div.49
  102.6 0.1 div.46
  102.6 0.6 pad_maximum_fusion.numbers
  103.2 0.8 convert_element_type.46
  104.0 0.9 reshape.167.final_ref
  104.9 77.3 %layer.1 = (bf16[1024,768]{1,0:T(8,128)(2,1)}, bf16[1024,3072]{1,0:T(8,128)(2,1)}, bf16[1024,768]{1,0:T(8,128)(2,1)}, bf16[1024,3072]{1,0:T(8,128)(2,1)}, bf16[1...) custom-call(f32[3,4]{1,0:T(4,128)} %pad_maximum_fusion.numbers, ...), custom_call_target="tpu_custom_call" | custom-call | flops 28991488000 | bytes 60000000 | tf_op jit(solution)/shard_map/layer/pallas_call | solution.py:1920
  182.2 1.8 reshape.169.refs_10_
  184.0 123.2 %reduce_gradients.1 = (f32[20,192,768]{2,1,0:T(8,128)}, f32[2112,768]{1,0:T(8,128)}, f32[544,768]{1,0:T(8,128)}, f32[8,768]{1,0:T(8,128)}, f32[8,128]{1,0:T(8,128)}) custom-call(bf16[1024,768]{1,0:T(8,128)(2,1)} %get-tuple-element.82.refs_0_, bf16[1024,768]{1,0:T(8,128)(2,1)} %get-tuple-element.83.mixed_ref.refs_1_, ...), custom_call_target="tpu_custom_call" | custom-call | flops 100000000 | bytes 300000000 | tf_op jit(solution)/shard_map/reduce_gradients/pallas_call | solution.py:1622
  307.2 33.5 %rotated_adam.1 = (f32[192,2304]{1,0:T(8,128)}, f32[192,2304]{1,0:T(8,128)}, f32[192,2304]{1,0:T(8,128)}, bf16[192,2304]{1,0:T(8,128)(2,1)}, f32[192,768]{1,0:T(...) custom-call(f32[8,128]{1,0:T(8,128)} %get-tuple-element.113.refs_0_,, ...), custom_call_target="tpu_custom_call" | custom-call | tf_op jit(solution)/shard_map/rotated_adam/pallas_call | solution.py:268
  340.7 1.3 fusion.7
  342.0 1.6 reshape.172
  343.6 0.3 copy-done
  343.9 6.5 %fusion.5 = (bf16[398212]{0:T(1024)(128)(2,1)}, f32[398212]{0:T(1024)}, f32[398212]{0:T(1024)}, f32[398212]{0:T(1024)}) fusion(f32[398212]{0:T(1024)S(1)} %copy-done, f32[]{:T(128)} %bitcast.10, f32[417792]{0:T(1024)S(1)} %reshape.172, s32[]{:T(128)S(6)} %select_n.18, f32[398212]{0:T(1024)} %param.68, f32[398212]{0:T(1024)} %param.69), kind=kLoop, calls=%fused_computation.25 | loop fusion | flops 6769604 | bytes 11946368 | tf_op jit(solution)/shard_map/convert_element_type | solution.py:2121
  350.4 1.3 slice.10
  (12 shorter events, 0.0 us)
Async XLA Ops:
  2.7 1.6 copy-start.3
  2.7 1.6 copy-start.4
  2.7 1.6 copy-start.5
  2.7 1.7 copy-start.6
  2.7 3.1 copy-start.1
  2.7 4.1 %copy-start.2 = (f32[2,2,256,16]{2,3,1,0:T(8,128)S(1)}, f32[2,2,256,16]{2,3,1,0:T(8,128)}, u32[]{:S(2)}) copy-start(f32[2,2,256,16]{2,3,1,0:T(8,128)} %param.37) | copy-start | bytes 196612
  342.0 1.9 copy-start

commit v5 on v4

--- a/solution.py
+++ b/solution.py
@@ -453,8 +453,25 @@
         part_recv,
         attend_sem,
         image_sem,
+        *early,
     ) = scratch[2 * count + 1 :]
     fulls = (gathered, attend_full) + tuple(outs[1:4])
+    early_targets = (time_two_out, sheet, time_pre, condition, own_act, adaptive_low, lefts_out, rights_out)
+    early_buffers, early_sem = early[:8], early[8]
+    (
+        time_two_out,
+        sheet,
+        time_pre,
+        condition,
+        own_act,
+        adaptive_low,
+        lefts_out,
+        rights_out,
+    ) = early_buffers
+    early_copies = [
+        pltpu.make_async_copy(source, target, early_sem.at[number])
+        for number, (source, target) in enumerate(zip(early_buffers, early_targets))
+    ]
     here = lax.axis_index("narrow")
     there = lax.axis_index("wide")
     core = there % 2
@@ -758,6 +775,9 @@
     pass_on([1], n_bits - 1)
     lay_bases()
 
+    for copy in early_copies:
+        copy.start()
+
     from_sibling(1)
     keeps[1].wait()
     attend_out = pltpu.make_async_copy(attend_full, outs[0], attend_sem)
@@ -829,6 +849,8 @@
         for copy in image_copies(image):
             copy.wait()
     attend_out.wait()
+    for copy in early_copies:
+        copy.wait()
 
 
 def gather_all(n_wide, n_narrow, images, shard, shards, adaptive, info, lefts, rights, data):
@@ -840,13 +862,26 @@
     rows = adaptive.shape[0]
     dma = pltpu.SemaphoreType.DMA
     total = devices * images
+    early = (3, 4, 5, 6, 7, 8, 11, 12)
+    early_shapes = [
+        ((WIDTH, WIDTH), bf16),
+        ((total, SHEET), f32),
+        ((total, WIDTH), f32),
+        ((total, WIDTH), f32),
+        ((total, rows), bf16),
+        (adaptive.shape, bf16),
+        ((8 * rows, BLOCK), f32),
+        ((len(tile_places()) * 6 * BLOCK, 4 * BLOCK), f32),
+    ]
     return pl.pallas_call(
         partial(gather_kernel, n_wide, n_narrow, images, shard),
         in_specs=[any_space] * (count + 2)
         + [vmem] * 10
         + [pl.BlockSpec(memory_space=pltpu.SMEM)]
         + [vmem] * 3,
-        out_specs=[any_space] * (count - 1) + [vmem] * 13 + [any_space] * 4,
+        out_specs=[any_space] * (count - 1)
+        + [any_space if number in early else vmem for number in range(13)]
+        + [any_space] * 4,
         out_shape=[
             jax.ShapeDtypeStruct((piece.shape[0] * n_narrow, piece.shape[1]), bf16)
             for piece in shards[1:]
@@ -898,6 +933,8 @@
             dma((n_bits, n_narrow)),
             dma,
             dma((2, 4)),
+            *[pltpu.VMEM(shape, dtype) for shape, dtype in early_shapes],
+            dma((8,)),
         ],
         compiler_params=pltpu.CompilerParams(
             collective_id=0, has_side_effects=True, vmem_limit_bytes=60 * 1024 * 1024
@@ -927,7 +964,19 @@
     ) = refs[8:20]
     turned_out, rows_out, window_out, totals_out, clip_out = refs[20:25]
     out_ref, pair, act_in, last_in, blocks, to_core = refs[25:31]
-    scratch = refs[31:]
+    late_inputs = refs[12:20]
+    late_buffers = refs[31:39]
+    (
+        adaptive_low,
+        sheet,
+        time_pre,
+        condition,
+        own_act,
+        time_two,
+        lefts,
+        rights,
+    ) = late_buffers
+    scratch = refs[39:]
     own, from_core, to_near, from_near, to_far, from_far, acc, acc_far = scratch[:8]
     load_sem, core_sem, near_sem, far_sem, back_sem, last_sem = scratch[8:14]
     (
@@ -940,6 +989,7 @@
         small_out,
         small_in,
         small_all,
+        late_sem,
         act_all,
         stage,
         norm_out,
@@ -1520,6 +1570,12 @@
     start_pair(jnp.int32(0))
     last_load().start()
     act_load(0).start()
+    late_copies = [
+        pltpu.make_async_copy(source, target, late_sem.at[number])
+        for number, (source, target) in enumerate(zip(late_inputs, late_buffers))
+    ]
+    for copy in late_copies:
+        copy.start()
 
     def wave(t, carry):
         for number, stage in [*enumerate(stages)][1:] + [(0, stages[0])]:
@@ -1532,6 +1588,8 @@
         @pl.when(t == 1)
         def _():
             last_load().wait()
+            for copy in late_copies:
+                copy.wait()
 
         @pl.when(jnp.logical_and(t % 2 == 1, t < 8))
         def _():
@@ -1539,11 +1597,11 @@
 
         for number, aside in enumerate(asides):
 
-            @pl.when(t == number)
+            @pl.when(t == number + 2)
             def _(aside=aside):
                 aside()
 
-        index = t - first_act
+        index = t - first_act - 2
 
         @pl.when(jnp.logical_and(index >= 0, index < 8))
         def _():
@@ -1551,7 +1609,7 @@
 
         return carry
 
-    lax.fori_loop(0, max(chunks + len(stages) - 1, len(asides), first_act + 8), wave, 0)
+    lax.fori_loop(0, max(chunks + len(stages) - 1, len(asides) + 2, first_act + 8 + 2), wave, 0)
 
     def finish(k, carry):
         for step in range(far_steps):
@@ -1621,7 +1679,7 @@
     height = flat_rows(n_narrow, shard)
     turned, _, window, totals, clip = pl.pallas_call(
         partial(reduce_kernel, n_wide, n_narrow, images, shard),
-        in_specs=[any_space] * 8 + [vmem] * len(asides),
+        in_specs=[any_space] * 8 + [vmem] * 4 + [any_space] * (len(asides) - 4),
         out_specs=[any_space, any_space, any_space, vmem, vmem],
         out_shape=[
             jax.ShapeDtypeStruct((chunks + 8, rows, WIDTH), f32),
@@ -1637,6 +1695,7 @@
             pltpu.VMEM((tokens, WIDTH), bf16),
             pltpu.VMEM((4 * n_narrow, rows, WIDTH), bf16),
             pltpu.VMEM((2, n_narrow, half, WIDTH), bf16),
+            *[pltpu.VMEM(array.shape, array.dtype) for array in asides[4:]],
             pltpu.VMEM((2, n_narrow, half, WIDTH), f32),
             pltpu.VMEM((RING, n_narrow, half, WIDTH), bf16),
             pltpu.VMEM((2, RING, n_narrow - 1, half, WIDTH // 2), bf16),
@@ -1660,6 +1719,7 @@
             pltpu.VMEM((hops, 3 * PATCH // 2, WIDTH), f32),
             pltpu.VMEM((hops, 3 * PATCH // 2, WIDTH), f32),
             pltpu.VMEM((3 * PATCH, WIDTH), f32),
+            dma((len(asides) - 4,)),
             pltpu.VMEM((n_narrow, count, rows), f32),
             pltpu.VMEM((height - ROW_TABLE, WIDTH), f32),
             pltpu.VMEM((bits_of(n_narrow), 8, 128), f32),
@@ -1791,7 +1851,7 @@
         slope[:, span] = steep
         return carry
 
-    lax.fori_loop(0, MLP_WIDTH // wide, widen, 0, unroll=6)
+    lax.fori_loop(0, MLP_WIDTH // wide, widen, 0, unroll=True)
 
     branch_two = dot(act_ref[...], shrink_ref[...]) + bias(8)
     upper = hidden[...] + row(5) * branch_two
@@ -1824,7 +1884,7 @@
         g_bias_ref[bias_wide(g_bias_ref, 4, index)] += jnp.sum(grad_pre.astype(f32), axis=0, keepdims=True)
         return carry
 
-    lax.fori_loop(0, MLP_WIDTH // wide, narrow, 0, unroll=6)
+    lax.fori_loop(0, MLP_WIDTH // wide, narrow, 0, unroll=True)
 
     grad = dot_t(g_pre_ref[...], expand_ref[...])
     normal = normal_two[...]

time: 354 us -> 342 us (0.966)
  Pallas kernels: 328 us -> 316 us
    pallas_call x1, Pallas kernels: 77.3 us -> 70.8 us  [layer(): pl.pallas_call(layer_kernel, grid=(images,), in_specs=[pl.BlockSpec(memor...]
where the time goes in v5:
time: 342 us
  Pallas kernels  316 us (92%)
  local copies, waits for them, and re-layouts  13.1 us (4%)
  other arithmetic  9.24 us (3%)
    pallas_call x1, Pallas kernels, reduce_all(): pl.pallas_call(partial(reduce_kernel, n_wide, n_narrow, images, shard), i...  120 us
    pallas_call x1, Pallas kernels, gather_all(): pl.pallas_call(partial(gather_kernel, n_wide, n_narrow, images, shard), i...  91.7 us
    pallas_call x1, Pallas kernels, layer(): pl.pallas_call(layer_kernel, grid=(images,), in_specs=[pl.BlockSpec(memor...  70.8 us
    pallas_call x1, Pallas kernels, rotated_update(): pl.pallas_call(partial(adam_kernel, count), in_specs=[pl.BlockSpec(memory...  33.5 us

profile of v5, /device:TPU:0, one launch (start us, length us, event | category | flops | bytes accessed | tf_op | source)
XLA Modules:
  0.0 341.7 jit_solution(6663655391260741354)
XLA Ops:
  0.7 2.0 pad_dynamic-slice_fusion
  2.7 0.0 copy-start.3
  2.7 0.0 copy-start.4
  2.7 0.0 copy-start.5
  2.7 0.0 copy-start.6
  2.7 0.0 copy-start.1
  2.7 0.0 copy-start.2
  2.8 1.5 reshape.164.refs_0_
  4.3 0.1 broadcast_in_dim_reshape.4
  4.4 0.1 convert_element_type.48
  4.5 0.1 add.47
  4.5 0.1 fusion.2
  4.7 0.7 fusion.1.refs_6_
  5.3 0.5 broadcast_multiply_fusion.2.refs_17_
  5.9 1.0 copy.69
  6.9 1.0 copy.70
  7.9 91.7 %gather_weights.1 = (bf16[768,2304]{1,0:T(8,128)(2,1)}, bf16[768,768]{1,0:T(8,128)(2,1)}, bf16[768,3072]{1,0:T(8,128)(2,1)}, bf16[3072,768]{1,0:T(8,128)(2,1)}, ...) custom-call(f32[544,768]{1,0:T(8,128)} %reshape.164.refs_0_, ...), custom_call_target="tpu_custom_call" | custom-call | tf_op jit(solution)/shard_map/gather_weights/pallas_call | solution.py:876
  100.2 0.1 div.51
  100.2 0.1 div.49
  100.3 0.1 div.46
  100.4 0.6 pad_maximum_fusion.numbers
  101.0 0.8 convert_element_type.46
  101.8 0.9 reshape.167.final_ref
  102.7 70.8 %layer.1 = (bf16[1024,768]{1,0:T(8,128)(2,1)}, bf16[1024,3072]{1,0:T(8,128)(2,1)}, bf16[1024,768]{1,0:T(8,128)(2,1)}, bf16[1024,3072]{1,0:T(8,128)(2,1)}, bf16[1...) custom-call(f32[3,4]{1,0:T(4,128)} %pad_maximum_fusion.numbers, ...), custom_call_target="tpu_custom_call" | custom-call | flops 28991488000 | bytes 60000000 | tf_op jit(solution)/shard_map/layer/pallas_call | solution.py:1980
  173.4 1.8 reshape.169.refs_10_
  175.2 120.3 %reduce_gradients.1 = (f32[20,192,768]{2,1,0:T(8,128)}, f32[2112,768]{1,0:T(8,128)}, f32[544,768]{1,0:T(8,128)}, f32[8,768]{1,0:T(8,128)}, f32[8,128]{1,0:T(8,128)}) custom-call(bf16[1024,768]{1,0:T(8,128)(2,1)} %get-tuple-element.82.refs_0_, bf16[1024,768]{1,0:T(8,128)(2,1)} %get-tuple-element.83.mixed_ref.refs_1_, ...), custom_call_target="tpu_custom_call" | custom-call | flops 100000000 | bytes 300000000 | tf_op jit(solution)/shard_map/reduce_gradients/pallas_call | solution.py:1680
  295.5 33.5 %rotated_adam.1 = (f32[192,2304]{1,0:T(8,128)}, f32[192,2304]{1,0:T(8,128)}, f32[192,2304]{1,0:T(8,128)}, bf16[192,2304]{1,0:T(8,128)(2,1)}, f32[192,768]{1,0:T(...) custom-call(f32[8,128]{1,0:T(8,128)} %get-tuple-element.113.refs_0_,, ...), custom_call_target="tpu_custom_call" | custom-call | tf_op jit(solution)/shard_map/rotated_adam/pallas_call | solution.py:268
  329.0 1.3 fusion.7
  330.3 1.6 reshape.172
  331.9 0.3 copy-done
  332.2 6.5 %fusion.5 = (bf16[398212]{0:T(1024)(128)(2,1)}, f32[398212]{0:T(1024)}, f32[398212]{0:T(1024)}, f32[398212]{0:T(1024)}) fusion(f32[398212]{0:T(1024)S(1)} %copy-done, f32[]{:T(128)} %bitcast.10, f32[417792]{0:T(1024)S(1)} %reshape.172, s32[]{:T(128)S(6)} %select_n.18, f32[398212]{0:T(1024)} %param.68, f32[398212]{0:T(1024)} %param.69), kind=kLoop, calls=%fused_computation.25 | loop fusion | flops 6769604 | bytes 11946368 | tf_op jit(solution)/shard_map/convert_element_type | solution.py:2181
  338.7 1.3 slice.10
  (12 shorter events, 0.0 us)
Async XLA Ops:
  2.7 1.6 copy-start.3
  2.7 1.6 copy-start.4
  2.7 1.6 copy-start.5
  2.7 1.7 copy-start.6
  2.7 3.1 copy-start.1
  2.7 4.1 %copy-start.2 = (f32[2,2,256,16]{2,3,1,0:T(8,128)S(1)}, f32[2,2,256,16]{2,3,1,0:T(8,128)}, u32[]{:S(2)}) copy-start(f32[2,2,256,16]{2,3,1,0:T(8,128)} %param.37) | copy-start | bytes 196612
  330.3 1.9 copy-start

commit v6 on v5

--- a/solution.py
+++ b/solution.py
@@ -1578,7 +1578,7 @@
         copy.start()
 
     def wave(t, carry):
-        for number, stage in [*enumerate(stages)][1:] + [(0, stages[0])]:
+        for number, stage in enumerate(stages):
             k = t - number
 
             @pl.when(jnp.logical_and(k >= 0, k < chunks))

time: 342 us -> 341 us (level)
  no operation moved by 1% of the time
where the time goes in v6:
time: 341 us
  Pallas kernels  315 us (92%)
  local copies, waits for them, and re-layouts  13.1 us (4%)
  other arithmetic  9.24 us (3%)
    pallas_call x1, Pallas kernels, reduce_all(): pl.pallas_call(partial(reduce_kernel, n_wide, n_narrow, images, shard), i...  119 us
    pallas_call x1, Pallas kernels, gather_all(): pl.pallas_call(partial(gather_kernel, n_wide, n_narrow, images, shard), i...  91.7 us
    pallas_call x1, Pallas kernels, layer(): pl.pallas_call(layer_kernel, grid=(images,), in_specs=[pl.BlockSpec(memor...  70.8 us
    pallas_call x1, Pallas kernels, rotated_update(): pl.pallas_call(partial(adam_kernel, count), in_specs=[pl.BlockSpec(memory...  33.5 us

profile of v6, /device:TPU:0, one launch (start us, length us, event | category | flops | bytes accessed | tf_op | source)
XLA Modules:
  0.0 340.7 jit_solution(7803766291292177874)
XLA Ops:
  0.7 2.0 pad_dynamic-slice_fusion
  2.7 0.0 copy-start.3
  2.7 0.0 copy-start.4
  2.7 0.0 copy-start.5
  2.7 0.0 copy-start.6
  2.7 0.0 copy-start.1
  2.7 0.0 copy-start.2
  2.8 1.5 reshape.164.refs_0_
  4.3 0.1 broadcast_in_dim_reshape.4
  4.4 0.1 convert_element_type.48
  4.5 0.1 add.47
  4.5 0.1 fusion.2
  4.7 0.7 fusion.1.refs_6_
  5.3 0.5 broadcast_multiply_fusion.2.refs_17_
  5.9 1.0 copy.69
  6.9 1.0 copy.70
  7.9 91.7 %gather_weights.1 = (bf16[768,2304]{1,0:T(8,128)(2,1)}, bf16[768,768]{1,0:T(8,128)(2,1)}, bf16[768,3072]{1,0:T(8,128)(2,1)}, bf16[3072,768]{1,0:T(8,128)(2,1)}, ...) custom-call(f32[544,768]{1,0:T(8,128)} %reshape.164.refs_0_, ...), custom_call_target="tpu_custom_call" | custom-call | tf_op jit(solution)/shard_map/gather_weights/pallas_call | solution.py:876
  100.2 0.1 div.51
  100.2 0.1 div.49
  100.3 0.1 div.46
  100.4 0.6 pad_maximum_fusion.numbers
  101.0 0.8 convert_element_type.46
  101.8 0.9 reshape.167.final_ref
  102.7 70.8 %layer.1 = (bf16[1024,768]{1,0:T(8,128)(2,1)}, bf16[1024,3072]{1,0:T(8,128)(2,1)}, bf16[1024,768]{1,0:T(8,128)(2,1)}, bf16[1024,3072]{1,0:T(8,128)(2,1)}, bf16[1...) custom-call(f32[3,4]{1,0:T(4,128)} %pad_maximum_fusion.numbers, ...), custom_call_target="tpu_custom_call" | custom-call | flops 28991488000 | bytes 60000000 | tf_op jit(solution)/shard_map/layer/pallas_call | solution.py:1980
  173.4 1.8 reshape.169.refs_10_
  175.2 119.2 %reduce_gradients.1 = (f32[20,192,768]{2,1,0:T(8,128)}, f32[2112,768]{1,0:T(8,128)}, f32[544,768]{1,0:T(8,128)}, f32[8,768]{1,0:T(8,128)}, f32[8,128]{1,0:T(8,128)}) custom-call(bf16[1024,768]{1,0:T(8,128)(2,1)} %get-tuple-element.82.refs_0_, bf16[1024,768]{1,0:T(8,128)(2,1)} %get-tuple-element.83.mixed_ref.refs_1_, ...), custom_call_target="tpu_custom_call" | custom-call | flops 100000000 | bytes 300000000 | tf_op jit(solution)/shard_map/reduce_gradients/pallas_call | solution.py:1680
  294.4 33.5 %rotated_adam.1 = (f32[192,2304]{1,0:T(8,128)}, f32[192,2304]{1,0:T(8,128)}, f32[192,2304]{1,0:T(8,128)}, bf16[192,2304]{1,0:T(8,128)(2,1)}, f32[192,768]{1,0:T(...) custom-call(f32[8,128]{1,0:T(8,128)} %get-tuple-element.113.refs_0_,, ...), custom_call_target="tpu_custom_call" | custom-call | tf_op jit(solution)/shard_map/rotated_adam/pallas_call | solution.py:268
  327.9 1.3 fusion.7
  329.2 1.6 reshape.172
  330.8 0.3 copy-done
  331.1 6.5 %fusion.5 = (bf16[398212]{0:T(1024)(128)(2,1)}, f32[398212]{0:T(1024)}, f32[398212]{0:T(1024)}, f32[398212]{0:T(1024)}) fusion(f32[398212]{0:T(1024)S(1)} %copy-done, f32[]{:T(128)} %bitcast.10, f32[417792]{0:T(1024)S(1)} %reshape.172, s32[]{:T(128)S(6)} %select_n.18, f32[398212]{0:T(1024)} %param.68, f32[398212]{0:T(1024)} %param.69), kind=kLoop, calls=%fused_computation.25 | loop fusion | flops 6769604 | bytes 11946368 | tf_op jit(solution)/shard_map/convert_element_type | solution.py:2181
  337.7 1.3 slice.10
  (12 shorter events, 0.0 us)
Async XLA Ops:
  2.7 1.6 copy-start.3
  2.7 1.6 copy-start.4
  2.7 1.6 copy-start.5
  2.7 1.7 copy-start.6
  2.7 3.1 copy-start.1
  2.7 4.1 %copy-start.2 = (f32[2,2,256,16]{2,3,1,0:T(8,128)S(1)}, f32[2,2,256,16]{2,3,1,0:T(8,128)}, u32[]{:S(2)}) copy-start(f32[2,2,256,16]{2,3,1,0:T(8,128)} %param.37) | copy-start | bytes 196612
  329.2 1.9 copy-start
